TPU v7x, 32 devices: a whole 2x2x4 slice. The times are simulated.
32 devices in a mesh: dp: 16 (over z, y, x), tensor: 2 (over core).
Axes of the slice: x: 2, y: 2, z: 4, core: 2. Of those that a mesh axis runs over, the one named last changes fastest.
Arguments:
- resid: bfloat16 [32768, 768], P(('dp', 'tensor')), may hold values from -6 to 6
- gain_in: float32 [768], replicated, may hold values from 0.5 to 1.5
- w_z: bfloat16 [768, 1536], P('dp', 'tensor'), may hold values from -0.21875 to 0.21875
- w_x: bfloat16 [768, 1536], P('dp', 'tensor'), may hold values from -0.21875 to 0.21875
- w_bc: bfloat16 [768, 256], P('dp'), may hold values from -0.21875 to 0.21875
- w_dt: bfloat16 [768, 24], P('dp', 'tensor'), may hold values from -0.21875 to 0.21875
- conv_x: float32 [4, 1536], P(None, 'tensor'), may hold values from -3 to 3
- bias_x: float32 [1536], P('tensor'), may hold values from -0.5 to 0.5
- conv_bc: float32 [4, 256], replicated, may hold values from -3 to 3
- bias_bc: float32 [256], replicated, may hold values from -0.5 to 0.5
- dt_bias: float32 [24], P('tensor'), may hold values from -6.5 to -2.5
- a_log: float32 [24], P('tensor'), may hold values from 0 to 2.5
- d_skip: float32 [24], P('tensor'), may hold values from 0.5 to 1.5
- gain_out: float32 [1536], P('tensor'), may hold values from 0.5 to 1.5
- w_out: bfloat16 [1536, 768], P('tensor', 'dp'), may hold values from -0.15625 to 0.15625
- cotangent: bfloat16 [32768, 768], P(('dp', 'tensor')), may hold values from -6 to 6
Outputs:
- block_out: bfloat16 [32768, 768], P(('dp', 'tensor'))
- grad_resid: float32 [32768, 768], P(('dp', 'tensor'))
- grad_gain_in: float32 [768], replicated
- grad_w_z: float32 [768, 1536], P('dp', 'tensor')
- grad_w_x: float32 [768, 1536], P('dp', 'tensor')
- grad_w_bc: float32 [768, 256], P('dp')
- grad_w_dt: float32 [768, 24], P('dp', 'tensor')
- grad_conv_x: float32 [4, 1536], P(None, 'tensor')
- grad_bias_x: float32 [1536], P('tensor')
- grad_conv_bc: float32 [4, 256], replicated
- grad_bias_bc: float32 [256], replicated
- grad_dt_bias: float32 [24], P('tensor')
- grad_a_log: float32 [24], P('tensor')
- grad_d_skip: float32 [24], P('tensor')
- grad_gain_out: float32 [1536], P('tensor')
- grad_w_out: float32 [1536, 768], P('tensor', 'dp')
All inputs are finite; a program needn't handle non-finite values.
Results may differ from a plain program's by a relative error of at most 0.012.
The roundings to bfloat16 on the way count: a program that leaves them out, or rounds other values in their place, can miss the bound.
Values may be sent and summed in bfloat16 or wider, within the bound.
No kernel may reach another device: no remote copies, remote signals or barrier semaphores. Data moves between devices by JAX's collectives and lax.ppermute only.
A program may use at most 192 MiB of HBM per device.

v0:
```python
import jax
import jax.numpy as jnp
from jax import lax
from jax.sharding import PartitionSpec as P

NS = 128
GROUP = 256
SEQ_LEN = 2048


highest = lax.Precision.HIGHEST
eps = 1e-05


def conv_silu(values, kernel, offset_bias):
    taps = kernel.shape[0]
    seq_length = values.shape[1]
    padded = jnp.pad(values, ((0, 0), (taps - 1, 0), (0, 0)))
    summed = jnp.zeros_like(values) + offset_bias[None, None, :]
    for offset in range(taps):
        summed = summed + kernel[offset][None, None, :] * padded[:, offset : offset + seq_length, :]
    return jax.nn.silu(summed)


def state_space(values, steps_pos, a_log, b_rows, c_rows, d_skip, block_len):
    seq_length, head_count, head_width = values.shape
    block_count = seq_length // block_len
    rates = (steps_pos * (-jnp.exp(a_log))[None, :]).reshape(block_count, block_len, head_count)
    within = jnp.cumsum(rates, axis=1)
    scaled = (values * steps_pos[:, :, None]).reshape(
        block_count, block_len, head_count, head_width
    )
    b_blocks = b_rows.reshape(block_count, block_len, -1)
    c_blocks = c_rows.reshape(block_count, block_len, -1)
    order = jnp.arange(block_len)
    lower_mask = order[:, None] >= order[None, :]
    differences = within[:, :, None, :] - within[:, None, :, :]
    decays = jnp.exp(jnp.where(lower_mask[None, :, :, None], differences, -1e30))
    intersection = jnp.einsum("ctn,csn->cts", c_blocks, b_blocks, precision=highest)
    inside = jnp.einsum("cts,ctsh,cshp->cthp", intersection, decays, scaled, precision=highest)
    tails = jnp.exp(within[:, -1:, :] - within)
    states = jnp.einsum("csn,csh,cshp->chnp", b_blocks, tails, scaled, precision=highest)
    totals = within[:, -1, :]
    ends = jnp.cumsum(totals, axis=0)
    block_order = jnp.arange(block_count)
    earlier = block_order[:, None] > block_order[None, :]
    spans = ends[:, None, :] - totals[:, None, :] - ends[None, :, :]
    carried = jnp.exp(jnp.where(earlier[:, :, None], spans, -1e30))
    entering = jnp.einsum("cdh,dhnp->chnp", carried, states, precision=highest)
    outside = jnp.einsum(
        "ctn,cth,chnp->cthp", c_blocks, jnp.exp(within), entering, precision=highest
    )
    joined = (inside + outside).reshape(seq_length, head_count, head_width)
    return joined + d_skip[None, :, None] * values


def local(
    resid,
    gain_in,
    w_z,
    w_x,
    w_bc,
    w_dt,
    conv_x,
    bias_x,
    conv_bc,
    bias_bc,
    dt_bias,
    a_log,
    d_skip,
    gain_out,
    w_out,
    cotangent,
):
    f32 = jnp.float32
    bf16 = jnp.bfloat16
    parts = lax.axis_size("tensor")
    place = lax.axis_index("tensor")
    local_rows = resid.shape[0]
    head_count = a_log.shape[0]
    full_z, full_x, full_bc, full_dt, full_out = (
        lax.all_gather(w_z, "dp", axis=0, tiled=True),
        lax.all_gather(w_x, "dp", axis=0, tiled=True),
        lax.all_gather(w_bc, "dp", axis=0, tiled=True),
        lax.all_gather(w_dt, "dp", axis=0, tiled=True),
        lax.all_gather(w_out, "dp", axis=1, tiled=True),
    )
    resid_f = resid.astype(f32)
    inv_rms = lax.rsqrt(jnp.mean(resid_f * resid_f, axis=1, keepdims=True) + eps)
    normed_local = (resid_f * inv_rms * gain_in[None, :]).astype(bf16)
    gathered = lax.all_gather(normed_local, "tensor", axis=0, tiled=True)
    all_rows = gathered.shape[0]
    seq_count = all_rows // SEQ_LEN
    gate_proj = jnp.dot(gathered, full_z, preferred_element_type=f32).astype(bf16)
    inner_proj = jnp.dot(gathered, full_x, preferred_element_type=f32).astype(bf16)
    shared_proj = jnp.dot(gathered, full_bc, preferred_element_type=f32).astype(bf16)
    step_raw = jnp.dot(gathered, full_dt, preferred_element_type=f32)
    inner_three = inner_proj.astype(f32).reshape(seq_count, SEQ_LEN, -1)
    shared_three = shared_proj.astype(f32).reshape(seq_count, SEQ_LEN, -1)
    conv_inner = lax.optimization_barrier(
        conv_silu(inner_three, conv_x, bias_x).astype(bf16)
    ).astype(f32)
    conv_shared = lax.optimization_barrier(
        conv_silu(shared_three, conv_bc, bias_bc).astype(bf16)
    ).astype(f32)
    step_sum = step_raw + dt_bias[None, :]
    steps_pos = jax.nn.softplus(step_sum)
    values_all = conv_inner.reshape(seq_count, SEQ_LEN, head_count, -1)
    steps_all = steps_pos.reshape(seq_count, SEQ_LEN, head_count)
    b_all = conv_shared[:, :, :NS]
    c_all = conv_shared[:, :, NS:]

    def mixer_one(item):
        return state_space(item[0], item[1], a_log, item[2], item[3], d_skip, GROUP)

    mixed = lax.map(mixer_one, (values_all, steps_all, b_all, c_all)).reshape(all_rows, -1)
    gate_f = gate_proj.astype(f32)
    silu_gate = jax.nn.silu(gate_f)
    gated = mixed * silu_gate
    inner_total = gated.shape[1] * parts
    squares = lax.psum(jnp.sum(gated * gated, axis=1), "tensor")
    out_scale = lax.rsqrt(squares / inner_total + eps)[:, None]
    normed_out = (gated * out_scale * gain_out[None, :]).astype(bf16)
    branch_sum = lax.psum_scatter(
        jnp.dot(normed_out, full_out, preferred_element_type=f32),
        "tensor",
        scatter_dimension=0,
        tiled=True,
    )
    block_out = (resid_f + branch_sum).astype(bf16)
    back_z, back_x, back_bc, back_dt, back_out = (
        lax.all_gather(w_z, "dp", axis=0, tiled=True),
        lax.all_gather(w_x, "dp", axis=0, tiled=True),
        lax.all_gather(w_bc, "dp", axis=0, tiled=True),
        lax.all_gather(w_dt, "dp", axis=0, tiled=True),
        lax.all_gather(w_out, "dp", axis=1, tiled=True),
    )
    cot_rows = lax.all_gather(cotangent, "tensor", axis=0, tiled=True)
    grad_w_out = jnp.einsum("ti,td->id", normed_out, cot_rows, preferred_element_type=f32)
    grad_normed_out = jnp.einsum("td,id->ti", cot_rows, back_out, preferred_element_type=f32)
    grad_gain_out = jnp.sum(grad_normed_out * gated * out_scale, axis=0)
    weighted_out = grad_normed_out * gain_out[None, :]
    products = lax.psum(jnp.sum(weighted_out * gated, axis=1), "tensor")
    grad_gated = out_scale * weighted_out - gated * out_scale**3 * (products / inner_total)[:, None]
    sigmoid_gate = jax.nn.sigmoid(gate_f)
    grad_gate = (grad_gated * mixed * sigmoid_gate * (1.0 + gate_f * (1.0 - sigmoid_gate))).astype(
        bf16
    )
    grad_mixed = (grad_gated * silu_gate).reshape(seq_count, SEQ_LEN, head_count, -1)

    def mixer_back(item):

        def local_mix(values, steps, rate_log, b_rows, c_rows, skips):
            return state_space(values, steps, rate_log, b_rows, c_rows, skips, GROUP)

        unused, pullback = jax.vjp(local_mix, item[0], item[1], a_log, item[2], item[3], d_skip)
        return pullback(item[4])

    grad_values, grad_steps, grad_rate, grad_b, grad_c, grad_skip = lax.map(
        mixer_back, (values_all, steps_all, b_all, c_all, grad_mixed)
    )
    grad_a_log = jnp.sum(grad_rate, axis=0)
    grad_d_skip = jnp.sum(grad_skip, axis=0)
    grad_shared_post = lax.psum(jnp.concatenate([grad_b, grad_c], axis=2), "tensor")
    grad_step_f = grad_steps.reshape(all_rows, head_count) * jax.nn.sigmoid(step_sum)
    grad_dt_bias = jnp.sum(grad_step_f, axis=0)
    grad_step_raw = grad_step_f.astype(bf16)
    unused_inner, pull_inner = jax.vjp(conv_silu, inner_three, conv_x, bias_x)
    grad_inner, grad_conv_x, grad_bias_x = pull_inner(grad_values.reshape(seq_count, SEQ_LEN, -1))
    grad_inner = grad_inner.reshape(all_rows, -1).astype(bf16)
    unused_shared, pull_shared = jax.vjp(conv_silu, shared_three, conv_bc, bias_bc)
    grad_shared, grad_conv_bc, grad_bias_bc = pull_shared(grad_shared_post)
    grad_shared = grad_shared.reshape(all_rows, -1).astype(bf16)
    summed = jnp.einsum("ti,di->td", grad_gate, back_z, preferred_element_type=f32)
    summed = summed + jnp.einsum("ti,di->td", grad_inner, back_x, preferred_element_type=f32)
    grad_normed = lax.psum_scatter(
        summed + jnp.einsum("th,dh->td", grad_step_raw, back_dt, preferred_element_type=f32),
        "tensor",
        scatter_dimension=0,
        tiled=True,
    )
    shared_local = lax.dynamic_slice_in_dim(grad_shared, place * local_rows, local_rows, 0)
    grad_normed = grad_normed + jnp.einsum(
        "tj,dj->td", shared_local, back_bc, preferred_element_type=f32
    )
    grad_w_z = jnp.einsum("td,ti->di", gathered, grad_gate, preferred_element_type=f32)
    grad_w_x = jnp.einsum("td,ti->di", gathered, grad_inner, preferred_element_type=f32)
    grad_w_bc = jnp.einsum("td,tj->dj", gathered, grad_shared, preferred_element_type=f32)
    grad_w_dt = jnp.einsum("td,th->dh", gathered, grad_step_raw, preferred_element_type=f32)
    grad_w_z, grad_w_x, grad_w_bc, grad_w_dt, grad_w_out = (
        lax.psum_scatter(grad_w_z, "dp", scatter_dimension=0, tiled=True),
        lax.psum_scatter(grad_w_x, "dp", scatter_dimension=0, tiled=True),
        lax.psum_scatter(grad_w_bc, "dp", scatter_dimension=0, tiled=True),
        lax.psum_scatter(grad_w_dt, "dp", scatter_dimension=0, tiled=True),
        lax.psum_scatter(grad_w_out, "dp", scatter_dimension=1, tiled=True),
    )
    gain_part = jnp.sum(grad_normed * resid_f * inv_rms, axis=0)
    weighted_in = grad_normed * gain_in[None, :]
    grad_resid = (
        cotangent.astype(f32)
        + inv_rms * weighted_in
        - resid_f * inv_rms**3 * jnp.mean(weighted_in * resid_f, axis=1, keepdims=True)
    )
    (
        grad_conv_x,
        grad_bias_x,
        grad_conv_bc,
        grad_bias_bc,
        grad_dt_bias,
        grad_a_log,
        grad_d_skip,
        grad_gain_out,
    ) = lax.psum(
        (
            grad_conv_x,
            grad_bias_x,
            grad_conv_bc,
            grad_bias_bc,
            grad_dt_bias,
            grad_a_log,
            grad_d_skip,
            grad_gain_out,
        ),
        "dp",
    )
    grad_gain_in = lax.psum(gain_part, ("dp", "tensor"))
    return (
        block_out,
        grad_resid,
        grad_gain_in,
        grad_w_z,
        grad_w_x,
        grad_w_bc,
        grad_w_dt,
        grad_conv_x,
        grad_bias_x,
        grad_conv_bc,
        grad_bias_bc,
        grad_dt_bias,
        grad_a_log,
        grad_d_skip,
        grad_gain_out,
        grad_w_out,
    )


def solution(mesh):
    in_specs = (
        P(("dp", "tensor"), None),
        P(),
        P("dp", "tensor"),
        P("dp", "tensor"),
        P("dp", None),
        P("dp", "tensor"),
        P(None, "tensor"),
        P("tensor"),
        P(),
        P(),
        P("tensor"),
        P("tensor"),
        P("tensor"),
        P("tensor"),
        P("tensor", "dp"),
        P(("dp", "tensor"), None),
    )
    out_specs = (
        P(("dp", "tensor"), None),
        P(("dp", "tensor"), None),
        P(),
        P("dp", "tensor"),
        P("dp", "tensor"),
        P("dp", None),
        P("dp", "tensor"),
        P(None, "tensor"),
        P("tensor"),
        P(),
        P(),
        P("tensor"),
        P("tensor"),
        P("tensor"),
        P("tensor"),
        P("tensor", "dp"),
    )
    return jax.shard_map(local, mesh=mesh, in_specs=in_specs, out_specs=out_specs, check_vma=False)
```

profile of v0, /device:TPU:0, one launch (start us, length us, event | category | flops | bytes accessed | tf_op | source)
XLA Modules:
  0.0 1193.8 jit_solution(8181344135981752925)
XLA Ops:
  18.1 42.8 %all-gather = bf16[16,48,12]{1,2,0:T(8,128)(2,1)S(1)} all-gather(bf16[1,48,12]{1,2,0:T(8,128)(2,1)S(1)} %bitcast.335), channel_id=1, replica_groups=mesh['dp'=16,'tensor'=2] {'dp'}, dimensions={0}, use_global_device_ids=true | all-gather | bytes 19584 | tf_op jit(solution)/shard_map/all_gather | solution.py:85
  61.0 40.6 %all_gather.27 = bf16[768,256]{1,0:T(8,128)(2,1)} all-gather(bf16[48,256]{1,0:T(8,128)(2,1)S(1)} %copy-done.59), channel_id=1, replica_groups=mesh['dp'=16,'tensor'=2] {'dp'}, dimensions={0}, use_global_device_ids=true | all-gather | bytes 417792 | tf_op jit(solution)/shard_map/all_gather | solution.py:84
  106.0 8.1 reduce-window.14
  165.2 39.7 %fusion.37 = f32[8,256,12,64]{1,3,2,0:T(8,128)S(1)} fusion(f32[8,12,64,256]{3,2,1,0:T(8,128)S(1)} %fusion.74, f32[8,256,12]{1,2,0:T(8,128)S(1)} %get-tuple-element.141, f32[8,256,12,64]{1,0,3,2:T(8,128)S(1)} %bitcast.270, f32[8,256,12]{1,2,0:T(8,128)S(1)} %copy.243, f32[8,256,12]{1,2,0:T(8,128)S(1)} %bitcast.310, f32[8,256,256]{2,1,0:T(8,128)S(1)} %fusion.166, ...), kind=kOutput, calls=%fused_computation.60 | convolution fusion | flops 4855431168 | bytes 21331968 | tf_op jit(solution)/shard_map/while/body/eval_jaxpr/cts,ctsh,cshp->cthp/dot_general | solution.py:40
  215.1 7.4 copy.251
  222.5 12.5 %multiply_reduce_fusion.8 = (f32[2048]{0:T(1024)S(1)}, f32[2048,768]{1,0:T(8,128)}, bf16[2048,768]{1,0:T(8,128)(2,1)}) fusion(f32[2048,768]{1,0:T(8,128)} %copy.251, bf16[1,2048,768]{2,1,0:T(8,128)(2,1)} %copy-done.6, f32[768]{0:T(1024)S(1)} %mul.549, bf16[2048,768]{1,0:T(8,128)(2,1)} %all-gather.7.cloned.1.call-done, ...), kind=kOutput, calls=%fused_computation.74 | convolution fusion | flops 2434791424 | bytes 23211008 | tf_op jit(solution)/shard_map/dot_general | solution.py:94
  237.5 10.5 multiply_reduce_fusion.1
  250.5 15.1 %fusion.36 = (f32[768]{0:T(1024)}, f32[2048,768]{1,0:T(8,128)}, bf16[2048,768]{1,0:T(8,128)(2,1)}) fusion(bf16[1,2048,768]{2,1,0:T(8,128)(2,1)} %copy-done.6, bf16[2048,768]{1,0:T(8,128)(2,1)} %get-tuple-element.152, f32[2048]{0:T(1024)S(1)} %broadcast_multiply_fusion.9, f32[2048,768]{1,0:T(8,128)} %get-tuple-element.120, f32[2048]{0:T(1024)S(1)} %get-tuple-element.143, ...), kind=kLoop, calls=%fused_computation.57 | loop fusion | flops 36175104 | bytes 34636800 | tf_op jit(solution)/shard_map/while/body/eval_jaxpr/transpose(jvp())/reduce_sum | solution.py:54
  265.6 6.8 copy.252
  278.2 8.7 fusion.38
  286.9 12.7 %fusion.107 = f32[8,256,128]{2,1,0:T(8,128)} fusion(f32[8,12,128,64]{2,0,3,1:T(8,128)S(1)} %copy-done.4, f32[8,256,12,64]{1,0,3,2:T(8,128)S(1)} %bitcast.265, f32[8,256,12]{1,2,0:T(8,128)S(1)} %get-tuple-element.141), kind=kOutput, calls=%fused_computation.150 | convolution fusion | flops 2417491968 | bytes 10584064 | tf_op jit(solution)/shard_map/while/body/eval_jaxpr/transpose(jvp(ctn,cth,chnp->cthp))/dot_general | solution.py:50
  304.3 10.4 fusion.156
  319.5 12.7 %fusion.102 = f32[8,256,128]{2,1,0:T(8,128)} fusion(f32[8,12,64,128]{3,0,2,1:T(8,128)S(1)} %fusion.93, f32[8,256,12,64]{1,0,3,2:T(8,128)S(1)} %bitcast.274, f32[8,256,12]{1,2,0:T(8,128)S(1)} %copy-done.33, f32[8,256,12]{1,2,0:T(8,128)S(1)} %copy.243), kind=kOutput, calls=%fused_computation.149 | convolution fusion | flops 2419064832 | bytes 10682368 | tf_op jit(solution)/shard_map/while/body/eval_jaxpr/transpose(jvp(csn,csh,cshp->chnp))/dot_general | solution.py:42
  332.2 6.9 multiply_reduce_fusion
  349.1 40.8 %fusion.9 = (f32[8,256,12]{1,2,0:T(8,128)}, f32[8,256,12]{1,2,0:T(8,128)}, f32[8,256,256]{2,1,0:T(8,128)S(1)}) fusion(f32[8,256,12]{1,2,0:T(8,128)} %bitcast.309, f32[8,256,256]{2,1,0:T(8,128)} %copy-done.27, pred[256,256]{1,0:T(8,128)(4,1)S(1)} %copy-done.47, f32[8,256,12,64]{1,0,3,2:T(8,128)} %bitcast.271, f32[8,256,12]{1,2,0:T(8,128)S(1)} %copy.243, ...), kind=kOutput, calls=%fused_computation.10 | convolution fusion | flops 4889460736 | bytes 17235968 | tf_op jit(solution)/shard_map/while/body/eval_jaxpr/transpose(jvp(cts,ctsh,cshp->cthp))/dot_general | solution.py:40
  396.5 25.7 %bitcast_add_fusion = f32[8,256,12,64]{1,3,2,0:T(8,128)} fusion(f32[8,256,12,64]{1,3,2,0:T(8,128)} %get-tuple-element.155, f32[8,256,12]{1,2,0:T(8,128)S(1)} %copy-done.33, f32[8,256,12]{1,2,0:T(8,128)S(1)} %bitcast.311, f32[8,256,256]{2,1,0:T(8,128)S(1)} %copy-done.28, pred[256,256]{1,0:T(8,128)(4,1)} %iota_compare_fusion, f32[8,12,256,64]{2,0,3,1:T(8,128)} %bitcast.268), kind=kOutput, calls=%fused_computation.49 | convolution fusion | flops 4853858304 | bytes 21233664 | tf_op jit(solution)/shard_map/while/body/eval_jaxpr/transpose(jvp(cts,ctsh,cshp->cthp))/dot_general | solution.py:40
  425.0 19.9 %reduce-window.16 = f32[8,12,2,128]{3,1,2,0:T(8,128)S(1)} reduce-window(f32[8,12,2,128]{3,1,2,0:T(8,128)S(1)} %copy.274, f32[]{:T(128)} %constant.97.clone.1), window={size=1x1x1x128 pad=0_0x0_0x0_0x0_127}, to_apply=%region_16.17 | reduce-window | flops 3121152 | bytes 196612 | tf_op jit(solution)/shard_map/reduce-window.2
  445.4 7.3 copy.258
  462.1 6.7 copy.259
  468.8 20.9 %multiply_reduce_fusion.4 = (f32[768]{0:T(1024)}, f32[768]{0:T(1024)}, f32[768]{0:T(1024)}, f32[768]{0:T(1024)}, f32[768]{0:T(1024)}, /*index=5*/f32[1,2048,768]{2,1,0:T(8,128)}) fusion(f32[1,2048,768]{2,1,0:T(8,128)} %copy-done.2, bf16[2048,768]{1,0:T(8,128)(2,1)} %copy-done.5, f32[1,2048,768]{2,1,0:T(8,128)} %get-tuple-element.122, f32[2048,768]{1,0:T(8,128)} %copy.259, ...), kind=kLoop, calls=%fused_computation.67 | loop fusion | flops 34599168 | bytes 40912896 | tf_op jit(solution)/shard_map/transpose(jvp())/reduce_sum | solution.py:21
  496.9 10.6 broadcast_multiply_fusion
  507.6 9.9 fusion.46
  527.8 8.1 fusion.155
  546.9 8.1 fusion.154
  561.2 7.1 fusion.170
  573.0 54.3 %reduce-scatter.22.cloned.1.call-done = f32[48,12]{1,0:T(8,128)} async-done(((f32[768,12]{1,0:T(8,128)}), f32[48,12]{1,0:T(8,128)}) %reduce-scatter.22.cloned.1.call-update) | async-done | bytes 2320
  630.0 75.3 %all-reduce.20 = (f32[4,768]{1,0:T(4,128)}, f32[768]{0:T(1024)}, f32[4,256]{1,0:T(4,128)}, f32[256]{0:T(256)}, f32[12]{0:T(128)}, /*index=5*/f32[12]{0:T(128)}, f32[12]{0:T(128)}, f32[768]{0:T(1024)}) all-reduce(f32[4,768]{1,0:T(4,128)S(1)} %pad_add_fusion.6, ...), channel_id=1, replica_groups=mesh['dp'=16,'tensor'=2] {'dp'}, use_global_device_ids=true, to_apply=%region_31.32 | all-reduce | flops 5924 | bytes 47392 | tf_op jit(solution)/shard_map/psum | solution.py:213
  710.1 36.8 %psum.87 = f32[768]{0:T(1024)} all-reduce(f32[768]{0:T(1024)S(1)} %get-tuple-element.92), channel_id=1, replica_groups=mesh['dp'=16,'tensor'=2] {'dp','tensor'}, use_global_device_ids=true, to_apply=%region_22.23 | all-reduce | flops 768 | bytes 6144 | tf_op jit(solution)/shard_map/psum | solution.py:226
  751.9 37.9 %reduce-scatter.18.cloned.1.call-done = f32[48,256]{1,0:T(8,128)} async-done(((f32[768,256]{1,0:T(8,128)}), f32[48,256]{1,0:T(8,128)}) %reduce-scatter.18.cloned.1.call-update) | async-done | bytes 49168 | tf_op jit(solution)/shard_map/reduce_scatter | solution.py:193
  789.8 132.2 %reduce-scatter.20.cloned.1.call-done = f32[768,48]{0,1:T(8,128)} async-done(((f32[768,768]{0,1:T(8,128)}), f32[768,48]{0,1:T(8,128)}) %reduce-scatter.20.cloned.1.call-update) | async-done | bytes 147472 | tf_op jit(solution)/shard_map/reduce_scatter | solution.py:195
  922.0 132.8 %reduce-scatter.14.cloned.1.call-done = f32[48,768]{1,0:T(8,128)} async-done(((f32[768,768]{1,0:T(8,128)}), f32[48,768]{1,0:T(8,128)}) %reduce-scatter.14.cloned.1.call-update) | async-done | bytes 147472 | tf_op jit(solution)/shard_map/reduce_scatter | solution.py:191
  1054.8 132.3 %reduce-scatter.16.cloned.1.call-done = f32[48,768]{1,0:T(8,128)} async-done(((f32[768,768]{1,0:T(8,128)}), f32[48,768]{1,0:T(8,128)}) %reduce-scatter.16.cloned.1.call-update) | async-done | bytes 147472 | tf_op jit(solution)/shard_map/reduce_scatter | solution.py:192
  (320 shorter events, 177.0 us)
Async XLA Ops:
  7.2 53.7 %copy-start.59 = (bf16[48,256]{1,0:T(8,128)(2,1)S(1)}, bf16[48,256]{1,0:T(8,128)(2,1)}, u32[]{:S(2)}) copy-start(bf16[48,256]{1,0:T(8,128)(2,1)} %param.20) | copy-start | bytes 73732
  7.2 94.4 %copy-start.76 = (f32[12]{0:T(128)S(1)}, f32[12]{0:T(128)}, u32[]{:S(2)}) copy-start(f32[12]{0:T(128)} %param.26) | copy-start | bytes 148
  7.3 94.3 %all-gather.7.cloned.1.call-start = ((), (), s32[]{:S(2)}) async-start(), calls=%async_computation.7 | async-start | bytes 4718592 | tf_op jit(solution)/shard_map/all_gather | solution.py:91
  13.3 116.3 %all-gather.9.cloned.1.call-start = ((), (), s32[]{:S(2)}) async-start(), calls=%async_computation.8 | async-start | bytes 1253376 | tf_op jit(solution)/shard_map/all_gather | solution.py:83
  14.0 208.5 %all-gather.11.cloned.1.call-start = ((), (), s32[]{:S(2)}) async-start(), calls=%async_computation.9 | async-start | bytes 1253376 | tf_op jit(solution)/shard_map/all_gather | solution.py:82
  14.8 222.7 %all-gather.13.cloned.1.call-start = ((), (), s32[]{:S(2)}) async-start(), calls=%async_computation.10 | async-start | bytes 1253376 | tf_op jit(solution)/shard_map/all_gather | solution.py:86
  15.4 222.2 %all-gather.15.cloned.1.call-start = ((), (), s32[]{:S(2)}) async-start(), calls=%async_computation.12 | async-start | bytes 4718592 | tf_op jit(solution)/shard_map/all_gather | solution.py:138
  15.9 520.1 %all-reduce.23.cloned.1.call-start = ((), (), s32[]{:S(2)}) async-start(), calls=%async_computation.14 | async-start | bytes 4194304 | tf_op jit(solution)/shard_map/psum | solution.py:164
  17.2 88.0 %copy-start.70 = (f32[12]{0:T(128)}, f32[12]{0:T(128)S(1)}, u32[]{:S(2)}) copy-start(f32[12]{0:T(128)S(1)} %exponential_negate_fusion) | copy-start | bytes 148
  17.8 105.8 %copy-start.62 = (f32[1,256]{1,0:T(1,128)}, f32[1,256]{1,0:T(1,128)S(1)}, u32[]{:S(2)}) copy-start(f32[1,256]{1,0:T(1,128)S(1)} %get-tuple-element.147) | copy-start | bytes 3076
  17.8 105.8 %copy-start.64 = (f32[1,256]{1,0:T(1,128)}, f32[1,256]{1,0:T(1,128)S(1)}, u32[]{:S(2)}) copy-start(f32[1,256]{1,0:T(1,128)S(1)} %get-tuple-element.148) | copy-start | bytes 3076
  17.8 105.8 %copy-start.66 = (f32[1,256]{1,0:T(1,128)}, f32[1,256]{1,0:T(1,128)S(1)}, u32[]{:S(2)}) copy-start(f32[1,256]{1,0:T(1,128)S(1)} %get-tuple-element.149) | copy-start | bytes 3076
  18.0 116.2 %copy-start.50 = (f32[768]{0:T(1024)}, f32[768]{0:T(1024)S(1)}, u32[]{:S(2)}) copy-start(f32[768]{0:T(1024)S(1)} %get-tuple-element.101) | copy-start | bytes 9220
  18.0 116.2 %copy-start.52 = (f32[768]{0:T(1024)}, f32[768]{0:T(1024)S(1)}, u32[]{:S(2)}) copy-start(f32[768]{0:T(1024)S(1)} %get-tuple-element.102) | copy-start | bytes 9220
  18.0 116.2 %copy-start.54 = (f32[768]{0:T(1024)}, f32[768]{0:T(1024)S(1)}, u32[]{:S(2)}) copy-start(f32[768]{0:T(1024)S(1)} %get-tuple-element.103) | copy-start | bytes 9220
  18.0 116.2 %copy-start.56 = (f32[768]{0:T(1024)}, f32[768]{0:T(1024)S(1)}, u32[]{:S(2)}) copy-start(f32[768]{0:T(1024)S(1)} %get-tuple-element.104) | copy-start | bytes 9220
  61.0 44.3 %copy-start.41 = (bf16[768,12]{0,1:T(8,128)(2,1)}, bf16[768,12]{0,1:T(8,128)(2,1)S(1)}, u32[]{:S(2)}) copy-start(bf16[768,12]{0,1:T(8,128)(2,1)S(1)} %reshape.379) | copy-start | bytes 55300
  165.1 39.7 %copy-start.7 = (f32[8,12,64,256]{3,2,1,0:T(8,128)}, f32[8,12,64,256]{3,2,1,0:T(8,128)S(1)}, u32[]{:S(2)}) copy-start(f32[8,12,64,256]{3,2,1,0:T(8,128)S(1)} %fusion.74) | copy-start | bytes 18874372
  286.9 32.5 %slice-start = ((s8[6291456]{0:T(1024)(128)(4,1)}), s8[4194304]{0:T(1024)(128)(4,1)S(1)}, s32[]{:S(2)}) async-start(s8[6291456]{0:T(1024)(128)(4,1)} %bitcast.272), calls=%async_computation.20 | async-start | bytes 8388608
  349.1 44.3 %copy-start.13 = (bf16[1,2048,128]{2,1,0:T(8,128)(2,1)S(1)}, bf16[1,2048,128]{2,1,0:T(8,128)(2,1)}, u32[]{:S(2)}) copy-start(bf16[1,2048,128]{2,1,0:T(8,128)(2,1)} %get-tuple-element.137) | copy-start | bytes 1572868
  423.8 203.5 %reduce-scatter.22.cloned.1.call-start = ((), (), s32[]{:S(2)}) async-start(), calls=%async_computation.19 | async-start | bytes 417792
  507.5 197.7 %reduce-scatter.12.cloned.1.call-start = ((), (), s32[]{:S(2)}) async-start(), calls=%async_computation.13 | async-start | bytes 9437184 | tf_op jit(solution)/shard_map/reduce_scatter | solution.py:176
  526.6 220.4 %reduce-scatter.10.cloned.1.call-start = ((), (), s32[]{:S(2)}) async-start(), calls=%async_computation.11 | async-start | bytes 9437184 | tf_op jit(solution)/shard_map/reduce_scatter | solution.py:124
  536.0 253.8 %reduce-scatter.18.cloned.1.call-start = ((), (), s32[]{:S(2)}) async-start(), calls=%async_computation.17 | async-start | bytes 835584 | tf_op jit(solution)/shard_map/reduce_scatter | solution.py:193
  546.9 375.1 %reduce-scatter.20.cloned.1.call-start = ((), (), s32[]{:S(2)}) async-start(), calls=%async_computation.18 | async-start | bytes 2506752 | tf_op jit(solution)/shard_map/reduce_scatter | solution.py:195
  555.0 499.8 %reduce-scatter.14.cloned.1.call-start = ((), (), s32[]{:S(2)}) async-start(), calls=%async_computation.15 | async-start | bytes 2506752 | tf_op jit(solution)/shard_map/reduce_scatter | solution.py:191
  561.1 144.1 %copy-start.8 = (bf16[1024,768]{1,0:T(8,128)(2,1)S(1)}, bf16[1024,768]{1,0:T(8,128)(2,1)}, u32[]{:S(2)}) copy-start(bf16[1024,768]{1,0:T(8,128)(2,1)} %param.16) | copy-start | bytes 4718596
  561.1 144.1 %copy-start.31 = (bf16[768,256]{1,0:T(8,128)(2,1)S(1)}, bf16[768,256]{1,0:T(8,128)(2,1)}, u32[]{:S(2)}) copy-start(bf16[768,256]{1,0:T(8,128)(2,1)} %all_gather.27) | copy-start | bytes 1179652
  561.1 144.1 %copy-start.49 = (f32[1024]{0:T(1024)S(1)}, f32[1024]{0:T(1024)}, u32[]{:S(2)}) copy-start(f32[1024]{0:T(1024)} %copy-done.48) | copy-start | bytes 12292
  561.1 625.9 %reduce-scatter.16.cloned.1.call-start = ((), (), s32[]{:S(2)}) async-start(), calls=%async_computation.16 | async-start | bytes 2506752 | tf_op jit(solution)/shard_map/reduce_scatter | solution.py:192
  568.3 178.7 %copy-start.21 = (bf16[1024,768]{1,0:T(8,128)(2,1)S(1)}, bf16[1024,768]{1,0:T(8,128)(2,1)}, u32[]{:S(2)}) copy-start(bf16[1024,768]{1,0:T(8,128)(2,1)} %param.31) | copy-start | bytes 4718596
  705.2 41.8 %copy-start.58 = (f32[768]{0:T(1024)S(1)}, f32[768]{0:T(1024)}, u32[]{:S(2)}) copy-start(f32[768]{0:T(1024)} %param.17) | copy-start | bytes 9220
  (69 other events, 509.3 us)
Sparse Core Ops, SparseCore 0:
  13.4 14.8 all-gather.6
  31.1 58.6 all-gather.8
  92.5 55.4 all-gather.10
  150.7 54.9 all-gather.12
  207.2 10.9 all-gather.14
  423.9 19.1 all-reduce.22
  507.6 119.5 reduce-scatter.21
  629.6 13.5 reduce-scatter.11
  645.6 15.6 reduce-scatter.9
  666.4 123.3 reduce-scatter.17
  795.3 126.6 reduce-scatter.19
  928.1 126.6 reduce-scatter.13
  1060.3 126.7 reduce-scatter.15
where the time goes:
time: 1200 us; the launch traced here: 1190 us
  waiting for transfers between devices  492 us (41%)
  matrix products  256 us (21%)
  blocking collectives  200 us (17%)
  other arithmetic  134 us (11%)
  local copies, waits for them, and re-layouts  95.8 us (8%)
  between operations  15.5 us (1%)
    reduce_scatter x1, waiting for transfers between devices, local(): lax.psum_scatter(grad_w_z, 'dp', scatter_dimension=0, tiled=True)  133 us
    reduce_scatter x1, waiting for transfers between devices, local(): lax.psum_scatter(grad_w_x, 'dp', scatter_dimension=0, tiled=True)  132 us
    reduce_scatter x1, waiting for transfers between devices, local(): lax.psum_scatter(grad_w_out, 'dp', scatter_dimension=1, tiled=True)  132 us
    dot_general x3, matrix products, state_space(): jnp.einsum('cts,ctsh,cshp->cthp', intersection, decays, scaled, precision...  106 us
    psum x1, blocking collectives, local(): lax.psum((grad_conv_x, grad_bias_x, grad_conv_bc, grad_bias_bc, grad_dt_b...  75.3 us
    unnamed x14, waiting for transfers between devices  56.9 us
    all_gather x1, blocking collectives, local(): lax.all_gather(w_dt, 'dp', axis=0, tiled=True)  42.8 us
    all_gather x1, blocking collectives, local(): lax.all_gather(w_bc, 'dp', axis=0, tiled=True)  40.6 us
  transfers between devices with their start and end apart: 13, of which 5 were waited for; matrix products, arithmetic and copies ran while one was open for 24% of the time, Pallas kernels for 0%

commit v1 on v0

v1 whole, which is shorter than its diff:
```python
import functools

import jax
import jax.numpy as jnp
from jax import lax
from jax.experimental import pallas as pl
from jax.experimental.pallas import tpu as pltpu
from jax.sharding import PartitionSpec as P

NS = 128
L = 256
SEQ_LEN = 2048
HEAD = 64
LANES = 128
VMEM = 52 * 1024 * 1024

f32 = jnp.float32
bf16 = jnp.bfloat16
highest = lax.Precision.HIGHEST
eps = 1e-05

NN = (((1,), (0,)), ((), ()))
NT = (((1,), (1,)), ((), ()))
TN = (((0,), (0,)), ((), ()))


def mm(a, b, dims=NN, precision=None):
    return lax.dot_general(a, b, dims, precision=precision, preferred_element_type=f32)


def iota(shape, dim):
    return lax.broadcasted_iota(jnp.int32, shape, dim)


def lower_tri():
    return (iota((L, L), 0) >= iota((L, L), 1)).astype(f32)


def upper_tri():
    return (iota((L, L), 0) <= iota((L, L), 1)).astype(f32)


def expander(heads):
    rows = iota((LANES, heads * HEAD), 0)
    cols = iota((LANES, heads * HEAD), 1) // HEAD
    return ((rows % 16 == cols) & (rows < 48)).astype(bf16)


def collector(heads):
    rows = iota((heads * HEAD, LANES), 0) // HEAD
    cols = iota((heads * HEAD, LANES), 1)
    return ((cols % 16 == rows) & (cols < 48)).astype(bf16)


def pack3(q):
    lane = iota(q.shape, 1)
    hi = q.astype(bf16).astype(f32)
    rest = q - hi
    mid = rest.astype(bf16).astype(f32)
    return jnp.where(lane < 16, hi, jnp.where(lane < 32, mid, rest - mid)).astype(bf16)


def head_sums(q, col):
    hi = q.astype(bf16)
    lo = (q - hi.astype(f32)).astype(bf16)
    return mm(hi, col) + mm(lo, col)


def softplus(v):
    return jnp.maximum(v, 0.0) + jnp.log1p(jnp.exp(-jnp.abs(v)))


def fold8(q):
    return jnp.sum(q.reshape(q.shape[0] // 8, 8, q.shape[1]), axis=0)


def scan_terms(step_raw, dtb, rate, expand):
    steps = softplus(step_raw + dtb)
    within = mm(lower_tri(), steps * rate, precision=highest)
    tails = jnp.exp(within[L - 1 : L, :] - within)
    steps_e = mm(pack3(steps), expand)
    grown_e = mm(pack3(jnp.exp(within)), expand)
    tails_e = mm(pack3(tails), expand)
    return steps, within, steps_e, grown_e, tails_e


def forward_kernel(
    place, own, oth, gin, w, conv, bias, dtb, rate, dsk, normed_o, xbc_o, step_o, mixed_o, sin_o,
    state, buf,
):
    c = pl.program_id(0)
    half = pl.num_programs(0) // 2
    width = dsk.shape[1]
    heads = width // HEAD
    cols = width + 2 * NS

    @pl.when(c == 0)
    def _():
        state[...] = jnp.zeros_like(state)
        buf[0:8, :] = jnp.zeros((8, cols), f32)

    mine = (c // half) == place[0]
    r = jnp.where(mine, own[...].astype(f32), oth[...].astype(f32))
    inv = lax.rsqrt(jnp.mean(r * r, axis=1, keepdims=True) + eps)
    normed = (r * inv * gin[...]).astype(bf16)
    normed_o[...] = normed
    proj = mm(normed, w[...])
    xbc = proj[:, :cols].astype(bf16)
    step_raw = proj[:, cols:]
    xbc_o[...] = xbc
    step_o[...] = step_raw
    buf[8:, :] = xbc.astype(f32)
    v = bias[...] + conv[3:4, :] * buf[8 : 8 + L, :]
    for k in range(3):
        v = v + conv[k : k + 1, :] * buf[5 + k : 5 + k + L, :]
    buf[0:8, :] = buf[L : L + 8, :]
    act = (v * jax.nn.sigmoid(v)).astype(bf16)
    x = act[:, :width].astype(f32)
    b = act[:, width : width + NS]
    cc = act[:, width + NS :]

    expand = expander(heads)
    steps, within, steps_e, grown_e, tails_e = scan_terms(step_raw, dtb[...], rate[...], expand)
    within_t = within.T
    scaled = x * steps_e
    scaled_b = scaled.astype(bf16)
    inter = mm(cc, b, NT)
    sin = state[...]
    sin_o[0] = sin
    outside = mm(cc, sin.astype(bf16)) * grown_e
    hl = L // 2
    tri = iota((hl, hl), 0) >= iota((hl, hl), 1)
    left = iota((hl, LANES), 1) < HEAD
    for pair in range(heads // 2):
        x2 = scaled_b[:, pair * LANES : (pair + 1) * LANES]
        tops, bots = [], []
        for h in (2 * pair, 2 * pair + 1):
            wc = within[:, h : h + 1]
            wr = within_t[h : h + 1, :]
            d_tl = jnp.exp(jnp.where(tri, wc[:hl] - wr[:, :hl], -1e30))
            d_bl = jnp.exp(wc[hl:] - wr[:, :hl])
            d_br = jnp.exp(jnp.where(tri, wc[hl:] - wr[:, hl:], -1e30))
            m_tl = (inter[:hl, :hl] * d_tl).astype(bf16)
            m_bl = (inter[hl:, :hl] * d_bl).astype(bf16)
            m_br = (inter[hl:, hl:] * d_br).astype(bf16)
            tops.append(mm(m_tl, x2[:hl]))
            bots.append(mm(m_bl, x2[:hl]) + mm(m_br, x2[hl:]))
        ps = slice(pair * LANES, (pair + 1) * LANES)
        skip = dsk[:, ps] * x[:, ps] + outside[:, ps]
        mixed_o[:hl, ps] = jnp.where(left, tops[0], tops[1]) + skip[:hl]
        mixed_o[hl:, ps] = jnp.where(left, bots[0], bots[1]) + skip[hl:]
    state[...] = sin * grown_e[L - 1 : L, :] + mm(b, (scaled * tails_e).astype(bf16), TN)


def gate_kernel(place, cown, coth, normed, mixed, w, gout, gate_o, gno_o, sums_o):
    c = pl.program_id(0)
    half = pl.num_programs(0) // 2
    width = gout.shape[1]
    mine = (c // half) == place[0]
    cot = jnp.where(mine, cown[...].astype(f32), coth[...].astype(f32)).astype(bf16)
    gate = mm(normed[...], w[:, :width]).astype(bf16)
    gate_o[...] = gate
    gf = gate.astype(f32)
    gated = mixed[...] * (gf * jax.nn.sigmoid(gf))
    gno = mm(cot, w[:, width:])
    gno_o[...] = gno
    squares = jnp.sum(gated * gated, axis=1, keepdims=True)
    products = jnp.sum(gno * gout[...] * gated, axis=1, keepdims=True)
    lane = iota((L, LANES), 1)
    sums_o[...] = jnp.where(lane < 64, squares, products)


def gate_back_kernel(
    place, cown, coth, normed, mixed, gate, gno, sown, soth, w, gout, branch_o, ggate_o, gm_o,
    gw_o, ggo_o, acc_z, acc_o, acc_g,
):
    c = pl.program_id(0)
    last = pl.num_programs(0) - 1
    half = pl.num_programs(0) // 2
    width = gout.shape[1]

    @pl.when(c == 0)
    def _():
        acc_z[...] = jnp.zeros_like(acc_z)
        acc_o[...] = jnp.zeros_like(acc_o)
        acc_g[...] = jnp.zeros_like(acc_g)

    mine = (c // half) == place[0]
    cot = jnp.where(mine, cown[...].astype(f32), coth[...].astype(f32)).astype(bf16)
    sums = sown[...] + soth[...]
    inner_total = 2.0 * width
    scale = lax.rsqrt(sums[:, 0:1] / inner_total + eps)
    coef = scale * scale * scale * (sums[:, 64:65] / inner_total)
    gf = gate[...].astype(f32)
    sig = jax.nn.sigmoid(gf)
    silu = gf * sig
    mix = mixed[...]
    gated = mix * silu
    grad = gno[...]
    normed_out = (gated * scale * gout[...]).astype(bf16)
    branch_o[...] = mm(normed_out, w[:, width:], NT).astype(bf16)
    acc_g[...] += fold8(grad * gated * scale)
    grad_gated = scale * (grad * gout[...]) - gated * coef
    grad_gate = (grad_gated * mix * sig * (1.0 + gf * (1.0 - sig))).astype(bf16)
    ggate_o[...] = grad_gate
    gm_o[...] = (grad_gated * silu).astype(bf16)
    acc_z[...] += mm(normed[...], grad_gate, TN)
    acc_o[...] += mm(cot, normed_out, TN)

    @pl.when(c == last)
    def _():
        gw_o[:, :width] = acc_z[...].astype(bf16)
        gw_o[:, width:] = acc_o[...].astype(bf16)
        ggo_o[...] = acc_g[...]


def scan_back_kernel(
    xbc, xprev, step, mixed, sin_r, gm, normed, conv, bias, dtb, rate, dsk,
    gx_o, gw_o, gconv_o, gskip_o, ghead_o,
    dstate, buf, dvbuf, acc_w, acc_c, acc_s, acc_h,
):
    i = pl.program_id(0)
    last = pl.num_programs(0) - 1
    c = last - i
    width = dsk.shape[1]
    heads = width // HEAD
    cols = width + 2 * NS

    @pl.when(i == 0)
    def _():
        dstate[...] = jnp.zeros_like(dstate)
        dvbuf[...] = jnp.zeros_like(dvbuf)
        acc_w[...] = jnp.zeros_like(acc_w)
        acc_c[...] = jnp.zeros_like(acc_c)
        acc_s[...] = jnp.zeros_like(acc_s)
        acc_h[...] = jnp.zeros_like(acc_h)

    buf[8:, :] = xbc[...].astype(f32)
    before = xprev[...].astype(f32)[8:, :]
    buf[0:8, :] = jnp.where(c == 0, 0.0, before)
    v = bias[...] + conv[3:4, :] * buf[8 : 8 + L, :]
    for k in range(3):
        v = v + conv[k : k + 1, :] * buf[5 + k : 5 + k + L, :]
    sig_v = jax.nn.sigmoid(v)
    act = (v * sig_v).astype(bf16)
    dsilu = sig_v * (1.0 + v * (1.0 - sig_v))
    x = act[:, :width].astype(f32)
    b = act[:, width : width + NS]
    cc = act[:, width + NS :]

    expand = expander(heads)
    collect = collector(heads)
    step_raw = step[...]
    steps, within, steps_e, grown_e, tails_e = scan_terms(step_raw, dtb[...], rate[...], expand)
    within_t = within.T
    scaled = x * steps_e
    scaled_b = scaled.astype(bf16)
    gmb = gm[...]
    gmf = gmb.astype(f32)
    sin = sin_r[0]
    ds = dstate[...]
    ds_b = ds.astype(bf16)
    inter_t = mm(b, cc, NT)
    state_part = mm(b, ds_b) * tails_e
    hl = L // 2
    tri = iota((hl, hl), 0) <= iota((hl, hl), 1)
    left = iota((hl, LANES), 1) < HEAD
    leftw = iota((L, LANES), 1) < HEAD
    dg_tl = jnp.zeros((hl, hl), f32)
    dg_tr = jnp.zeros((hl, hl), f32)
    dg_br = jnp.zeros((hl, hl), f32)
    dscaled = []
    for pair in range(heads // 2):
        ps = slice(pair * LANES, (pair + 1) * LANES)
        x2 = scaled_b[:, ps]
        g2 = gmb[:, ps]
        x2f = x2.astype(f32)
        tops, bots = [], []
        for h in (2 * pair, 2 * pair + 1):
            wc = within[:, h : h + 1]
            wr = within_t[h : h + 1, :]
            d_tl = jnp.exp(jnp.where(tri, wr[:, :hl] - wc[:hl], -1e30))
            d_tr = jnp.exp(wr[:, hl:] - wc[:hl])
            d_br = jnp.exp(jnp.where(tri, wr[:, hl:] - wc[hl:], -1e30))
            m_tl = (inter_t[:hl, :hl] * d_tl).astype(bf16)
            m_tr = (inter_t[:hl, hl:] * d_tr).astype(bf16)
            m_br = (inter_t[hl:, hl:] * d_br).astype(bf16)
            tops.append(mm(m_tl, g2[:hl]) + mm(m_tr, g2[hl:]))
            bots.append(mm(m_br, g2[hl:]))
            sel = leftw if h % 2 == 0 else jnp.logical_not(leftw)
            xm = jnp.where(sel, x2f, 0.0).astype(bf16)
            dg_tl += mm(xm[:hl], g2[:hl], NT) * d_tl
            dg_tr += mm(xm[:hl], g2[hl:], NT) * d_tr
            dg_br += mm(xm[hl:], g2[hl:], NT) * d_br
        dscaled.append(
            jnp.concatenate(
                [jnp.where(left, tops[0], tops[1]), jnp.where(left, bots[0], bots[1])], axis=0
            )
        )
    dscaled = jnp.concatenate(dscaled, axis=1) + state_part
    top = jnp.concatenate([dg_tl, dg_tr], axis=1)
    bot = jnp.concatenate([jnp.zeros((hl, hl), f32), dg_br], axis=1)
    dg = jnp.concatenate([top, bot], axis=0).astype(bf16)
    gm_grown = (gmf * grown_e).astype(bf16)
    dc = mm(dg, b, TN) + mm(gm_grown, sin.astype(bf16), NT)
    db = mm(dg, cc) + mm((scaled * tails_e).astype(bf16), ds_b, NT)
    scaled_f = scaled_b.astype(f32)
    y = mixed[...] - dsk[...] * x
    q = gmf * y - scaled_f * dscaled
    last_grown = grown_e[L - 1 : L, :]
    ends = jnp.sum(scaled_f * state_part, axis=0, keepdims=True) + last_grown * jnp.sum(
        sin * ds, axis=0, keepdims=True
    )
    ends_h = head_sums(jnp.broadcast_to(ends, (8, width)), collect)[0:1, :]
    d_rate = mm(upper_tri(), head_sums(q, collect), precision=highest) + ends_h
    d_steps = d_rate * rate[...] + head_sums(dscaled * x, collect)
    sig_s = jax.nn.sigmoid(step_raw + dtb[...])
    keep = iota((L, LANES), 1) < heads
    d_raw = jnp.where(keep, d_steps * sig_s, 0.0)
    acc_h[0:8, :] += fold8(d_raw)
    acc_h[8:16, :] += fold8(d_rate * steps * rate[...])
    acc_s[...] += fold8(gmf * x)
    dx = dscaled * steps_e + dsk[...] * gmf
    dstate[...] = ds * last_grown + mm(cc, gm_grown, TN)

    dv = jnp.concatenate([dx, db, dc], axis=1) * dsilu
    dvbuf[0:L, :] = dv
    acc_c[4] += fold8(dv)
    for k in range(4):
        acc_c[k] += fold8(dv * buf[5 + k : 5 + k + L, :])
    dxin = conv[3:4, :] * dv
    for k in range(3):
        dxin = dxin + conv[k : k + 1, :] * dvbuf[3 - k : 3 - k + L, :]
    dvbuf[L : L + 8, :] = dvbuf[0:8, :]
    gx_o[:, :cols] = dxin.astype(bf16)
    gx_o[:, cols:] = d_raw.astype(bf16)
    acc_w[...] += mm(normed[...], gx_o[...], TN)

    @pl.when(i == last)
    def _():
        gw_o[...] = acc_w[...].astype(bf16)
        gconv_o[...] = acc_c[...]
        gskip_o[...] = acc_s[...]
        ghead_o[...] = acc_h[...]


def input_back_kernel(place, own, oth, ggate, gx, wz, wx, dn_o, gain_o, acc):
    c = pl.program_id(0)
    half = pl.num_programs(0) // 2

    @pl.when(c == 0)
    def _():
        acc[...] = jnp.zeros_like(acc)

    mine = (c // half) == place[0]
    r = jnp.where(mine, own[...].astype(f32), oth[...].astype(f32))
    inv = lax.rsqrt(jnp.mean(r * r, axis=1, keepdims=True) + eps)
    width = ggate.shape[1]
    dn = mm(ggate[...], wz[:, :width], NT) + mm(gx[...], wx[...], NT)
    dn_o[...] = dn.astype(bf16)
    acc[...] += fold8(dn * r * inv)

    @pl.when(c == pl.num_programs(0) - 1)
    def _():
        gain_o[...] = acc[...]


def finish_kernel(resid, cot, gin, dn_own, dn_oth, br_own, br_oth, out_o, gres_o):
    r = resid[...].astype(f32)
    inv = lax.rsqrt(jnp.mean(r * r, axis=1, keepdims=True) + eps)
    out_o[...] = (r + (br_own[...].astype(f32) + br_oth[...].astype(f32))).astype(bf16)
    u = (dn_own[...].astype(f32) + dn_oth[...].astype(f32)) * gin[...]
    mean = jnp.mean(u * r, axis=1, keepdims=True)
    gres_o[...] = cot[...].astype(f32) + inv * u - r * (inv * inv * inv * mean)


def swap(v, bit, axis):
    size = lax.axis_size(axis)
    return lax.ppermute(v, axis, [(i, i ^ bit) for i in range(size)])


def gather_rows(v, bits, axis):
    me = lax.axis_index(axis)
    rows, cols = v.shape
    held = {0: v}
    for bit in bits:
        for slot in list(held):
            held[slot ^ bit] = swap(held[slot], bit, axis)
    stacked = jnp.stack([held[j] for j in range(len(held))])
    return stacked, me


def in_order(stacked, axis):
    size = lax.axis_size(axis)
    me = lax.axis_index(axis)
    count, rows, cols = stacked.shape
    bit = 1
    while bit < size:
        v = stacked.reshape(size // (2 * bit), 2, bit, rows, cols)
        stacked = jnp.where((me & bit) != 0, v[:, ::-1], v).reshape(size, rows, cols)
        bit *= 2
    return stacked.reshape(size * rows, cols)


def scatter_sum(g, bits, axis):
    size = lax.axis_size(axis)
    me = lax.axis_index(axis)
    rows = g.shape[0] // size
    left = sorted(bits, reverse=True)
    cur = g.reshape([2] * len(left) + [rows, g.shape[1]])
    for bit in bits:
        dim = left.index(bit)
        mine = ((me & bit) != 0).astype(jnp.int32)
        send = lax.dynamic_index_in_dim(cur, 1 - mine, dim, keepdims=False)
        keep = lax.dynamic_index_in_dim(cur, mine, dim, keepdims=False)
        got = swap(send.astype(bf16), bit, axis)
        cur = keep.astype(f32) + got.astype(f32)
        left.pop(dim)
    return cur.astype(f32)


def full(shape):
    zeros = (0,) * len(shape)
    return pl.BlockSpec(shape, lambda c, *_: zeros)


def rows_spec(count, width, index=lambda c: c):
    return pl.BlockSpec((count, width), lambda c, *_: (index(c), 0))


def params():
    return pltpu.CompilerParams(dimension_semantics=("arbitrary",), vmem_limit_bytes=VMEM)


def local(
    resid, gain_in, w_z, w_x, w_bc, w_dt, conv_x, bias_x, conv_bc, bias_bc, dt_bias, a_log, d_skip,
    gain_out, w_out, cotangent,
):
    size = lax.axis_size("dp")
    place = lax.axis_index("tensor")
    heads = a_log.shape[0]
    width = heads * HEAD
    dim = resid.shape[1]
    cols = width + 2 * NS
    half_rows = resid.shape[0]
    tokens = 2 * half_rows
    assert tokens == SEQ_LEN
    chunks = tokens // L
    half = chunks // 2
    shape = jax.ShapeDtypeStruct

    bits = []
    bit = size // 2
    while bit:
        bits.append(bit)
        bit //= 2
    order_a = bits
    order_b = bits[:-2] + bits[-2:][::-1]
    order_c = bits[-2:] + bits[:-2]

    def lanes3(v):
        pad = [(0, 0)] * (v.ndim - 1)
        group = jnp.pad(v, pad + [(0, 16 - heads)])
        return jnp.pad(jnp.concatenate([group] * 3, axis=-1), pad + [(0, LANES - 48)])

    resid_oth = swap(resid, 1, "tensor")
    cot_oth = swap(cotangent, 1, "tensor")
    first = jnp.concatenate([w_x, w_bc, lanes3(w_dt)], axis=1)
    second = jnp.concatenate([w_z, w_out.T], axis=1)

    def gather(v, cuts, orders):
        parts = []
        start = 0
        for stop, order in zip(cuts, orders):
            stacked, _ = gather_rows(v[:, start:stop], order, "dp")
            parts.append(stacked)
            start = stop
        return in_order(jnp.concatenate(parts, axis=2), "dp")

    wx = gather(first, (384, 768, 1152), (order_a, order_b, order_c))
    wz = gather(second, (640, 1280, 1536), (order_a, order_b, order_c))

    conv = jnp.concatenate([conv_x, conv_bc], axis=1)
    bias = jnp.concatenate([bias_x, bias_bc])[None]
    dtb = lanes3(dt_bias[None])
    rate = lanes3(-jnp.exp(a_log)[None])
    dsk = jnp.repeat(d_skip, HEAD)[None]
    gin = gain_in[None]
    gout = gain_out[None]
    place1 = place.astype(jnp.int32)[None]

    half_spec = rows_spec(L, dim, lambda c: c % half)
    wide = rows_spec(L, width)
    normed, xbc, step_raw, mixed, sin = pl.pallas_call(
        forward_kernel,
        grid_spec=pltpu.PrefetchScalarGridSpec(
            num_scalar_prefetch=1,
            grid=(chunks,),
            in_specs=[
                half_spec, half_spec, full((1, dim)), full((dim, cols + LANES)), full((4, cols)),
                full((1, cols)), full((1, LANES)), full((1, LANES)), full((1, width)),
            ],
            out_specs=[
                rows_spec(L, dim), rows_spec(L, cols), rows_spec(L, LANES), wide,
                pl.BlockSpec((1, NS, width), lambda c, *_: (c, 0, 0)),
            ],
            scratch_shapes=[pltpu.VMEM((NS, width), f32), pltpu.VMEM((L + 8, cols), f32)],
        ),
        out_shape=[
            shape((tokens, dim), bf16), shape((tokens, cols), bf16), shape((tokens, LANES), f32),
            shape((tokens, width), f32), shape((chunks, NS, width), f32),
        ],
        compiler_params=params(),
        name="mix_forward",
    )(place1, resid, resid_oth, gin, wx, conv, bias, dtb, rate, dsk)

    gate, gno, sums = pl.pallas_call(
        gate_kernel,
        grid_spec=pltpu.PrefetchScalarGridSpec(
            num_scalar_prefetch=1,
            grid=(chunks,),
            in_specs=[
                half_spec, half_spec, rows_spec(L, dim), wide, full((dim, 2 * width)),
                full((1, width)),
            ],
            out_specs=[wide, wide, rows_spec(L, LANES)],
        ),
        out_shape=[
            shape((tokens, width), bf16), shape((tokens, width), f32), shape((tokens, LANES), f32),
        ],
        compiler_params=params(),
        name="gate_forward",
    )(place1, cotangent, cot_oth, normed, mixed, wz, gout)

    sums_oth = swap(sums, 1, "tensor")
    branch, ggate, gm, gw_zo, g_gout = pl.pallas_call(
        gate_back_kernel,
        grid_spec=pltpu.PrefetchScalarGridSpec(
            num_scalar_prefetch=1,
            grid=(chunks,),
            in_specs=[
                half_spec, half_spec, rows_spec(L, dim), wide, wide, wide, rows_spec(L, LANES),
                rows_spec(L, LANES), full((dim, 2 * width)), full((1, width)),
            ],
            out_specs=[
                rows_spec(L, dim), wide, wide, full((dim, 2 * width)), full((8, width)),
            ],
            scratch_shapes=[
                pltpu.VMEM((dim, width), f32), pltpu.VMEM((dim, width), f32),
                pltpu.VMEM((8, width), f32),
            ],
        ),
        out_shape=[
            shape((tokens, dim), bf16), shape((tokens, width), bf16), shape((tokens, width), bf16),
            shape((dim, 2 * width), bf16), shape((8, width), f32),
        ],
        compiler_params=params(),
        name="gate_backward",
    )(place1, cotangent, cot_oth, normed, mixed, gate, gno, sums, sums_oth, wz, gout)

    rs_a = bits[::-1]
    rs_b = (bits[-2:] + bits[:-2][::-1]) if size > 2 else bits
    grad_w_z = scatter_sum(gw_zo[:, :width], rs_a, "dp")
    grad_w_out = scatter_sum(gw_zo[:, width:], rs_b, "dp").T

    half_of = lambda v, which: lax.dynamic_slice_in_dim(v, which * half_rows, half_rows, 0)
    branch_own = half_of(branch, place)
    branch_oth = swap(half_of(branch, 1 - place), 1, "tensor")

    def back(c):
        return chunks - 1 - c

    rwide = rows_spec(L, width, back)
    gx, gw_x, g_conv, g_skip, g_head = pl.pallas_call(
        scan_back_kernel,
        grid=(chunks,),
        in_specs=[
            rows_spec(L, cols, back),
            rows_spec(16, cols, lambda c: jnp.maximum(back(c) * (L // 16) - 1, 0)),
            rows_spec(L, LANES, back), rwide,
            pl.BlockSpec((1, NS, width), lambda c: (back(c), 0, 0)),
            rwide, rows_spec(L, dim, back), full((4, cols)), full((1, cols)), full((1, LANES)),
            full((1, LANES)), full((1, width)),
        ],
        out_specs=[
            rows_spec(L, cols + LANES, back), full((dim, cols + LANES)), full((5, 8, cols)),
            full((8, width)), full((16, LANES)),
        ],
        scratch_shapes=[
            pltpu.VMEM((NS, width), f32), pltpu.VMEM((L + 8, cols), f32),
            pltpu.VMEM((L + 8, cols), f32), pltpu.VMEM((dim, cols + LANES), f32),
            pltpu.VMEM((5, 8, cols), f32), pltpu.VMEM((8, width), f32),
            pltpu.VMEM((16, LANES), f32),
        ],
        out_shape=[
            shape((tokens, cols + LANES), bf16), shape((dim, cols + LANES), bf16),
            shape((5, 8, cols), f32), shape((8, width), f32), shape((16, LANES), f32),
        ],
        compiler_params=params(),
        name="mix_backward",
    )(xbc, xbc, step_raw, mixed, sin, gm, normed, conv, bias, dtb, rate, dsk)

    grad_w_x = scatter_sum(gw_x[:, :width], rs_a, "dp")
    grad_rest = scatter_sum(gw_x[:, width:], rs_b, "dp")
    grad_w_bc = grad_rest[:, : 2 * NS]
    grad_w_bc = grad_w_bc + swap(grad_w_bc, 1, "tensor")
    grad_w_dt = grad_rest[:, 2 * NS : 2 * NS + heads]

    dn, g_gin = pl.pallas_call(
        input_back_kernel,
        grid_spec=pltpu.PrefetchScalarGridSpec(
            num_scalar_prefetch=1,
            grid=(chunks,),
            in_specs=[
                half_spec, half_spec, wide, rows_spec(L, cols + LANES), full((dim, 2 * width)),
                full((dim, cols + LANES)),
            ],
            out_specs=[rows_spec(L, dim), full((8, dim))],
            scratch_shapes=[pltpu.VMEM((8, dim), f32)],
        ),
        out_shape=[shape((tokens, dim), bf16), shape((8, dim), f32)],
        compiler_params=params(),
        name="input_backward",
    )(place1, resid, resid_oth, ggate, gx, wz, wx)
    dn_own = half_of(dn, place)
    dn_oth = swap(half_of(dn, 1 - place), 1, "tensor")

    dspec = rows_spec(L, dim)
    block_out, grad_resid = pl.pallas_call(
        finish_kernel,
        grid=(half,),
        in_specs=[dspec, dspec, full((1, dim)), dspec, dspec, dspec, dspec],
        out_specs=[dspec, dspec],
        out_shape=[shape((half_rows, dim), bf16), shape((half_rows, dim), f32)],
        compiler_params=params(),
        name="finish",
    )(resid, cotangent, gin, dn_own, dn_oth, branch_own, branch_oth)

    conv_sum = jnp.sum(g_conv, axis=1)
    both = jnp.concatenate([conv_sum[:, width:].reshape(-1), jnp.sum(g_gin, axis=0)])
    both = both + swap(both, 1, "tensor")
    head_sum = jnp.sum(g_head.reshape(2, 8, LANES), axis=1)[:, :heads]
    skip_sum = jnp.sum(g_skip, axis=0).reshape(heads, HEAD).sum(axis=1)
    flat = [
        conv_sum[:, :width].reshape(-1), both, jnp.sum(g_gout, axis=0), head_sum.reshape(-1),
        skip_sum,
    ]
    sizes = [v.shape[0] for v in flat]
    vec = jnp.concatenate(flat)
    for bit in bits:
        vec = vec + swap(vec, bit, "dp")
    out = []
    start = 0
    for count in sizes:
        out.append(vec[start : start + count])
        start += count
    conv_g = out[0].reshape(5, width)
    bc_g = out[1][: 10 * NS].reshape(5, 2 * NS)
    grad_gain_in = out[1][10 * NS :]
    head_g = out[3].reshape(2, heads)
    return (
        block_out, grad_resid, grad_gain_in, grad_w_z, grad_w_x, grad_w_bc, grad_w_dt,
        conv_g[:4], conv_g[4], bc_g[:4], bc_g[4], head_g[0], head_g[1], out[4], out[2],
        grad_w_out,
    )


def solution(mesh):
    in_specs = (
        P(("dp", "tensor"), None),
        P(),
        P("dp", "tensor"),
        P("dp", "tensor"),
        P("dp", None),
        P("dp", "tensor"),
        P(None, "tensor"),
        P("tensor"),
        P(),
        P(),
        P("tensor"),
        P("tensor"),
        P("tensor"),
        P("tensor"),
        P("tensor", "dp"),
        P(("dp", "tensor"), None),
    )
    out_specs = (
        P(("dp", "tensor"), None),
        P(("dp", "tensor"), None),
        P(),
        P("dp", "tensor"),
        P("dp", "tensor"),
        P("dp", None),
        P("dp", "tensor"),
        P(None, "tensor"),
        P("tensor"),
        P(),
        P(),
        P("tensor"),
        P("tensor"),
        P("tensor"),
        P("tensor"),
        P("tensor", "dp"),
    )
    return jax.shard_map(local, mesh=mesh, in_specs=in_specs, out_specs=out_specs, check_vma=False)
```

time: 1200 us -> 551 us (0.46)
  waiting for transfers between devices: 492 us -> 228 us
  matrix products: 256 us -> 0 us
  blocking collectives: 200 us -> 0 us
  Pallas kernels: 0 us -> 130 us
  starting transfers between devices: 0.52 us -> 115 us
  other arithmetic: 134 us -> 21.3 us
  local copies, waits for them, and re-layouts: 95.8 us -> 53.5 us
  between operations: 15.5 us -> 1.38 us
    reduce_scatter x6 -> x0, waiting for transfers between devices: 435 us -> none  [the longest x1 133 us: local(): lax.psum_scatter(grad_w_z, 'dp', scatter_dimension=0, tiled=True)]
    dot_general x29 -> x0, matrix products: 254 us -> none  [the longest x3 106 us: state_space(): jnp.einsum('cts,ctsh,cshp->cthp', intersection, decays, scaled, precision...]
    ppermute x0 -> x117, waiting for transfers between devices: none -> 228 us  [swap(): return lax.ppermute(v, axis, [(i, i ^ bit) for i in range(size)])]
    pallas_call x0 -> x6, Pallas kernels: none -> 130 us  [the longest x1 51 us: local(): pl.pallas_call(scan_back_kernel, grid=(chunks,), in_specs=[rows_spec(L, c...]
    psum x4 -> x0, blocking collectives: 117 us -> none  [the longest x1 75.3 us: local(): lax.psum((grad_conv_x, grad_bias_x, grad_conv_bc, grad_bias_bc, grad_dt_b...]
    ppermute x0 -> x117, starting transfers between devices: none -> 115 us  [swap(): return lax.ppermute(v, axis, [(i, i ^ bit) for i in range(size)])]
    all_gather x2 -> x0, blocking collectives: 83.4 us -> none  [the longest x1 42.8 us: local(): lax.all_gather(w_dt, 'dp', axis=0, tiled=True)]
    unnamed x14 -> x0, waiting for transfers between devices: 56.9 us -> none
  transfers between devices with their start and end apart: 13 -> 117, of which waited for: 5 -> 87; matrix products, arithmetic and copies ran while one was open for 24% -> 12% of each run, Pallas kernels for 0% -> 7%
where the time goes in v1:
time: 551 us; the launch traced here: 549 us
  waiting for transfers between devices  228 us (41%)
  Pallas kernels  130 us (24%)
  starting transfers between devices  115 us (21%)
  local copies, waits for them, and re-layouts  53.5 us (10%)
  other arithmetic  21.3 us (4%)
    ppermute x117, waiting for transfers between devices, swap(): return lax.ppermute(v, axis, [(i, i ^ bit) for i in range(size)])  228 us
    ppermute x117, starting transfers between devices, swap(): return lax.ppermute(v, axis, [(i, i ^ bit) for i in range(size)])  115 us
    pallas_call x1, Pallas kernels, local(): pl.pallas_call(scan_back_kernel, grid=(chunks,), in_specs=[rows_spec(L, c...  51 us
    unnamed x127, local copies, waits for them, and re-layouts  26.2 us
    pallas_call x1, Pallas kernels, local(): pl.pallas_call(forward_kernel, grid_spec=pltpu.PrefetchScalarGridSpec(num...  25.3 us
    pallas_call x1, Pallas kernels, local(): pl.pallas_call(gate_back_kernel, grid_spec=pltpu.PrefetchScalarGridSpec(n...  20.6 us
    pallas_call x1, Pallas kernels, local(): pl.pallas_call(gate_kernel, grid_spec=pltpu.PrefetchScalarGridSpec(num_sc...  13.7 us
    pallas_call x1, Pallas kernels, local(): pl.pallas_call(input_back_kernel, grid_spec=pltpu.PrefetchScalarGridSpec(...  13.3 us
  transfers between devices with their start and end apart: 117, of which 87 were waited for; matrix products, arithmetic and copies ran while one was open for 12% of the time, Pallas kernels for 7%

profile of v1, /device:TPU:0, one launch (start us, length us, event | category | flops | bytes accessed | tf_op | source)
XLA Modules:
  0.0 549.1 jit_solution(1131269519591160163)
XLA Ops:
  44.5 3.7 collective-permute-done.18
  52.8 3.7 collective-permute-done.33
  91.8 3.3 collective-permute-done.20
  95.5 3.6 collective-permute-done.7
  103.4 3.6 collective-permute-done.22
  107.7 3.3 collective-permute-done.34
  130.9 4.2 collective-permute-done.85
  135.9 3.9 collective-permute-done.86
  174.4 3.3 collective-permute-done.23
  178.7 3.8 collective-permute-done.24
  190.9 3.5 collective-permute-done.26
  194.9 3.5 collective-permute-done.27
  202.8 3.5 collective-permute-done.15
  210.7 3.5 collective-permute-done.30
  219.2 3.8 collective-permute-done.39
  224.1 3.8 collective-permute-done.40
  228.9 3.8 collective-permute-done.41
  233.8 3.8 collective-permute-done.42
  250.0 3.7 collective-permute-done.64
  263.5 3.3 collective-permute-done.67
  273.1 3.6 collective-permute-done.16
  280.9 3.8 collective-permute-done.46
  290.1 3.6 collective-permute-done.53
  298.9 3.3 collective-permute-done.72
  325.5 25.3 %mix_forward.1 = (bf16[2048,768]{1,0:T(8,128)(2,1)}, bf16[2048,1024]{1,0:T(8,128)(2,1)}, f32[2048,128]{1,0:T(8,128)S(1)}, f32[2048,768]{1,0:T(8,128)}, f32[8,128,768]{2,1,0:T(8,128)}) custom-call(s32[1]{0:T(128)} %bitcast.place, bf16[1024,768]{1,0:T(8,128)(2,1)} %resid.1, bf16[1024,768]{1,0:T(8,128)(2,1)} %copy-done.4, f32[1,768]{1,0:T(1,128)S(1)} %broadcast_in_dim.19.gin, ...), custom_call_target="tpu_custom_call" | custom-call | tf_op jit(solution)/shard_map/mix_forward/pallas_call | solution.py:494
  352.0 13.7 %gate_forward.1 = (bf16[2048,768]{1,0:T(8,128)(2,1)}, f32[2048,768]{1,0:T(8,128)}, f32[2048,128]{1,0:T(8,128)S(1)}) custom-call(s32[1]{0:T(128)} %bitcast.place, bf16[1024,768]{1,0:T(8,128)(2,1)} %cot.1, bf16[1024,768]{1,0:T(8,128)(2,1)} %copy-done.3, bf16[2048,768]{1,0:T(8,128)(2,1)} %get-tuple-element.38.normed, f32[2048,768]{1,0:T(8,128)} %get-tuple-element.39.mixed, ...), custom_call_target="tpu_custom_call" | custom-call | tf_op jit(solution)/shard_map/gate_forward/pallas_call | solution.py:517
  369.4 20.6 %gate_backward.1 = (bf16[2048,768]{1,0:T(8,128)(2,1)}, bf16[2048,768]{1,0:T(8,128)(2,1)}, bf16[2048,768]{1,0:T(8,128)(2,1)}, bf16[768,1536]{1,0:T(8,128)(2,1)}, f32[8,768]{1,0:T(8,128)S(1)}) custom-call(s32[1]{0:T(128)} %bitcast.place, bf16[1024,768]{1,0:T(8,128)(2,1)} %cot.1, bf16[1024,768]{1,0:T(8,128)(2,1)} %copy-done.3, ...), custom_call_target="tpu_custom_call" | custom-call | tf_op jit(solution)/shard_map/gate_backward/pallas_call | solution.py:536
  390.0 51.0 %mix_backward.1 = (bf16[2048,1152]{1,0:T(8,128)(2,1)}, bf16[768,1152]{1,0:T(8,128)(2,1)}, f32[5,8,1024]{2,1,0:T(8,128)S(1)}, f32[8,768]{1,0:T(8,128)S(1)}, f32[16,128]{1,0:T(8,128)S(1)}) custom-call(bf16[2048,1024]{1,0:T(8,128)(2,1)} %get-tuple-element.44.xbc.xprev, bf16[2048,1024]{1,0:T(8,128)(2,1)} %get-tuple-element.44.xbc.xprev, ...), custom_call_target="tpu_custom_call" | custom-call | tf_op jit(solution)/shard_map/mix_backward/pallas_call | solution.py:574
  449.0 13.3 %input_backward.1 = (bf16[2048,768]{1,0:T(8,128)(2,1)}, f32[8,768]{1,0:T(8,128)S(1)}) custom-call(s32[1]{0:T(128)} %bitcast.place, bf16[1024,768]{1,0:T(8,128)(2,1)S(1)} %copy-done.1, bf16[1024,768]{1,0:T(8,128)(2,1)} %copy-done.4, bf16[2048,768]{1,0:T(8,128)(2,1)} %get-tuple-element.43.ggate, bf16[2048,1152]{1,0:T(8,128)(2,1)} %get-tuple-element.48.gx, ...), custom_call_target="tpu_custom_call" | custom-call | tf_op jit(solution)/shard_map/input_backward/pallas_call | solution.py:609
  481.5 13.3 %collective-permute-done.99 = f32[6692]{0:T(1024)S(1)} collective-permute-done((f32[6692]{0:T(1024)S(1)}, f32[6692]{0:T(1024)S(1)}, u32[]{:S(2)}, u32[]{:S(2)}) %collective-permute-start.99) | collective-permute-done | bytes 26800 | tf_op jit(solution)/shard_map/ppermute | solution.py:379
  525.5 3.2 collective-permute-done.101
  542.9 6.2 %finish.1 = (bf16[1024,768]{1,0:T(8,128)(2,1)}, f32[1024,768]{1,0:T(8,128)}) custom-call(bf16[1024,768]{1,0:T(8,128)(2,1)S(1)} %copy-done.1, bf16[1024,768]{1,0:T(8,128)(2,1)} %cot.1, f32[1,768]{1,0:T(1,128)S(1)} %broadcast_in_dim.19.gin, bf16[1024,768]{1,0:T(8,128)(2,1)} %get-tuple-element.113.dn_own, bf16[1024,768]{1,0:T(8,128)(2,1)} %collective-permute-done.93.dn_oth, ...), custom_call_target="tpu_custom_call" | custom-call | tf_op jit(solution)/shard_map/finish/pallas_call | solution.py:629
  (438 shorter events, 314.1 us)
Async XLA Ops:
  1.5 71.6 %collective-permute-start.62 = (bf16[48,640]{1,0:T(8,128)(2,1)S(1)}, bf16[48,640]{1,0:T(8,128)(2,1)S(1)}, u32[]{:S(2)}, u32[]{:S(2)}) collective-permute-start(bf16[48,640]{1,0:T(8,128)(2,1)S(1)} %get-tuple-element.109), channel_id=1, source_target_pairs={{0,2},{2,0},{4,6},{6,4},{8,10},{10,8},{12,14},{14,12},{16,18},{18,... | collective-permute-start | bytes 184328 | tf_op jit(solution)/shard_map/ppermute | solution.py:379
  4.5 70.1 %collective-permute-start.63 = (bf16[48,640]{1,0:T(8,128)(2,1)S(1)}, bf16[48,640]{1,0:T(8,128)(2,1)S(1)}, u32[]{:S(2)}, u32[]{:S(2)}) collective-permute-start(bf16[48,640]{1,0:T(8,128)(2,1)S(1)} %get-tuple-element.109), channel_id=1, source_target_pairs={{0,4},{2,6},{4,0},{6,2},{8,12},{10,14},{12,8},{14,10},{16,20},{18,... | collective-permute-start | bytes 184328 | tf_op jit(solution)/shard_map/ppermute | solution.py:379
  6.1 243.9 %collective-permute-start.65 = (bf16[48,640]{1,0:T(8,128)(2,1)S(1)}, bf16[48,640]{1,0:T(8,128)(2,1)S(1)}, u32[]{:S(2)}, u32[]{:S(2)}) collective-permute-start(bf16[48,640]{1,0:T(8,128)(2,1)S(1)} %get-tuple-element.109), channel_id=1, source_target_pairs={{0,8},{2,10},{4,12},{6,14},{8,0},{10,2},{12,4},{14,6},{16,24},{18,... | collective-permute-start | bytes 184328 | tf_op jit(solution)/shard_map/ppermute | solution.py:379
  7.6 260.9 %collective-permute-start.69 = (bf16[48,640]{1,0:T(8,128)(2,1)S(1)}, bf16[48,640]{1,0:T(8,128)(2,1)S(1)}, u32[]{:S(2)}, u32[]{:S(2)}) collective-permute-start(bf16[48,640]{1,0:T(8,128)(2,1)S(1)} %get-tuple-element.109), channel_id=1, source_target_pairs={{0,16},{2,18},{4,20},{6,22},{8,24},{10,26},{12,28},{14,30},{16,0},... | collective-permute-start | bytes 184328 | tf_op jit(solution)/shard_map/ppermute | solution.py:379
  11.6 15.5 %collective-permute-start.77 = (bf16[48,256]{1,0:T(8,128)(2,1)}, bf16[48,256]{1,0:T(8,128)(2,1)}, u32[]{:S(2)}, u32[]{:S(2)}) collective-permute-start(bf16[48,256]{1,0:T(8,128)(2,1)} %slice.120), channel_id=1, source_target_pairs={{0,2},{2,0},{4,6},{6,4},{8,10},{10,8},{12,14},{14,12},{16,18},{18,... | collective-permute-start | bytes 73736 | tf_op jit(solution)/shard_map/ppermute | solution.py:379
  72.3 57.8 %collective-permute-start.84 = (bf16[48,256]{1,0:T(8,128)(2,1)}, bf16[48,256]{1,0:T(8,128)(2,1)S(1)}, u32[]{:S(2)}, u32[]{:S(2)}) collective-permute-start(bf16[48,256]{1,0:T(8,128)(2,1)} %slice.120), channel_id=1, source_target_pairs={{0,16},{2,18},{4,20},{6,22},{8,24},{10,26},{12,28},{14,30},{16,0},... | collective-permute-start | bytes 73736 | tf_op jit(solution)/shard_map/ppermute | solution.py:379
  81.5 180.8 %collective-permute-start.50 = (bf16[48,640]{1,0:T(8,128)(2,1)S(1)}, bf16[48,640]{1,0:T(8,128)(2,1)S(1)}, u32[]{:S(2)}, u32[]{:S(2)}) collective-permute-start(bf16[48,640]{1,0:T(8,128)(2,1)S(1)} %slice.97), channel_id=1, source_target_pairs={{0,8},{2,10},{4,12},{6,14},{8,0},{10,2},{12,4},{14,6},{16,24},{18,... | collective-permute-start | bytes 184328 | tf_op jit(solution)/shard_map/ppermute | solution.py:379
  126.7 13.9 %collective-permute-start.9 = (bf16[48,384]{1,0:T(8,128)(2,1)S(1)}, bf16[48,384]{1,0:T(8,128)(2,1)S(1)}, u32[]{:S(2)}, u32[]{:S(2)}) collective-permute-start(bf16[48,384]{1,0:T(8,128)(2,1)S(1)} %copy-done.18), channel_id=1, source_target_pairs={{0,16},{2,18},{4,20},{6,22},{8,24},{10,26},{12,28},{14,30},{16,0},... | collective-permute-start | bytes 110600 | tf_op jit(solution)/shard_map/ppermute | solution.py:379
  144.6 18.3 %collective-permute-start.10 = (bf16[48,384]{1,0:T(8,128)(2,1)S(1)}, bf16[48,384]{1,0:T(8,128)(2,1)S(1)}, u32[]{:S(2)}, u32[]{:S(2)}) collective-permute-start(bf16[48,384]{1,0:T(8,128)(2,1)S(1)} %collective-permute-done.9), channel_id=1, source_target_pairs={{0,2},{2,0},{4,6},{6,4},{8,10},{10,8},{12,14},{14,12},{16,18},{18,... | collective-permute-start | bytes 110600 | tf_op jit(solution)/shard_map/ppermute | solution.py:379
  162.9 131.8 %collective-permute-start.54 = (bf16[48,640]{1,0:T(8,128)(2,1)S(1)}, bf16[48,640]{1,0:T(8,128)(2,1)S(1)}, u32[]{:S(2)}, u32[]{:S(2)}) collective-permute-start(bf16[48,640]{1,0:T(8,128)(2,1)S(1)} %slice.97), channel_id=1, source_target_pairs={{0,16},{2,18},{4,20},{6,22},{8,24},{10,26},{12,28},{14,30},{16,0},... | collective-permute-start | bytes 184328 | tf_op jit(solution)/shard_map/ppermute | solution.py:379
  249.9 74.4 %collective-permute-start = (bf16[1024,768]{1,0:T(8,128)(2,1)S(1)}, bf16[1024,768]{1,0:T(8,128)(2,1)S(1)}, u32[]{:S(2)}, u32[]{:S(2)}) collective-permute-start(bf16[1024,768]{1,0:T(8,128)(2,1)S(1)} %copy-done), channel_id=1, source_target_pairs={{0,1},{1,0},{2,3},{3,2},{4,5},{5,4},{6,7},{7,6},{8,9},{9,8},{10,11... | collective-permute-start | bytes 4718600 | tf_op jit(solution)/shard_map/ppermute | solution.py:379
  262.3 88.5 %collective-permute-start.1 = (bf16[1024,768]{1,0:T(8,128)(2,1)S(1)}, bf16[1024,768]{1,0:T(8,128)(2,1)S(1)}, u32[]{:S(2)}, u32[]{:S(2)}) collective-permute-start(bf16[1024,768]{1,0:T(8,128)(2,1)S(1)} %copy-done.2), channel_id=1, source_target_pairs={{0,1},{1,0},{2,3},{3,2},{4,5},{5,4},{6,7},{7,6},{8,9},{9,8},{10,11... | collective-permute-start | bytes 4718600 | tf_op jit(solution)/shard_map/ppermute | solution.py:379
  271.0 24.0 %collective-permute-start.70 = (bf16[48,640]{1,0:T(8,128)(2,1)S(1)}, bf16[48,640]{1,0:T(8,128)(2,1)S(1)}, u32[]{:S(2)}, u32[]{:S(2)}) collective-permute-start(bf16[48,640]{1,0:T(8,128)(2,1)S(1)} %collective-permute-done.69), channel_id=1, source_target_pairs={{0,2},{2,0},{4,6},{6,4},{8,10},{10,8},{12,14},{14,12},{16,18},{18,... | collective-permute-start | bytes 184328 | tf_op jit(solution)/shard_map/ppermute | solution.py:379
  294.7 8.4 %collective-permute-start.73 = (bf16[48,640]{1,0:T(8,128)(2,1)S(1)}, bf16[48,640]{1,0:T(8,128)(2,1)S(1)}, u32[]{:S(2)}, u32[]{:S(2)}) collective-permute-start(bf16[48,640]{1,0:T(8,128)(2,1)S(1)} %collective-permute-done.69), channel_id=1, source_target_pairs={{0,8},{2,10},{4,12},{6,14},{8,0},{10,2},{12,4},{14,6},{16,24},{18,... | collective-permute-start | bytes 184328 | tf_op jit(solution)/shard_map/ppermute | solution.py:379
  295.0 8.4 %collective-permute-start.55 = (bf16[48,640]{1,0:T(8,128)(2,1)S(1)}, bf16[48,640]{1,0:T(8,128)(2,1)S(1)}, u32[]{:S(2)}, u32[]{:S(2)}) collective-permute-start(bf16[48,640]{1,0:T(8,128)(2,1)S(1)} %collective-permute-done.54), channel_id=1, source_target_pairs={{0,2},{2,0},{4,6},{6,4},{8,10},{10,8},{12,14},{14,12},{16,18},{18,... | collective-permute-start | bytes 184328 | tf_op jit(solution)/shard_map/ppermute | solution.py:379
  303.4 8.2 %collective-permute-start.74 = (bf16[48,640]{1,0:T(8,128)(2,1)S(1)}, bf16[48,640]{1,0:T(8,128)(2,1)S(1)}, u32[]{:S(2)}, u32[]{:S(2)}) collective-permute-start(bf16[48,640]{1,0:T(8,128)(2,1)S(1)} %collective-permute-done.73), channel_id=1, source_target_pairs={{0,2},{2,0},{4,6},{6,4},{8,10},{10,8},{12,14},{14,12},{16,18},{18,... | collective-permute-start | bytes 184328 | tf_op jit(solution)/shard_map/ppermute | solution.py:379
  307.4 10.1 %collective-permute-start.75 = (bf16[48,640]{1,0:T(8,128)(2,1)S(1)}, bf16[48,640]{1,0:T(8,128)(2,1)S(1)}, u32[]{:S(2)}, u32[]{:S(2)}) collective-permute-start(bf16[48,640]{1,0:T(8,128)(2,1)S(1)} %collective-permute-done.73), channel_id=1, source_target_pairs={{0,4},{2,6},{4,0},{6,2},{8,12},{10,14},{12,8},{14,10},{16,20},{18,... | collective-permute-start | bytes 184328 | tf_op jit(solution)/shard_map/ppermute | solution.py:379
  446.9 62.5 %collective-permute-start.113 = (bf16[2,2,2,48,768]{4,3,0,1,2:T(8,128)(2,1)}, bf16[2,2,2,48,768]{4,3,0,1,2:T(8,128)(2,1)}, u32[]{:S(2)}, u32[]{:S(2)}) collective-permute-start(bf16[2,2,2,48,768]{4,3,0,1,2:T(8,128)(2,1)} %bitcast.294), channel_id=1, source_target_pairs={{0,4},{2,6},{4,0},{6,2},{8,12},{10,14},{12,8},{14,10},{16,20},{18,... | collective-permute-start | bytes 1769480 | tf_op jit(solution)/shard_map/ppermute | solution.py:379
  448.0 29.4 %collective-permute-start.108 = (bf16[2,2,2,48,384]{4,3,2,1,0:T(8,128)(2,1)S(1)}, bf16[2,2,2,48,384]{4,3,2,1,0:T(8,128)(2,1)}, u32[]{:S(2)}, u32[]{:S(2)}) collective-permute-start(bf16[2,2,2,48,384]{4,3,2,1,0:T(8,128)(2,1)S(1)} %dynamic-slice_bitcast_fusion), channel_id=1, source_target_pairs={{0,4},{2,6},{4,0},{6,2},{8,12},{10,14},{12,8},{14,10},{16,20},{18,... | collective-permute-start | bytes 884744 | tf_op jit(solution)/shard_map/ppermute | solution.py:379
  465.2 46.0 %collective-permute-start.104 = (bf16[2,2,2,48,768]{4,3,0,1,2:T(8,128)(2,1)S(1)}, bf16[2,2,2,48,768]{4,3,0,1,2:T(8,128)(2,1)}, u32[]{:S(2)}, u32[]{:S(2)}) collective-permute-start(bf16[2,2,2,48,768]{4,3,0,1,2:T(8,128)(2,1)S(1)} %bitcast.318), channel_id=1, source_target_pairs={{0,2},{2,0},{4,6},{6,4},{8,10},{10,8},{12,14},{14,12},{16,18},{18,... | collective-permute-start | bytes 1769480 | tf_op jit(solution)/shard_map/ppermute | solution.py:379
  470.6 43.1 %collective-permute-start.100 = (bf16[2,2,2,48,768]{4,3,0,1,2:T(8,128)(2,1)}, bf16[2,2,2,48,768]{4,3,0,1,2:T(8,128)(2,1)}, u32[]{:S(2)}, u32[]{:S(2)}) collective-permute-start(bf16[2,2,2,48,768]{4,3,0,1,2:T(8,128)(2,1)} %bitcast.296), channel_id=1, source_target_pairs={{0,2},{2,0},{4,6},{6,4},{8,10},{10,8},{12,14},{14,12},{16,18},{18,... | collective-permute-start | bytes 1769480 | tf_op jit(solution)/shard_map/ppermute | solution.py:379
  476.4 18.4 %collective-permute-start.99 = (f32[6692]{0:T(1024)S(1)}, f32[6692]{0:T(1024)S(1)}, u32[]{:S(2)}, u32[]{:S(2)}) collective-permute-start(f32[6692]{0:T(1024)S(1)} %add.152), channel_id=1, source_target_pairs={{0,2},{2,0},{4,6},{6,4},{8,10},{10,8},{12,14},{14,12},{16,18},{18,... | collective-permute-start | bytes 80312 | tf_op jit(solution)/shard_map/ppermute | solution.py:379
  478.5 18.2 %collective-permute-start.109 = (bf16[2,2,48,384]{3,2,1,0:T(8,128)(2,1)S(1)}, bf16[2,2,48,384]{3,2,1,0:T(8,128)(2,1)S(1)}, u32[]{:S(2)}, u32[]{:S(2)}) collective-permute-start(bf16[2,2,48,384]{3,2,1,0:T(8,128)(2,1)S(1)} %fusion.5), channel_id=1, source_target_pairs={{0,2},{2,0},{4,6},{6,4},{8,10},{10,8},{12,14},{14,12},{16,18},{18,... | collective-permute-start | bytes 442376 | tf_op jit(solution)/shard_map/ppermute | solution.py:379
  494.7 48.2 %collective-permute-start.93 = (bf16[1024,768]{1,0:T(8,128)(2,1)}, bf16[1024,768]{1,0:T(8,128)(2,1)}, u32[]{:S(2)}, u32[]{:S(2)}) collective-permute-start(bf16[1024,768]{1,0:T(8,128)(2,1)} %get-tuple-element.112), channel_id=1, source_target_pairs={{0,1},{1,0},{2,3},{3,2},{4,5},{5,4},{6,7},{7,6},{8,9},{9,8},{10,11... | collective-permute-start | bytes 4718600 | tf_op jit(solution)/shard_map/ppermute | solution.py:379
  507.8 35.1 %collective-permute-start.94 = (bf16[1024,768]{1,0:T(8,128)(2,1)}, bf16[1024,768]{1,0:T(8,128)(2,1)}, u32[]{:S(2)}, u32[]{:S(2)}) collective-permute-start(bf16[1024,768]{1,0:T(8,128)(2,1)} %get-tuple-element.110), channel_id=1, source_target_pairs={{0,1},{1,0},{2,3},{3,2},{4,5},{5,4},{6,7},{7,6},{8,9},{9,8},{10,11... | collective-permute-start | bytes 4718600 | tf_op jit(solution)/shard_map/ppermute | solution.py:379
  511.2 9.0 %collective-permute-start.114 = (bf16[2,2,48,768]{3,2,0,1:T(8,128)(2,1)S(1)}, bf16[2,2,48,768]{3,2,0,1:T(8,128)(2,1)S(1)}, u32[]{:S(2)}, u32[]{:S(2)}) collective-permute-start(bf16[2,2,48,768]{3,2,0,1:T(8,128)(2,1)S(1)} %fusion.2), channel_id=1, source_target_pairs={{0,2},{2,0},{4,6},{6,4},{8,10},{10,8},{12,14},{14,12},{16,18},{18,... | collective-permute-start | bytes 884744 | tf_op jit(solution)/shard_map/ppermute | solution.py:379
  513.7 10.0 %collective-permute-start.105 = (bf16[2,2,48,768]{3,2,0,1:T(8,128)(2,1)S(1)}, bf16[2,2,48,768]{3,2,0,1:T(8,128)(2,1)S(1)}, u32[]{:S(2)}, u32[]{:S(2)}) collective-permute-start(bf16[2,2,48,768]{3,2,0,1:T(8,128)(2,1)S(1)} %fusion.1), channel_id=1, source_target_pairs={{0,4},{2,6},{4,0},{6,2},{8,12},{10,14},{12,8},{14,10},{16,20},{18,... | collective-permute-start | bytes 884744 | tf_op jit(solution)/shard_map/ppermute | solution.py:379
  515.9 12.9 %collective-permute-start.101 = (bf16[2,2,48,768]{3,2,0,1:T(8,128)(2,1)S(1)}, bf16[2,2,48,768]{3,2,0,1:T(8,128)(2,1)S(1)}, u32[]{:S(2)}, u32[]{:S(2)}) collective-permute-start(bf16[2,2,48,768]{3,2,0,1:T(8,128)(2,1)S(1)} %fusion), channel_id=1, source_target_pairs={{0,4},{2,6},{4,0},{6,2},{8,12},{10,14},{12,8},{14,10},{16,20},{18,... | collective-permute-start | bytes 884744 | tf_op jit(solution)/shard_map/ppermute | solution.py:379
  520.2 10.3 %collective-permute-start.115 = (bf16[2,48,768]{2,1,0:T(8,128)(2,1)S(1)}, bf16[2,48,768]{2,1,0:T(8,128)(2,1)S(1)}, u32[]{:S(2)}, u32[]{:S(2)}) collective-permute-start(bf16[2,48,768]{2,1,0:T(8,128)(2,1)S(1)} %fusion.6), channel_id=1, source_target_pairs={{0,8},{2,10},{4,12},{6,14},{8,0},{10,2},{12,4},{14,6},{16,24},{18,... | collective-permute-start | bytes 442376 | tf_op jit(solution)/shard_map/ppermute | solution.py:379
  523.8 7.8 %collective-permute-start.106 = (bf16[2,48,768]{2,1,0:T(8,128)(2,1)S(1)}, bf16[2,48,768]{2,1,0:T(8,128)(2,1)S(1)}, u32[]{:S(2)}, u32[]{:S(2)}) collective-permute-start(bf16[2,48,768]{2,1,0:T(8,128)(2,1)S(1)} %fusion.4), channel_id=1, source_target_pairs={{0,8},{2,10},{4,12},{6,14},{8,0},{10,2},{12,4},{14,6},{16,24},{18,... | collective-permute-start | bytes 442376 | tf_op jit(solution)/shard_map/ppermute | solution.py:379
  530.7 9.1 %collective-permute-start.116 = (bf16[48,768]{1,0:T(8,128)(2,1)S(1)}, bf16[48,768]{1,0:T(8,128)(2,1)S(1)}, u32[]{:S(2)}, u32[]{:S(2)}) collective-permute-start(bf16[48,768]{1,0:T(8,128)(2,1)S(1)} %fusion.11), channel_id=1, source_target_pairs={{0,16},{2,18},{4,20},{6,22},{8,24},{10,26},{12,28},{14,30},{16,0},... | collective-permute-start | bytes 221192 | tf_op jit(solution)/shard_map/ppermute | solution.py:379
  531.7 9.0 %collective-permute-start.107 = (bf16[48,768]{1,0:T(8,128)(2,1)S(1)}, bf16[48,768]{1,0:T(8,128)(2,1)S(1)}, u32[]{:S(2)}, u32[]{:S(2)}) collective-permute-start(bf16[48,768]{1,0:T(8,128)(2,1)S(1)} %fusion.9), channel_id=1, source_target_pairs={{0,16},{2,18},{4,20},{6,22},{8,24},{10,26},{12,28},{14,30},{16,0},... | collective-permute-start | bytes 221192 | tf_op jit(solution)/shard_map/ppermute | solution.py:379
  (104 other events, 1167.1 us)

commit v2 on v1

v2 whole, which is shorter than its diff:
```python
import functools

import jax
import jax.numpy as jnp
from jax import lax
from jax.experimental import pallas as pl
from jax.experimental.pallas import tpu as pltpu
from jax.sharding import PartitionSpec as P

NS = 128
L = 256
SEQ_LEN = 2048
HEAD = 64
LANES = 128
VMEM = 52 * 1024 * 1024

f32 = jnp.float32
bf16 = jnp.bfloat16
highest = lax.Precision.HIGHEST
eps = 1e-05

NN = (((1,), (0,)), ((), ()))
NT = (((1,), (1,)), ((), ()))
TN = (((0,), (0,)), ((), ()))


def mm(a, b, dims=NN, precision=None):
    return lax.dot_general(a, b, dims, precision=precision, preferred_element_type=f32)


def iota(shape, dim):
    return lax.broadcasted_iota(jnp.int32, shape, dim)


def lower_tri():
    return (iota((L, L), 0) >= iota((L, L), 1)).astype(f32)


def upper_tri():
    return (iota((L, L), 0) <= iota((L, L), 1)).astype(f32)


def expander(heads):
    rows = iota((LANES, heads * HEAD), 0)
    cols = iota((LANES, heads * HEAD), 1) // HEAD
    return ((rows % 16 == cols) & (rows < 48)).astype(bf16)


def collector(heads):
    rows = iota((heads * HEAD, LANES), 0) // HEAD
    cols = iota((heads * HEAD, LANES), 1)
    return ((cols % 16 == rows) & (cols < 48)).astype(bf16)


def pack3(q):
    lane = iota(q.shape, 1)
    hi = q.astype(bf16).astype(f32)
    rest = q - hi
    mid = rest.astype(bf16).astype(f32)
    return jnp.where(lane < 16, hi, jnp.where(lane < 32, mid, rest - mid)).astype(bf16)


def head_sums(q, col):
    hi = q.astype(bf16)
    lo = (q - hi.astype(f32)).astype(bf16)
    return mm(hi, col) + mm(lo, col)


def softplus(v):
    return jnp.maximum(v, 0.0) + jnp.log1p(jnp.exp(-jnp.abs(v)))


def fold8(q):
    return jnp.sum(q.reshape(q.shape[0] // 8, 8, q.shape[1]), axis=0)


def spread(steps, within, expand):
    tails = jnp.exp(within[L - 1 : L, :] - within)
    return (
        mm(pack3(steps), expand),
        mm(pack3(jnp.exp(within)), expand),
        mm(pack3(tails), expand),
    )


def load_rows(info, pieces, places, w, sem, cols=slice(None)):
    copies = []
    for piece, (offset, masks) in zip(pieces, places):
        count = piece.shape[1]
        for k, mask in enumerate(masks):
            slot = 0 if mask is None else (info[1] ^ mask)
            rows = pl.ds(pl.multiple_of(slot * count, 16), count)
            if cols == slice(None):
                src = piece.at[k]
                dst = w.at[rows, pl.ds(offset, piece.shape[2])]
            else:
                src = piece.at[k, :, cols]
                dst = w.at[rows, :]
            copies.append(pltpu.make_async_copy(src, dst, sem.at[len(copies)]))
    for copy in copies:
        copy.start()
    for copy in copies:
        copy.wait()


def store_rows(info, acc, outs, masks):
    at = 0
    for out in outs:
        count = out.shape[1]
        for k in range(out.shape[0]):
            mask = masks[at]
            slot = 0 if mask is None else (info[1] ^ mask)
            rows = pl.ds(pl.multiple_of(slot * count, 16), count)
            out[k] = acc[rows, :].astype(bf16)
            at += 1


def forward_kernel(places, info, own, oth, gin, conv, bias, dtb, rate, dsk, *rest):
    count = len(places)
    pieces = rest[:count]
    (normed_o, xbc_o, act_o, dsilu_o, step_o, within_o, mixed_o, sin_o, state, buf, w, sem) = rest[
        count:
    ]
    c = pl.program_id(0)
    half = pl.num_programs(0) // 2
    width = dsk.shape[1]
    heads = width // HEAD
    cols = width + 2 * NS

    @pl.when(c == 0)
    def _():
        load_rows(info, pieces, places, w, sem)
        state[...] = jnp.zeros_like(state)
        buf[0:8, :] = jnp.zeros((8, cols), f32)

    mine = (c // half) == info[0]
    r = jnp.where(mine, own[...].astype(f32), oth[...].astype(f32))
    inv = lax.rsqrt(jnp.mean(r * r, axis=1, keepdims=True) + eps)
    normed = (r * inv * gin[...]).astype(bf16)
    normed_o[...] = normed
    proj = mm(normed, w[...])
    xbc = proj[:, :cols].astype(bf16)
    step_raw = proj[:, cols:]
    xbc_o[...] = xbc
    step_o[...] = step_raw
    xin = xbc.astype(f32)
    buf[8:, :] = xin
    v = bias[...] + conv[3:4, :] * xin
    for k in range(3):
        v = v + conv[k : k + 1, :] * buf[5 + k : 5 + k + L, :]
    buf[0:8, :] = xin[L - 8 :, :]
    sig = jax.nn.sigmoid(v)
    act = (v * sig).astype(bf16)
    act_o[...] = act
    dsilu_o[...] = (sig * (1.0 + v * (1.0 - sig))).astype(bf16)
    x = act[:, :width].astype(f32)
    b = act[:, width : width + NS]
    cc = act[:, width + NS :]

    expand = expander(heads)
    steps = softplus(step_raw + dtb[...])
    within = mm(lower_tri(), steps * rate[...], precision=highest)
    within_o[...] = within
    steps_e, grown_e, tails_e = spread(steps, within, expand)
    within_t = within.T
    scaled = x * steps_e
    scaled_b = scaled.astype(bf16)
    inter = mm(cc, b, NT)
    sin = state[...]
    sin_o[0] = sin
    outside = mm(cc, sin.astype(bf16)) * grown_e
    state[...] = sin * grown_e[L - 1 : L, :] + mm(b, (scaled * tails_e).astype(bf16), TN)
    hl = L // 2
    tri = iota((hl, hl), 0) >= iota((hl, hl), 1)
    left = iota((hl, LANES), 1) < HEAD
    for pair in range(heads // 2):
        ps = slice(pair * LANES, (pair + 1) * LANES)
        x2 = scaled_b[:, ps]
        tops, bots = [], []
        for h in (2 * pair, 2 * pair + 1):
            wc = within[:, h : h + 1]
            wr = within_t[h : h + 1, :]
            d_tl = jnp.exp(jnp.where(tri, wc[:hl] - wr[:, :hl], -1e30))
            d_bl = jnp.exp(wc[hl:] - wr[:, :hl])
            d_br = jnp.exp(jnp.where(tri, wc[hl:] - wr[:, hl:], -1e30))
            tops.append((inter[:hl, :hl] * d_tl).astype(bf16))
            bots.append(
                jnp.concatenate(
                    [
                        (inter[hl:, :hl] * d_bl).astype(bf16),
                        (inter[hl:, hl:] * d_br).astype(bf16),
                    ],
                    axis=1,
                )
            )
        top = mm(jnp.concatenate(tops, axis=0), x2[:hl])
        bot = mm(jnp.concatenate(bots, axis=0), x2)
        skip = dsk[:, ps] * x[:, ps] + outside[:, ps]
        mixed_o[:hl, ps] = jnp.where(left, top[:hl], top[hl:]) + skip[:hl]
        mixed_o[hl:, ps] = jnp.where(left, bot[:hl], bot[hl:]) + skip[hl:]


def gate_kernel(places, info, cown, coth, normed, mixed, gout, *rest):
    count = len(places)
    pieces = rest[:count]
    gate_o, gno_o, sums_o, w, sem = rest[count:]
    c = pl.program_id(0)
    half = pl.num_programs(0) // 2
    width = gout.shape[1]

    @pl.when(c == 0)
    def _():
        load_rows(info, pieces, places, w, sem)

    mine = (c // half) == info[0]
    cot = jnp.where(mine, cown[...].astype(f32), coth[...].astype(f32)).astype(bf16)
    gate = mm(normed[...], w[:, :width]).astype(bf16)
    gate_o[...] = gate
    gf = gate.astype(f32)
    gated = mixed[...] * (gf * jax.nn.sigmoid(gf))
    gno = mm(cot, w[:, width:])
    gno_o[...] = gno
    squares = jnp.sum(gated * gated, axis=1, keepdims=True)
    products = jnp.sum(gno * gout[...] * gated, axis=1, keepdims=True)
    lane = iota((L, LANES), 1)
    sums = jnp.where(lane < 64, squares, products).T
    sums_o[0:8, :] = sums[0:8]
    sums_o[8:16, :] = sums[64:72]


def gate_back_kernel(
    places, masks, info, cown, coth, normed, mixed, gate, gno, sown, soth, gout, *rest
):
    count = len(places)
    pieces = rest[:count]
    rest = rest[count:]
    parts = len(rest) - 9
    (sent_o, kept_o, ggate_o, gm_o, ggo_o) = rest[:5]
    gw_o = rest[5 : 5 + parts]
    acc, acc_g, w, sem = rest[5 + parts :]
    c = pl.program_id(0)
    last = pl.num_programs(0) - 1
    half = pl.num_programs(0) // 2
    width = gout.shape[1]

    @pl.when(c == 0)
    def _():
        load_rows(info, pieces, places, w, sem, pl.ds(width, width))
        acc[...] = jnp.zeros_like(acc)
        acc_g[...] = jnp.zeros_like(acc_g)

    cot = jnp.where(c < half, coth[...].astype(f32), cown[...].astype(f32)).astype(bf16)
    s = sown[...] + soth[...]
    sums = jnp.concatenate(
        [jnp.broadcast_to(s[0:1], (64, L)), jnp.broadcast_to(s[8:9], (64, L))], axis=0
    ).T
    inner_total = 2.0 * width
    scale = lax.rsqrt(sums[:, 0:1] / inner_total + eps)
    coef = scale * scale * scale * (sums[:, 64:65] / inner_total)
    gf = gate[...].astype(f32)
    sig = jax.nn.sigmoid(gf)
    silu = gf * sig
    mix = mixed[...]
    gated = mix * silu
    grad = gno[...]
    unit = gated * scale
    normed_out = (unit * gout[...]).astype(bf16)
    branch = mm(normed_out, w[...], NT).astype(bf16)

    @pl.when(c < half)
    def _():
        sent_o[...] = branch

    @pl.when(c >= half)
    def _():
        kept_o[...] = branch

    acc_g[...] += fold8(grad * unit)
    grad_gated = scale * (grad * gout[...]) - gated * coef
    grad_gate = (grad_gated * mix * (sig + silu * (1.0 - sig))).astype(bf16)
    ggate_o[...] = grad_gate
    gm_o[...] = (grad_gated * silu).astype(bf16)
    acc[:, :width] += mm(normed[...], grad_gate, TN)
    acc[:, width:] += mm(cot, normed_out, TN)

    @pl.when(c == last)
    def _():
        store_rows(info, acc, gw_o, masks)
        ggo_o[...] = acc_g[...]


def scan_back_kernel(
    masks, info, xbc, act_r, dsilu, step, within_r, mixed, sin_r, gm, normed, conv, dtb, rate, dsk,
    gx_o, gconv_o, gskip_o, ghead_o, *rest,
):
    gw_o = rest[:-6]
    dstate, dvbuf, acc_w, acc_c, acc_s, acc_h = rest[-6:]
    i = pl.program_id(0)
    last = pl.num_programs(0) - 1
    width = dsk.shape[1]
    heads = width // HEAD
    cols = width + 2 * NS

    @pl.when(i == 0)
    def _():
        dstate[...] = jnp.zeros_like(dstate)
        dvbuf[...] = jnp.zeros_like(dvbuf)
        acc_w[...] = jnp.zeros_like(acc_w)
        acc_c[...] = jnp.zeros_like(acc_c)
        acc_s[...] = jnp.zeros_like(acc_s)
        acc_h[...] = jnp.zeros_like(acc_h)

    x = act_r[:, :width].astype(f32)
    b = act_r[:, width : width + NS]
    cc = act_r[:, width + NS :]

    expand = expander(heads)
    collect = collector(heads)
    step_raw = step[...]
    within = within_r[...]
    steps = softplus(step_raw + dtb[...])
    steps_e, grown_e, tails_e = spread(steps, within, expand)
    within_t = within.T
    scaled = x * steps_e
    scaled_b = scaled.astype(bf16)
    gmb = gm[...]
    gmf = gmb.astype(f32)
    sin = sin_r[0]
    ds = dstate[...]
    ds_b = ds.astype(bf16)
    inter_t = mm(b, cc, NT)
    state_part = mm(b, ds_b) * tails_e
    gm_grown = (gmf * grown_e).astype(bf16)
    last_grown = grown_e[L - 1 : L, :]
    dstate[...] = ds * last_grown + mm(cc, gm_grown, TN)
    hl = L // 2
    tri = iota((hl, hl), 0) <= iota((hl, hl), 1)
    left = iota((hl, LANES), 1) < HEAD
    leftw = iota((L, LANES), 1) < HEAD
    dg_tl = jnp.zeros((hl, hl), f32)
    dg_tr = jnp.zeros((hl, hl), f32)
    dg_br = jnp.zeros((hl, hl), f32)
    dscaled = []
    for pair in range(heads // 2):
        ps = slice(pair * LANES, (pair + 1) * LANES)
        x2 = scaled_b[:, ps]
        g2 = gmb[:, ps]
        zero = jnp.zeros_like(x2)
        xe = jnp.where(leftw, x2, zero)
        xo = jnp.where(leftw, zero, x2)
        dm_top = mm(jnp.concatenate([xe[:hl], xo[:hl]], axis=0), g2, NT)
        dm_bot = mm(jnp.concatenate([xe[hl:], xo[hl:]], axis=0), g2[hl:], NT)
        tops, bots = [], []
        for side, h in enumerate((2 * pair, 2 * pair + 1)):
            wc = within[:, h : h + 1]
            wr = within_t[h : h + 1, :]
            d_tl = jnp.exp(jnp.where(tri, wr[:, :hl] - wc[:hl], -1e30))
            d_tr = jnp.exp(wr[:, hl:] - wc[:hl])
            d_br = jnp.exp(jnp.where(tri, wr[:, hl:] - wc[hl:], -1e30))
            tops.append(
                jnp.concatenate(
                    [
                        (inter_t[:hl, :hl] * d_tl).astype(bf16),
                        (inter_t[:hl, hl:] * d_tr).astype(bf16),
                    ],
                    axis=1,
                )
            )
            bots.append((inter_t[hl:, hl:] * d_br).astype(bf16))
            rows = slice(side * hl, (side + 1) * hl)
            dg_tl += dm_top[rows, :hl] * d_tl
            dg_tr += dm_top[rows, hl:] * d_tr
            dg_br += dm_bot[rows] * d_br
        top = mm(jnp.concatenate(tops, axis=0), g2)
        bot = mm(jnp.concatenate(bots, axis=0), g2[hl:])
        dscaled.append(
            jnp.concatenate(
                [jnp.where(left, top[:hl], top[hl:]), jnp.where(left, bot[:hl], bot[hl:])], axis=0
            )
        )
    dscaled = jnp.concatenate(dscaled, axis=1) + state_part
    top = jnp.concatenate([dg_tl, dg_tr], axis=1)
    bot = jnp.concatenate([jnp.zeros((hl, hl), f32), dg_br], axis=1)
    dg = jnp.concatenate([top, bot], axis=0).astype(bf16)
    dc = mm(dg, b, TN) + mm(gm_grown, sin.astype(bf16), NT)
    db = mm(dg, cc) + mm((scaled * tails_e).astype(bf16), ds_b, NT)
    scaled_f = scaled_b.astype(f32)
    y = mixed[...] - dsk[...] * x
    q = gmf * y - scaled_f * dscaled
    ends = jnp.sum(scaled_f * state_part, axis=0, keepdims=True) + last_grown * jnp.sum(
        sin * ds, axis=0, keepdims=True
    )
    ends_h = head_sums(jnp.broadcast_to(ends, (8, width)), collect)[0:1, :]
    d_rate = mm(upper_tri(), head_sums(q, collect), precision=highest) + ends_h
    d_steps = d_rate * rate[...] + head_sums(dscaled * x, collect)
    sig_s = jax.nn.sigmoid(step_raw + dtb[...])
    keep = iota((L, LANES), 1) < heads
    d_raw = jnp.where(keep, d_steps * sig_s, 0.0)
    acc_h[0:8, :] += fold8(d_raw)
    acc_h[8:16, :] += fold8(d_rate * steps * rate[...])
    acc_s[...] += fold8(gmf * x)
    dx = dscaled * steps_e + dsk[...] * gmf

    dv = jnp.concatenate([dx, db, dc], axis=1) * dsilu[...].astype(f32)
    dvbuf[0:L, :] = dv
    xin = xbc[...].astype(f32)
    acc_c[4] += fold8(dv)
    acc_c[3] += fold8(dv * xin)
    dxin = conv[3:4, :] * dv
    for k in range(3):
        ahead = dvbuf[3 - k : 3 - k + L, :]
        acc_c[k] += fold8(ahead * xin)
        dxin = dxin + conv[k : k + 1, :] * ahead
    dvbuf[L : L + 8, :] = dv[0:8, :]
    gx = jnp.concatenate([dxin.astype(bf16), d_raw.astype(bf16)], axis=1)
    gx_o[...] = gx
    acc_w[...] += mm(normed[...], gx, TN)

    @pl.when(i == last)
    def _():
        store_rows(info, acc_w, gw_o, masks)
        gconv_o[...] = acc_c[...]
        gskip_o[...] = acc_s[...]
        ghead_o[...] = acc_h[...]


def input_back_kernel(zplaces, xplaces, info, own, oth, ggate, gx, *rest):
    zcount, xcount = len(zplaces), len(xplaces)
    zpieces = rest[:zcount]
    xpieces = rest[zcount : zcount + xcount]
    sent_o, kept_o, gain_o, wz, wx, zsem, xsem = rest[zcount + xcount :]
    c = pl.program_id(0)
    half = pl.num_programs(0) // 2
    width = ggate.shape[1]

    @pl.when(c == 0)
    def _():
        load_rows(info, zpieces, zplaces, wz, zsem, pl.ds(0, width))
        load_rows(info, xpieces, xplaces, wx, xsem)
        gain_o[...] = jnp.zeros_like(gain_o)

    r = jnp.where(c < half, oth[...].astype(f32), own[...].astype(f32))
    inv = lax.rsqrt(jnp.mean(r * r, axis=1, keepdims=True) + eps)
    dn = mm(ggate[...], wz[...], NT) + mm(gx[...], wx[...], NT)
    dnb = dn.astype(bf16)

    @pl.when(c < half)
    def _():
        sent_o[...] = dnb

    @pl.when(c >= half)
    def _():
        kept_o[...] = dnb

    gain_o[...] += fold8(dn * (r * inv))


def finish_kernel(resid, cot, gin, dn_own, dn_oth, br_own, br_oth, out_o, gres_o):
    r = resid[...].astype(f32)
    inv = lax.rsqrt(jnp.mean(r * r, axis=1, keepdims=True) + eps)
    out_o[...] = (r + (br_own[...].astype(f32) + br_oth[...].astype(f32))).astype(bf16)
    u = (dn_own[...].astype(f32) + dn_oth[...].astype(f32)) * gin[...]
    mean = jnp.mean(u * r, axis=1, keepdims=True)
    gres_o[...] = cot[...].astype(f32) + inv * u - r * (inv * inv * inv * mean)


def swap(v, bit, axis):
    size = lax.axis_size(axis)
    return lax.ppermute(v, axis, [(i, i ^ bit) for i in range(size)])


NEAR = (0, 1, 2, 3)
FAR = (0, 4, 8, 12)


def direct(size, rows):
    return size == 16 and rows % 16 == 0


def gather_whole(v, bits):
    size = lax.axis_size("dp")
    me = lax.axis_index("dp")
    held = v[None]
    for bit in sorted(bits):
        got = swap(held, bit, "dp")
        upper = (me & bit) != 0
        held = jnp.where(
            upper, jnp.concatenate([got, held]), jnp.concatenate([held, got])
        )
    return held.reshape(1, size * v.shape[0], v.shape[1])


def whole_pieces(v, bits):
    return [gather_whole(v, bits)], [(0, (None,))]


def gather_far(v):
    return [swap(v, far, "dp") for far in FAR[1:]]


def gather_near(held):
    pieces = [held] + [swap(held, near, "dp") for near in NEAR[1:]]
    return pieces, [(0, tuple(near ^ far for far in FAR)) for near in NEAR]


def scatter_shapes(size, rows, cols):
    if not direct(size, rows):
        return [jax.ShapeDtypeStruct((1, size * rows, cols), bf16)], (None,)
    masks = tuple(near ^ far for near in NEAR for far in FAR)
    return [jax.ShapeDtypeStruct((4, rows, cols), bf16)] * 4, masks


def scatter_near(pieces):
    return [pieces[0]] + [swap(p, near, "dp") for p, near in zip(pieces[1:], NEAR[1:])]


def scatter_far(total):
    sent = total.astype(bf16)
    return [total[0]] + [swap(sent[k], FAR[k], "dp") for k in range(1, 4)]


def sum_pieces(pieces):
    return sum(p.astype(f32) for p in pieces)


def scatter_whole(g, bits):
    me = lax.axis_index("dp")
    rows = g.shape[0] // lax.axis_size("dp")
    left = sorted(bits, reverse=True)
    cur = g.reshape([2] * len(left) + [rows, g.shape[1]])
    for bit in sorted(bits):
        dim = left.index(bit)
        mine = ((me & bit) != 0).astype(jnp.int32)
        send = lax.dynamic_index_in_dim(cur, 1 - mine, dim, keepdims=False)
        keep = lax.dynamic_index_in_dim(cur, mine, dim, keepdims=False)
        got = swap(send.astype(bf16), bit, "dp")
        cur = keep.astype(f32) + got.astype(f32)
        left.pop(dim)
    return cur.astype(f32)


def full(shape):
    zeros = (0,) * len(shape)
    return pl.BlockSpec(shape, lambda c, *_: zeros)


def rows_spec(count, width, index=lambda c, info: c):
    return pl.BlockSpec((count, width), lambda c, info: (index(c, info), 0))


def call(kernel, name, grid, ins, outs, scratch, info, *args):
    specs = [spec for spec, _ in outs]
    shapes = [item for _, item in outs]
    return pl.pallas_call(
        kernel,
        grid_spec=pltpu.PrefetchScalarGridSpec(
            num_scalar_prefetch=1, grid=(grid,), in_specs=ins, out_specs=specs,
            scratch_shapes=scratch,
        ),
        out_shape=shapes,
        compiler_params=pltpu.CompilerParams(
            dimension_semantics=("arbitrary",), vmem_limit_bytes=VMEM
        ),
        name=name,
    )(info, *args)


def local(
    resid, gain_in, w_z, w_x, w_bc, w_dt, conv_x, bias_x, conv_bc, bias_bc, dt_bias, a_log, d_skip,
    gain_out, w_out, cotangent,
):
    size = lax.axis_size("dp")
    place = lax.axis_index("tensor")
    heads = a_log.shape[0]
    width = heads * HEAD
    dim = resid.shape[1]
    rows = w_z.shape[0]
    cols = width + 2 * NS
    half_rows = resid.shape[0]
    tokens = 2 * half_rows
    assert tokens == SEQ_LEN
    chunks = tokens // L
    half = chunks // 2
    shape = jax.ShapeDtypeStruct
    bits = [1 << k for k in range(size.bit_length() - 1)]

    def lanes3(v):
        pad = [(0, 0)] * (v.ndim - 1)
        group = jnp.pad(v, pad + [(0, 16 - heads)])
        return jnp.pad(jnp.concatenate([group] * 3, axis=-1), pad + [(0, LANES - 48)])

    first = jnp.concatenate([w_x, w_bc, lanes3(w_dt)], axis=1)
    second = jnp.concatenate([w_z, w_out.T], axis=1)
    conv = jnp.concatenate([conv_x, conv_bc], axis=1)
    bias = jnp.concatenate([bias_x, bias_bc])[None]
    dtb = lanes3(dt_bias[None])
    rate = lanes3(-jnp.exp(a_log)[None])
    dsk = jnp.repeat(d_skip, HEAD)[None]
    gin = gain_in[None]
    gout = gain_out[None]
    if direct(size, rows):
        first, got, second, resid_in, cot_in, conv, bias, dtb, rate, dsk, gin, gout = (
            lax.optimization_barrier(
                (
                    first, gather_far(first), second, resid, cotangent, conv, bias, dtb, rate, dsk,
                    gin, gout,
                )
            )
        )
        wx, wx_at = gather_near(jnp.stack([first] + got))
        got = gather_far(second)
        resid_oth = swap(resid_in, 1, "tensor")
        cot_oth = swap(cot_in, 1, "tensor")
        second, resid_oth, cot_oth, wx, got = lax.optimization_barrier(
            (second, resid_oth, cot_oth, wx, got)
        )
        wz, wz_at = gather_near(jnp.stack([second] + got))
    else:
        resid_oth = swap(resid, 1, "tensor")
        cot_oth = swap(cotangent, 1, "tensor")
        wx, wx_at = whole_pieces(first, bits)
        wz, wz_at = whole_pieces(second, bits)

    info = jnp.stack([place, lax.axis_index("dp")]).astype(jnp.int32)
    anywhere = pl.BlockSpec(memory_space=pl.ANY)

    def copies(at):
        return pltpu.SemaphoreType.DMA((sum(len(masks) for _, masks in at),))

    def tok(width, dtype):
        return shape((tokens, width), dtype)

    own_spec = rows_spec(L, dim, lambda c, info: jnp.clip(c - half * info[0], 0, half - 1))
    oth_spec = rows_spec(L, dim, lambda c, info: jnp.clip(c - half * (1 - info[0]), 0, half - 1))
    wide = rows_spec(L, width)
    normed, xbc, act, dsilu, step_raw, within, mixed, sin = call(
        functools.partial(forward_kernel, wx_at),
        "mix_forward",
        chunks,
        [
            own_spec, oth_spec, full((1, dim)), full((4, cols)), full((1, cols)),
            full((1, LANES)), full((1, LANES)), full((1, width)),
        ]
        + [anywhere] * len(wx),
        [
            (rows_spec(L, dim), tok(dim, bf16)),
            (rows_spec(L, cols), tok(cols, bf16)),
            (rows_spec(L, cols), tok(cols, bf16)),
            (rows_spec(L, cols), tok(cols, bf16)),
            (rows_spec(L, LANES), tok(LANES, f32)),
            (rows_spec(L, LANES), tok(LANES, f32)),
            (wide, tok(width, f32)),
            (
                pl.BlockSpec((1, NS, width), lambda c, info: (c, 0, 0)),
                shape((chunks, NS, width), f32),
            ),
        ],
        [
            pltpu.VMEM((NS, width), f32), pltpu.VMEM((L + 8, cols), f32),
            pltpu.VMEM((dim, cols + LANES), bf16), copies(wx_at),
        ],
        info, resid, resid_oth, gin, conv, bias, dtb, rate, dsk, *wx,
    )

    sums_shape = shape((chunks * 16, L), f32)
    gate, gno, sums = call(
        functools.partial(gate_kernel, wz_at),
        "gate_forward",
        chunks,
        [own_spec, oth_spec, rows_spec(L, dim), wide, full((1, width))] + [anywhere] * len(wz),
        [(wide, tok(width, bf16)), (wide, tok(width, f32)), (rows_spec(16, L), sums_shape)],
        [pltpu.VMEM((dim, 2 * width), bf16), copies(wz_at)],
        info, cotangent, cot_oth, normed, mixed, gout, *wz,
    )
    sums_oth = swap(sums, 1, "tensor")

    def turned(c, info):
        return jnp.where(c < half, c + half * (1 - info[0]), c - half + half * info[0])

    gw_shapes, masks = scatter_shapes(size, rows, 2 * width)
    twide = rows_spec(L, width, turned)
    lead = rows_spec(L, dim, lambda c, info: jnp.minimum(c, half - 1))
    trail = rows_spec(L, dim, lambda c, info: jnp.maximum(c - half, 0))
    half_shape = shape((half_rows, dim), bf16)
    branch_sent, branch_own, ggate, gm, g_gout, *gw_zo = call(
        functools.partial(gate_back_kernel, wz_at, masks),
        "gate_backward",
        chunks,
        [
            trail, lead, rows_spec(L, dim, turned), twide, twide, twide,
            rows_spec(16, L, turned), rows_spec(16, L, turned), full((1, width)),
        ]
        + [anywhere] * len(wz),
        [
            (lead, half_shape), (trail, half_shape), (twide, tok(width, bf16)),
            (twide, tok(width, bf16)), (full((8, width)), shape((8, width), f32)),
        ]
        + [(full(item.shape), item) for item in gw_shapes],
        [
            pltpu.VMEM((dim, 2 * width), f32), pltpu.VMEM((8, width), f32),
            pltpu.VMEM((dim, width), bf16), copies(wz_at),
        ],
        info, cotangent, cot_oth, normed, mixed, gate, gno, sums, sums_oth, gout, *wz,
    )
    branch_oth = swap(branch_sent, 1, "tensor")
    sent_zo = scatter_near(gw_zo) if direct(size, rows) else gw_zo

    def back(c, info):
        return chunks - 1 - c

    rwide = rows_spec(L, width, back)
    rcols = rows_spec(L, cols, back)
    rlanes = rows_spec(L, LANES, back)
    gwx_shapes, masks = scatter_shapes(size, rows, cols + LANES)
    gx, g_conv, g_skip, g_head, *gw_x = call(
        functools.partial(scan_back_kernel, masks),
        "mix_backward",
        chunks,
        [
            rcols, rcols, rcols, rlanes, rlanes, rwide,
            pl.BlockSpec((1, NS, width), lambda c, info: (chunks - 1 - c, 0, 0)),
            rwide, rows_spec(L, dim, back), full((4, cols)), full((1, LANES)),
            full((1, LANES)), full((1, width)),
        ],
        [
            (rows_spec(L, cols + LANES, back), tok(cols + LANES, bf16)),
            (full((5, 8, cols)), shape((5, 8, cols), f32)),
            (full((8, width)), shape((8, width), f32)),
            (full((16, LANES)), shape((16, LANES), f32)),
        ]
        + [(full(item.shape), item) for item in gwx_shapes],
        [
            pltpu.VMEM((NS, width), f32), pltpu.VMEM((L + 8, cols), f32),
            pltpu.VMEM((dim, cols + LANES), f32), pltpu.VMEM((5, 8, cols), f32),
            pltpu.VMEM((8, width), f32), pltpu.VMEM((16, LANES), f32),
        ],
        info, xbc, act, dsilu, step_raw, within, mixed, sin, gm, normed, conv, dtb, rate, dsk,
    )

    sent_zo, branch_oth, gx, gw_x = lax.optimization_barrier((sent_zo, branch_oth, gx, gw_x))
    if direct(size, rows):
        far_zo = scatter_far(sum_pieces(sent_zo))
        sent_x = scatter_near(gw_x)

    dn_sent, dn_own, g_gin = call(
        functools.partial(input_back_kernel, wz_at, wx_at),
        "input_backward",
        chunks,
        [trail, lead, twide, rows_spec(L, cols + LANES, turned)]
        + [anywhere] * (len(wz) + len(wx)),
        [(lead, half_shape), (trail, half_shape), (full((8, dim)), shape((8, dim), f32))],
        [
            pltpu.VMEM((dim, width), bf16), pltpu.VMEM((dim, cols + LANES), bf16),
            copies(wz_at), copies(wx_at),
        ],
        info, resid, resid_oth, ggate, gx, *wz, *wx,
    )
    if direct(size, rows):
        far_zo, sent_x, dn_own, dn_sent, g_gin = lax.optimization_barrier(
            (far_zo, sent_x, dn_own, dn_sent, g_gin)
        )
        far_x = scatter_far(sum_pieces(sent_x))
    dn_oth = swap(dn_sent, 1, "tensor")

    conv_sum = jnp.sum(g_conv, axis=1)
    both = jnp.concatenate([conv_sum[:, width:].reshape(-1), jnp.sum(g_gin, axis=0)])
    both = both + swap(both, 1, "tensor")
    head_sum = jnp.sum(g_head.reshape(2, 8, LANES), axis=1)[:, :heads]
    skip_sum = jnp.sum(g_skip, axis=0).reshape(heads, HEAD).sum(axis=1)
    flat = [
        conv_sum[:, :width].reshape(-1), both, jnp.sum(g_gout, axis=0), head_sum.reshape(-1),
        skip_sum,
    ]
    sizes = [v.shape[0] for v in flat]
    vec = jnp.concatenate(flat)
    if direct(size, rows):
        near_vec = [vec] + [swap(vec, near, "dp") for near in NEAR[1:]]

    dspec = rows_spec(L, dim)
    block_out, grad_resid = call(
        lambda info, *refs: finish_kernel(*refs),
        "finish",
        half,
        [dspec, dspec, full((1, dim)), dspec, dspec, dspec, dspec],
        [(dspec, half_shape), (dspec, shape((half_rows, dim), f32))],
        [],
        info, resid, cotangent, gin, dn_own, dn_oth, branch_own, branch_oth,
    )

    if direct(size, rows):
        block_out, grad_resid, near_vec = lax.optimization_barrier(
            (block_out, grad_resid, near_vec)
        )
        vec = sum(near_vec)
        vec = vec + sum(swap(vec, far, "dp") for far in FAR[1:])
        sum_zo = sum_pieces(far_zo)
        sum_x = sum_pieces(far_x)
    else:
        sum_zo = scatter_whole(sent_zo[0][0], bits)
        sum_x = scatter_whole(gw_x[0][0], bits)
        for bit in bits:
            vec = vec + swap(vec, bit, "dp")
    grad_w_z = sum_zo[:, :width]
    grad_w_out = sum_zo[:, width:].T
    grad_w_x = sum_x[:, :width]
    grad_w_bc = sum_x[:, width:cols]
    grad_w_bc = grad_w_bc + swap(grad_w_bc, 1, "tensor")
    grad_w_dt = sum_x[:, cols : cols + heads]
    out = []
    start = 0
    for count in sizes:
        out.append(vec[start : start + count])
        start += count
    conv_g = out[0].reshape(5, width)
    bc_g = out[1][: 10 * NS].reshape(5, 2 * NS)
    grad_gain_in = out[1][10 * NS :]
    head_g = out[3].reshape(2, heads)
    return (
        block_out, grad_resid, grad_gain_in, grad_w_z, grad_w_x, grad_w_bc, grad_w_dt,
        conv_g[:4], conv_g[4], bc_g[:4], bc_g[4], head_g[0], head_g[1], out[4], out[2],
        grad_w_out,
    )


def solution(mesh):
    in_specs = (
        P(("dp", "tensor"), None),
        P(),
        P("dp", "tensor"),
        P("dp", "tensor"),
        P("dp", None),
        P("dp", "tensor"),
        P(None, "tensor"),
        P("tensor"),
        P(),
        P(),
        P("tensor"),
        P("tensor"),
        P("tensor"),
        P("tensor"),
        P("tensor", "dp"),
        P(("dp", "tensor"), None),
    )
    out_specs = (
        P(("dp", "tensor"), None),
        P(("dp", "tensor"), None),
        P(),
        P("dp", "tensor"),
        P("dp", "tensor"),
        P("dp", None),
        P("dp", "tensor"),
        P(None, "tensor"),
        P("tensor"),
        P(),
        P(),
        P("tensor"),
        P("tensor"),
        P("tensor"),
        P("tensor"),
        P("tensor", "dp"),
    )
    return jax.shard_map(local, mesh=mesh, in_specs=in_specs, out_specs=out_specs, check_vma=False)
```

time: 551 us -> 252 us (0.46)
  waiting for transfers between devices: 228 us -> 31.1 us
  starting transfers between devices: 115 us -> 46.4 us
  local copies, waits for them, and re-layouts: 53.5 us -> 20.3 us
  Pallas kernels: 130 us -> 141 us
  other arithmetic: 21.3 us -> 10.6 us
    ppermute x117 -> x37, waiting for transfers between devices: 228 us -> 31.1 us  [swap(): return lax.ppermute(v, axis, [(i, i ^ bit) for i in range(size)])]
    ppermute x117 -> x37, starting transfers between devices: 115 us -> 46.4 us  [swap(): return lax.ppermute(v, axis, [(i, i ^ bit) for i in range(size)])]
    unnamed x127 -> x68, local copies, waits for them, and re-layouts: 26.2 us -> 8.17 us
    pallas_call x6, Pallas kernels: 130 us -> 141 us  [call(): pl.pallas_call(kernel, grid_spec=pltpu.PrefetchScalarGridSpec(num_scalar_...]
    dynamic_slice x8 -> x0, local copies, waits for them, and re-layouts: 8.28 us -> none  [the longest x2 3.8 us: local(): lax.dynamic_slice_in_dim(v, which * half_rows, half_rows, 0)]
    add x19 -> x4, other arithmetic: 7.78 us -> 0.14 us  [the longest x2 0.12 us: sum_pieces(): return sum((p.astype(f32) for p in pieces))]
    slice x8 -> x3, local copies, waits for them, and re-layouts: 7.64 us -> 0.68 us  [the longest x1 0.67 us: local(): grad_w_x = sum_x[:, :width]]
    select_n x8 -> x0, other arithmetic: 6.03 us -> none  [in_order(): stacked = jnp.where(me & bit != 0, v[:, ::-1], v).reshape(size, rows, cols)]
  transfers between devices with their start and end apart: 117 -> 37, of which waited for: 87 -> 10; matrix products, arithmetic and copies ran while one was open for 12% -> 7% of each run, Pallas kernels for 7% -> 40%
where the time goes in v2:
time: 252 us; the launch traced here: 250 us
  Pallas kernels  141 us (56%)
  starting transfers between devices  46.4 us (18%)
  waiting for transfers between devices  31.1 us (12%)
  local copies, waits for them, and re-layouts  20.3 us (8%)
  other arithmetic  10.6 us (4%)
    pallas_call x6, Pallas kernels, call(): pl.pallas_call(kernel, grid_spec=pltpu.PrefetchScalarGridSpec(num_scalar_...  141 us
    ppermute x37, starting transfers between devices, swap(): return lax.ppermute(v, axis, [(i, i ^ bit) for i in range(size)])  46.4 us
    ppermute x37, waiting for transfers between devices, swap(): return lax.ppermute(v, axis, [(i, i ^ bit) for i in range(size)])  31.1 us
    unnamed x68, local copies, waits for them, and re-layouts  8.17 us
  transfers between devices with their start and end apart: 37, of which 10 were waited for; matrix products, arithmetic and copies ran while one was open for 7% of the time, Pallas kernels for 40%

profile of v2, /device:TPU:0, one launch (start us, length us, event | category | flops | bytes accessed | tf_op | source)
XLA Modules:
  0.0 250.5 jit_solution(2841446246725641371)
XLA Ops:
  2.4 5.1 %collective-permute-start.2 = (bf16[48,1152]{1,0:T(8,128)(2,1)S(1)}, bf16[48,1152]{1,0:T(8,128)(2,1)S(1)}, u32[]{:S(2)}, u32[]{:S(2)}) collective-permute-start(bf16[48,1152]{1,0:T(8,128)(2,1)S(1)} %pad_maximum_fusion.3), channel_id=1, source_target_pairs={{0,24},{2,26},{4,28},{6,30},{8,16},{10,18},{12,20},{14,22},{16,8},... | collective-permute-start | bytes 331784 | tf_op jit(solution)/shard_map/ppermute | solution.py:469
  13.4 1.3 pad_maximum_fusion.6
  17.6 3.7 %collective-permute-start.10 = (bf16[48,1536]{1,0:T(8,128)(2,1)S(1)}, bf16[48,1536]{1,0:T(8,128)(2,1)S(1)}, u32[]{:S(2)}, u32[]{:S(2)}) collective-permute-start(bf16[48,1536]{1,0:T(8,128)(2,1)S(1)} %pad_maximum_fusion.2), channel_id=1, source_target_pairs={{0,24},{2,26},{4,28},{6,30},{8,16},{10,18},{12,20},{14,22},{16,8},... | collective-permute-start | bytes 442376 | tf_op jit(solution)/shard_map/ppermute | solution.py:469
  22.1 4.1 %collective-permute-done.10 = bf16[48,1536]{1,0:T(8,128)(2,1)S(1)} collective-permute-done((bf16[48,1536]{1,0:T(8,128)(2,1)S(1)}, bf16[48,1536]{1,0:T(8,128)(2,1)S(1)}, u32[]{:S(2)}, u32[]{:S(2)}) %collective-permute-start.10) | collective-permute-done | bytes 147488 | tf_op jit(solution)/shard_map/ppermute | solution.py:469
  26.2 2.6 %collective-permute-start.7 = (bf16[4,48,1152]{2,1,0:T(8,128)(2,1)S(1)}, bf16[4,48,1152]{2,1,0:T(8,128)(2,1)S(1)}, u32[]{:S(2)}, u32[]{:S(2)}) collective-permute-start(bf16[4,48,1152]{2,1,0:T(8,128)(2,1)S(1)} %pad_maximum_fusion.1.rest_0_.rest_4_), channel_id=1, source_target_pairs={{0,6},{2,4},{4,2},{6,0},{8,14},{10,12},{12,10},{14,8},{16,22},{18,... | collective-permute-start | bytes 1327112 | tf_op jit(solution)/shard_map/ppermute | solution.py:469
  28.8 5.0 %collective-permute-done.9 = bf16[48,1536]{1,0:T(8,128)(2,1)S(1)} collective-permute-done((bf16[48,1536]{1,0:T(8,128)(2,1)S(1)}, bf16[48,1536]{1,0:T(8,128)(2,1)S(1)}, u32[]{:S(2)}, u32[]{:S(2)}) %collective-permute-start.9) | collective-permute-done | bytes 147488 | tf_op jit(solution)/shard_map/ppermute | solution.py:469
  33.7 1.5 collective-permute-start.6
  35.3 1.5 collective-permute-start.5
  36.7 2.3 collective-permute-done.7.rest_3_.rest_7_
  39.0 8.4 %collective-permute-done.6.rest_2_.rest_6_ = bf16[4,48,1152]{2,1,0:T(8,128)(2,1)S(1)} collective-permute-done((bf16[4,48,1152]{2,1,0:T(8,128)(2,1)S(1)}, bf16[4,48,1152]{2,1,0:T(8,128)(2,1)S(1)}, u32[]{:S(2)}, u32[]{:S(2)}) %collective-permute-start.6) | collective-permute-done | bytes 442400 | tf_op jit(solution)/shard_map/ppermute | solution.py:469
  49.2 2.4 collective-permute-start.13
  56.2 30.5 %mix_forward.1 = (bf16[2048,768]{1,0:T(8,128)(2,1)}, bf16[2048,1024]{1,0:T(8,128)(2,1)}, bf16[2048,1024]{1,0:T(8,128)(2,1)}, bf16[2048,1024]{1,0:T(8,128)(2,1)},...) custom-call(s32[2]{0:T(128)S(1)} %pad_add_fusion.info, ...), custom_call_target="tpu_custom_call" | custom-call | tf_op jit(solution)/shard_map/mix_forward/pallas_call | solution.py:554
  86.7 16.6 %gate_forward.1 = (bf16[2048,768]{1,0:T(8,128)(2,1)}, f32[2048,768]{1,0:T(8,128)}, f32[128,256]{1,0:T(8,128)S(1)}) custom-call(s32[2]{0:T(128)S(1)} %pad_add_fusion.info, bf16[1024,768]{1,0:T(8,128)(2,1)} %refs_1_.1, bf16[1024,768]{1,0:T(8,128)(2,1)} %copy-done.19, bf16[2048,768]{1,0:T(8,128)(2,1)} %get-tuple-element.119.normed, ...), custom_call_target="tpu_custom_call" | custom-call | tf_op jit(solution)/shard_map/gate_forward/pallas_call | solution.py:554
  103.5 1.3 collective-permute-done.14.soth
  104.8 25.4 %gate_backward.1 = (bf16[1024,768]{1,0:T(8,128)(2,1)}, bf16[1024,768]{1,0:T(8,128)(2,1)}, bf16[2048,768]{1,0:T(8,128)(2,1)}, bf16[2048,768]{1,0:T(8,128)(2,1)}, ...) custom-call(s32[2]{0:T(128)S(1)} %pad_add_fusion.info, ...), custom_call_target="tpu_custom_call" | custom-call | tf_op jit(solution)/shard_map/gate_backward/pallas_call | solution.py:554
  130.4 1.4 collective-permute-start.15
  131.8 1.5 collective-permute-start.16
  133.9 44.7 %mix_backward.1 = (bf16[2048,1152]{1,0:T(8,128)(2,1)}, f32[5,8,1024]{2,1,0:T(8,128)S(1)}, f32[8,768]{1,0:T(8,128)S(1)}, f32[16,128]{1,0:T(8,128)S(1)}, bf16[4,48...) custom-call(s32[2]{0:T(128)S(1)} %pad_add_fusion.info, ...), custom_call_target="tpu_custom_call" | custom-call | tf_op jit(solution)/shard_map/mix_backward/pallas_call | solution.py:554
  178.7 1.5 fusion.9
  180.6 3.4 %collective-permute-start.21 = (bf16[48,1536]{1,0:T(8,128)(2,1)S(1)}, bf16[48,1536]{1,0:T(8,128)(2,1)S(1)}, u32[]{:S(2)}, u32[]{:S(2)}) collective-permute-start(bf16[48,1536]{1,0:T(8,128)(2,1)S(1)} %get-tuple-element.220), channel_id=1, source_target_pairs={{0,24},{2,26},{4,28},{6,30},{8,16},{10,18},{12,20},{14,22},{16,8},... | collective-permute-start | bytes 442376 | tf_op jit(solution)/shard_map/ppermute | solution.py:469
  186.7 3.6 %collective-permute-start.20 = (bf16[48,1536]{1,0:T(8,128)(2,1)S(1)}, bf16[48,1536]{1,0:T(8,128)(2,1)S(1)}, u32[]{:S(2)}, u32[]{:S(2)}) collective-permute-start(bf16[48,1536]{1,0:T(8,128)(2,1)S(1)} %get-tuple-element.221), channel_id=1, source_target_pairs={{0,16},{2,18},{4,20},{6,22},{8,24},{10,26},{12,28},{14,30},{16,0},... | collective-permute-start | bytes 442376 | tf_op jit(solution)/shard_map/ppermute | solution.py:469
  190.3 1.5 collective-permute-start.22
  191.8 1.4 collective-permute-start.23
  194.8 17.1 %input_backward.1 = (bf16[1024,768]{1,0:T(8,128)(2,1)}, bf16[1024,768]{1,0:T(8,128)(2,1)}, f32[8,768]{1,0:T(8,128)S(1)}) custom-call(s32[2]{0:T(128)S(1)} %copy-done.10, bf16[1024,768]{1,0:T(8,128)(2,1)} %refs_0_.1, bf16[1024,768]{1,0:T(8,128)(2,1)} %copy-done.20, bf16[2048,768]{1,0:T(8,128)(2,1)} %get-tuple-element.154.ggate, ...), custom_call_target="tpu_custom_call" | custom-call | tf_op jit(solution)/shard_map/input_backward/pallas_call | solution.py:554
  213.3 1.5 fusion.8
  216.4 2.3 collective-permute-start.33
  218.8 3.0 %collective-permute-start.35 = (bf16[48,1152]{1,0:T(8,128)(2,1)}, bf16[48,1152]{1,0:T(8,128)(2,1)S(1)}, u32[]{:S(2)}, u32[]{:S(2)}) collective-permute-start(bf16[48,1152]{1,0:T(8,128)(2,1)} %get-tuple-element.224), channel_id=1, source_target_pairs={{0,24},{2,26},{4,28},{6,30},{8,16},{10,18},{12,20},{14,22},{16,8},... | collective-permute-start | bytes 331784 | tf_op jit(solution)/shard_map/ppermute | solution.py:469
  223.9 4.4 %collective-permute-done.35 = bf16[48,1152]{1,0:T(8,128)(2,1)S(1)} collective-permute-done((bf16[48,1152]{1,0:T(8,128)(2,1)}, bf16[48,1152]{1,0:T(8,128)(2,1)S(1)}, u32[]{:S(2)}, u32[]{:S(2)}) %collective-permute-start.35) | collective-permute-done | bytes 110624 | tf_op jit(solution)/shard_map/ppermute | solution.py:469
  228.8 3.5 %collective-permute-done.34 = bf16[48,1152]{1,0:T(8,128)(2,1)S(1)} collective-permute-done((bf16[48,1152]{1,0:T(8,128)(2,1)}, bf16[48,1152]{1,0:T(8,128)(2,1)S(1)}, u32[]{:S(2)}, u32[]{:S(2)}) %collective-permute-start.34) | collective-permute-done | bytes 110624 | tf_op jit(solution)/shard_map/ppermute | solution.py:469
  233.8 6.7 %finish.1 = (bf16[1024,768]{1,0:T(8,128)(2,1)}, f32[1024,768]{1,0:T(8,128)}) custom-call(s32[2]{0:T(128)S(1)} %copy-done.10, bf16[1024,768]{1,0:T(8,128)(2,1)S(1)} %copy-done, bf16[1024,768]{1,0:T(8,128)(2,1)} %refs_1_.1, f32[1,768]{1,0:T(1,128)S(1)} %copy-done.6, bf16[1024,768]{1,0:T(8,128)(2,1)} %get-tuple-element.159.refs_3_, ...), custom_call_target="tpu_custom_call" | custom-call | tf_op jit(solution)/shard_map/finish/pallas_call | solution.py:554
  240.6 1.7 collective-permute-start.32
  242.3 2.7 %collective-permute-start.30 = (f32[6692]{0:T(1024)S(1)}, f32[6692]{0:T(1024)S(1)}, u32[]{:S(2)}, u32[]{:S(2)}) collective-permute-start(f32[6692]{0:T(1024)S(1)} %add_add_fusion.1), channel_id=1, source_target_pairs={{0,8},{2,10},{4,12},{6,14},{8,0},{10,2},{12,4},{14,6},{16,24},{18,... | collective-permute-start | bytes 80312 | tf_op jit(solution)/shard_map/ppermute | solution.py:469
  (169 shorter events, 35.5 us)
Async XLA Ops:
  2.4 14.6 %collective-permute-start.2 = (bf16[48,1152]{1,0:T(8,128)(2,1)S(1)}, bf16[48,1152]{1,0:T(8,128)(2,1)S(1)}, u32[]{:S(2)}, u32[]{:S(2)}) collective-permute-start(bf16[48,1152]{1,0:T(8,128)(2,1)S(1)} %pad_maximum_fusion.3), channel_id=1, source_target_pairs={{0,24},{2,26},{4,28},{6,30},{8,16},{10,18},{12,20},{14,22},{16,8},... | collective-permute-start | bytes 331784 | tf_op jit(solution)/shard_map/ppermute | solution.py:469
  7.6 9.5 %collective-permute-start.1 = (bf16[48,1152]{1,0:T(8,128)(2,1)S(1)}, bf16[48,1152]{1,0:T(8,128)(2,1)S(1)}, u32[]{:S(2)}, u32[]{:S(2)}) collective-permute-start(bf16[48,1152]{1,0:T(8,128)(2,1)S(1)} %pad_maximum_fusion.3), channel_id=1, source_target_pairs={{0,16},{2,18},{4,20},{6,22},{8,24},{10,26},{12,28},{14,30},{16,0},... | collective-permute-start | bytes 331784 | tf_op jit(solution)/shard_map/ppermute | solution.py:469
  7.6 9.5 %collective-permute-start = (bf16[48,1152]{1,0:T(8,128)(2,1)S(1)}, bf16[48,1152]{1,0:T(8,128)(2,1)S(1)}, u32[]{:S(2)}, u32[]{:S(2)}) collective-permute-start(bf16[48,1152]{1,0:T(8,128)(2,1)S(1)} %pad_maximum_fusion.3), channel_id=1, source_target_pairs={{0,8},{2,10},{4,12},{6,14},{8,0},{10,2},{12,4},{14,6},{16,24},{18,... | collective-permute-start | bytes 331784 | tf_op jit(solution)/shard_map/ppermute | solution.py:469
  17.0 30.4 %collective-permute-start.3 = (bf16[1024,768]{1,0:T(8,128)(2,1)}, bf16[1024,768]{1,0:T(8,128)(2,1)S(1)}, u32[]{:S(2)}, u32[]{:S(2)}) collective-permute-start(bf16[1024,768]{1,0:T(8,128)(2,1)} %refs_0_.1), channel_id=1, source_target_pairs={{0,1},{1,0},{2,3},{3,2},{4,5},{5,4},{6,7},{7,6},{8,9},{9,8},{10,11... | collective-permute-start | bytes 4718600 | tf_op jit(solution)/shard_map/ppermute | solution.py:469
  17.1 30.3 %collective-permute-start.4 = (bf16[1024,768]{1,0:T(8,128)(2,1)}, bf16[1024,768]{1,0:T(8,128)(2,1)S(1)}, u32[]{:S(2)}, u32[]{:S(2)}) collective-permute-start(bf16[1024,768]{1,0:T(8,128)(2,1)} %refs_1_.1), channel_id=1, source_target_pairs={{0,1},{1,0},{2,3},{3,2},{4,5},{5,4},{6,7},{7,6},{8,9},{9,8},{10,11... | collective-permute-start | bytes 4718600 | tf_op jit(solution)/shard_map/ppermute | solution.py:469
  17.6 8.6 %collective-permute-start.10 = (bf16[48,1536]{1,0:T(8,128)(2,1)S(1)}, bf16[48,1536]{1,0:T(8,128)(2,1)S(1)}, u32[]{:S(2)}, u32[]{:S(2)}) collective-permute-start(bf16[48,1536]{1,0:T(8,128)(2,1)S(1)} %pad_maximum_fusion.2), channel_id=1, source_target_pairs={{0,24},{2,26},{4,28},{6,30},{8,16},{10,18},{12,20},{14,22},{16,8},... | collective-permute-start | bytes 442376 | tf_op jit(solution)/shard_map/ppermute | solution.py:469
  21.3 12.4 %collective-permute-start.9 = (bf16[48,1536]{1,0:T(8,128)(2,1)S(1)}, bf16[48,1536]{1,0:T(8,128)(2,1)S(1)}, u32[]{:S(2)}, u32[]{:S(2)}) collective-permute-start(bf16[48,1536]{1,0:T(8,128)(2,1)S(1)} %pad_maximum_fusion.2), channel_id=1, source_target_pairs={{0,16},{2,18},{4,20},{6,22},{8,24},{10,26},{12,28},{14,30},{16,0},... | collective-permute-start | bytes 442376 | tf_op jit(solution)/shard_map/ppermute | solution.py:469
  21.3 13.9 %collective-permute-start.8 = (bf16[48,1536]{1,0:T(8,128)(2,1)S(1)}, bf16[48,1536]{1,0:T(8,128)(2,1)S(1)}, u32[]{:S(2)}, u32[]{:S(2)}) collective-permute-start(bf16[48,1536]{1,0:T(8,128)(2,1)S(1)} %pad_maximum_fusion.2), channel_id=1, source_target_pairs={{0,8},{2,10},{4,12},{6,14},{8,0},{10,2},{12,4},{14,6},{16,24},{18,... | collective-permute-start | bytes 442376 | tf_op jit(solution)/shard_map/ppermute | solution.py:469
  26.2 12.8 %collective-permute-start.7 = (bf16[4,48,1152]{2,1,0:T(8,128)(2,1)S(1)}, bf16[4,48,1152]{2,1,0:T(8,128)(2,1)S(1)}, u32[]{:S(2)}, u32[]{:S(2)}) collective-permute-start(bf16[4,48,1152]{2,1,0:T(8,128)(2,1)S(1)} %pad_maximum_fusion.1.rest_0_.rest_4_), channel_id=1, source_target_pairs={{0,6},{2,4},{4,2},{6,0},{8,14},{10,12},{12,10},{14,8},{16,22},{18,... | collective-permute-start | bytes 1327112 | tf_op jit(solution)/shard_map/ppermute | solution.py:469
  33.7 13.7 %collective-permute-start.6 = (bf16[4,48,1152]{2,1,0:T(8,128)(2,1)S(1)}, bf16[4,48,1152]{2,1,0:T(8,128)(2,1)S(1)}, u32[]{:S(2)}, u32[]{:S(2)}) collective-permute-start(bf16[4,48,1152]{2,1,0:T(8,128)(2,1)S(1)} %pad_maximum_fusion.1.rest_0_.rest_4_), channel_id=1, source_target_pairs={{0,4},{2,6},{4,0},{6,2},{8,12},{10,14},{12,8},{14,10},{16,20},{18,... | collective-permute-start | bytes 1327112 | tf_op jit(solution)/shard_map/ppermute | solution.py:469
  35.3 12.1 %collective-permute-start.5 = (bf16[4,48,1152]{2,1,0:T(8,128)(2,1)S(1)}, bf16[4,48,1152]{2,1,0:T(8,128)(2,1)S(1)}, u32[]{:S(2)}, u32[]{:S(2)}) collective-permute-start(bf16[4,48,1152]{2,1,0:T(8,128)(2,1)S(1)} %pad_maximum_fusion.1.rest_0_.rest_4_), channel_id=1, source_target_pairs={{0,2},{2,0},{4,6},{6,4},{8,10},{10,8},{12,14},{14,12},{16,18},{18,... | collective-permute-start | bytes 1327112 | tf_op jit(solution)/shard_map/ppermute | solution.py:469
  49.2 37.5 %collective-permute-start.13 = (bf16[4,48,1536]{2,1,0:T(8,128)(2,1)S(1)}, bf16[4,48,1536]{2,1,0:T(8,128)(2,1)}, u32[]{:S(2)}, u32[]{:S(2)}) collective-permute-start(bf16[4,48,1536]{2,1,0:T(8,128)(2,1)S(1)} %pad_maximum_fusion.rest_0_), channel_id=1, source_target_pairs={{0,6},{2,4},{4,2},{6,0},{8,14},{10,12},{12,10},{14,8},{16,22},{18,... | collective-permute-start | bytes 1769480 | tf_op jit(solution)/shard_map/ppermute | solution.py:469
  51.5 35.1 %collective-permute-start.12 = (bf16[4,48,1536]{2,1,0:T(8,128)(2,1)S(1)}, bf16[4,48,1536]{2,1,0:T(8,128)(2,1)S(1)}, u32[]{:S(2)}, u32[]{:S(2)}) collective-permute-start(bf16[4,48,1536]{2,1,0:T(8,128)(2,1)S(1)} %pad_maximum_fusion.rest_0_), channel_id=1, source_target_pairs={{0,4},{2,6},{4,0},{6,2},{8,12},{10,14},{12,8},{14,10},{16,20},{18,... | collective-permute-start | bytes 1769480 | tf_op jit(solution)/shard_map/ppermute | solution.py:469
  52.1 34.6 %collective-permute-start.11 = (bf16[4,48,1536]{2,1,0:T(8,128)(2,1)S(1)}, bf16[4,48,1536]{2,1,0:T(8,128)(2,1)S(1)}, u32[]{:S(2)}, u32[]{:S(2)}) collective-permute-start(bf16[4,48,1536]{2,1,0:T(8,128)(2,1)S(1)} %pad_maximum_fusion.rest_0_), channel_id=1, source_target_pairs={{0,2},{2,0},{4,6},{6,4},{8,10},{10,8},{12,14},{14,12},{16,18},{18,... | collective-permute-start | bytes 1769480 | tf_op jit(solution)/shard_map/ppermute | solution.py:469
  130.2 48.5 %collective-permute-start.18 = (bf16[1024,768]{1,0:T(8,128)(2,1)}, bf16[1024,768]{1,0:T(8,128)(2,1)S(1)}, u32[]{:S(2)}, u32[]{:S(2)}) collective-permute-start(bf16[1024,768]{1,0:T(8,128)(2,1)} %get-tuple-element.133), channel_id=1, source_target_pairs={{0,1},{1,0},{2,3},{3,2},{4,5},{5,4},{6,7},{7,6},{8,9},{9,8},{10,11... | collective-permute-start | bytes 4718600 | tf_op jit(solution)/shard_map/ppermute | solution.py:469
  130.4 48.2 %collective-permute-start.15 = (bf16[4,48,1536]{2,1,0:T(8,128)(2,1)S(1)}, bf16[4,48,1536]{2,1,0:T(8,128)(2,1)S(1)}, u32[]{:S(2)}, u32[]{:S(2)}) collective-permute-start(bf16[4,48,1536]{2,1,0:T(8,128)(2,1)S(1)} %get-tuple-element.130), channel_id=1, source_target_pairs={{0,2},{2,0},{4,6},{6,4},{8,10},{10,8},{12,14},{14,12},{16,18},{18,... | collective-permute-start | bytes 1769480 | tf_op jit(solution)/shard_map/ppermute | solution.py:469
  131.8 46.8 %collective-permute-start.16 = (bf16[4,48,1536]{2,1,0:T(8,128)(2,1)}, bf16[4,48,1536]{2,1,0:T(8,128)(2,1)S(1)}, u32[]{:S(2)}, u32[]{:S(2)}) collective-permute-start(bf16[4,48,1536]{2,1,0:T(8,128)(2,1)} %get-tuple-element.131), channel_id=1, source_target_pairs={{0,4},{2,6},{4,0},{6,2},{8,12},{10,14},{12,8},{14,10},{16,20},{18,... | collective-permute-start | bytes 1769480 | tf_op jit(solution)/shard_map/ppermute | solution.py:469
  133.3 45.4 %collective-permute-start.17 = (bf16[4,48,1536]{2,1,0:T(8,128)(2,1)}, bf16[4,48,1536]{2,1,0:T(8,128)(2,1)S(1)}, u32[]{:S(2)}, u32[]{:S(2)}) collective-permute-start(bf16[4,48,1536]{2,1,0:T(8,128)(2,1)} %get-tuple-element.132), channel_id=1, source_target_pairs={{0,6},{2,4},{4,2},{6,0},{8,14},{10,12},{12,10},{14,8},{16,22},{18,... | collective-permute-start | bytes 1769480 | tf_op jit(solution)/shard_map/ppermute | solution.py:469
  180.6 12.6 %collective-permute-start.21 = (bf16[48,1536]{1,0:T(8,128)(2,1)S(1)}, bf16[48,1536]{1,0:T(8,128)(2,1)S(1)}, u32[]{:S(2)}, u32[]{:S(2)}) collective-permute-start(bf16[48,1536]{1,0:T(8,128)(2,1)S(1)} %get-tuple-element.220), channel_id=1, source_target_pairs={{0,24},{2,26},{4,28},{6,30},{8,16},{10,18},{12,20},{14,22},{16,8},... | collective-permute-start | bytes 442376 | tf_op jit(solution)/shard_map/ppermute | solution.py:469
  186.7 25.2 %collective-permute-start.20 = (bf16[48,1536]{1,0:T(8,128)(2,1)S(1)}, bf16[48,1536]{1,0:T(8,128)(2,1)S(1)}, u32[]{:S(2)}, u32[]{:S(2)}) collective-permute-start(bf16[48,1536]{1,0:T(8,128)(2,1)S(1)} %get-tuple-element.221), channel_id=1, source_target_pairs={{0,16},{2,18},{4,20},{6,22},{8,24},{10,26},{12,28},{14,30},{16,0},... | collective-permute-start | bytes 442376 | tf_op jit(solution)/shard_map/ppermute | solution.py:469
  190.3 21.6 %collective-permute-start.19 = (bf16[48,1536]{1,0:T(8,128)(2,1)S(1)}, bf16[48,1536]{1,0:T(8,128)(2,1)S(1)}, u32[]{:S(2)}, u32[]{:S(2)}) collective-permute-start(bf16[48,1536]{1,0:T(8,128)(2,1)S(1)} %get-tuple-element.222), channel_id=1, source_target_pairs={{0,8},{2,10},{4,12},{6,14},{8,0},{10,2},{12,4},{14,6},{16,24},{18,... | collective-permute-start | bytes 442376 | tf_op jit(solution)/shard_map/ppermute | solution.py:469
  190.3 21.6 %collective-permute-start.22 = (bf16[4,48,1152]{2,1,0:T(8,128)(2,1)}, bf16[4,48,1152]{2,1,0:T(8,128)(2,1)S(1)}, u32[]{:S(2)}, u32[]{:S(2)}) collective-permute-start(bf16[4,48,1152]{2,1,0:T(8,128)(2,1)} %copy-done.18), channel_id=1, source_target_pairs={{0,2},{2,0},{4,6},{6,4},{8,10},{10,8},{12,14},{14,12},{16,18},{18,... | collective-permute-start | bytes 1327112 | tf_op jit(solution)/shard_map/ppermute | solution.py:469
  191.8 20.8 %collective-permute-start.23 = (bf16[4,48,1152]{2,1,0:T(8,128)(2,1)}, bf16[4,48,1152]{2,1,0:T(8,128)(2,1)}, u32[]{:S(2)}, u32[]{:S(2)}) collective-permute-start(bf16[4,48,1152]{2,1,0:T(8,128)(2,1)} %copy-done.17), channel_id=1, source_target_pairs={{0,4},{2,6},{4,0},{6,2},{8,12},{10,14},{12,8},{14,10},{16,20},{18,... | collective-permute-start | bytes 1327112 | tf_op jit(solution)/shard_map/ppermute | solution.py:469
  193.2 19.4 %collective-permute-start.24 = (bf16[4,48,1152]{2,1,0:T(8,128)(2,1)}, bf16[4,48,1152]{2,1,0:T(8,128)(2,1)}, u32[]{:S(2)}, u32[]{:S(2)}) collective-permute-start(bf16[4,48,1152]{2,1,0:T(8,128)(2,1)} %copy-done.16), channel_id=1, source_target_pairs={{0,6},{2,4},{4,2},{6,0},{8,14},{10,12},{12,10},{14,8},{16,22},{18,... | collective-permute-start | bytes 1327112 | tf_op jit(solution)/shard_map/ppermute | solution.py:469
  212.7 9.1 %collective-permute-start.26 = (f32[2048]{0:T(1024)S(1)}, f32[2048]{0:T(1024)S(1)}, u32[]{:S(2)}, u32[]{:S(2)}) collective-permute-start(f32[2048]{0:T(1024)S(1)} %pad_maximum_fusion.5), channel_id=1, source_target_pairs={{0,1},{1,0},{2,3},{3,2},{4,5},{5,4},{6,7},{7,6},{8,9},{9,8},{10,11... | collective-permute-start | bytes 24584 | tf_op jit(solution)/shard_map/ppermute | solution.py:469
  213.3 20.5 %collective-permute-start.25 = (bf16[1024,768]{1,0:T(8,128)(2,1)}, bf16[1024,768]{1,0:T(8,128)(2,1)}, u32[]{:S(2)}, u32[]{:S(2)}) collective-permute-start(bf16[1024,768]{1,0:T(8,128)(2,1)} %get-tuple-element.160), channel_id=1, source_target_pairs={{0,1},{1,0},{2,3},{3,2},{4,5},{5,4},{6,7},{7,6},{8,9},{9,8},{10,11... | collective-permute-start | bytes 4718600 | tf_op jit(solution)/shard_map/ppermute | solution.py:469
  218.8 9.5 %collective-permute-start.35 = (bf16[48,1152]{1,0:T(8,128)(2,1)}, bf16[48,1152]{1,0:T(8,128)(2,1)S(1)}, u32[]{:S(2)}, u32[]{:S(2)}) collective-permute-start(bf16[48,1152]{1,0:T(8,128)(2,1)} %get-tuple-element.224), channel_id=1, source_target_pairs={{0,24},{2,26},{4,28},{6,30},{8,16},{10,18},{12,20},{14,22},{16,8},... | collective-permute-start | bytes 331784 | tf_op jit(solution)/shard_map/ppermute | solution.py:469
  221.8 10.6 %collective-permute-start.34 = (bf16[48,1152]{1,0:T(8,128)(2,1)}, bf16[48,1152]{1,0:T(8,128)(2,1)S(1)}, u32[]{:S(2)}, u32[]{:S(2)}) collective-permute-start(bf16[48,1152]{1,0:T(8,128)(2,1)} %get-tuple-element.225), channel_id=1, source_target_pairs={{0,16},{2,18},{4,20},{6,22},{8,24},{10,26},{12,28},{14,30},{16,0},... | collective-permute-start | bytes 331784 | tf_op jit(solution)/shard_map/ppermute | solution.py:469
  221.9 18.6 %collective-permute-start.29 = (f32[6692]{0:T(1024)S(1)}, f32[6692]{0:T(1024)S(1)}, u32[]{:S(2)}, u32[]{:S(2)}) collective-permute-start(f32[6692]{0:T(1024)S(1)} %concatenate.35), channel_id=1, source_target_pairs={{0,6},{2,4},{4,2},{6,0},{8,14},{10,12},{12,10},{14,8},{16,22},{18,... | collective-permute-start | bytes 80312 | tf_op jit(solution)/shard_map/ppermute | solution.py:469
  222.7 17.9 %collective-permute-start.28 = (f32[6692]{0:T(1024)S(1)}, f32[6692]{0:T(1024)S(1)}, u32[]{:S(2)}, u32[]{:S(2)}) collective-permute-start(f32[6692]{0:T(1024)S(1)} %concatenate.35), channel_id=1, source_target_pairs={{0,4},{2,6},{4,0},{6,2},{8,12},{10,14},{12,8},{14,10},{16,20},{18,... | collective-permute-start | bytes 80312 | tf_op jit(solution)/shard_map/ppermute | solution.py:469
  228.3 12.3 %collective-permute-start.27 = (f32[6692]{0:T(1024)S(1)}, f32[6692]{0:T(1024)S(1)}, u32[]{:S(2)}, u32[]{:S(2)}) collective-permute-start(f32[6692]{0:T(1024)S(1)} %concatenate.35), channel_id=1, source_target_pairs={{0,2},{2,0},{4,6},{6,4},{8,10},{10,8},{12,14},{14,12},{16,18},{18,... | collective-permute-start | bytes 80312 | tf_op jit(solution)/shard_map/ppermute | solution.py:469
  233.8 11.3 %collective-permute-start.36 = (f32[48,256]{1,0:T(8,128)S(1)}, f32[48,256]{1,0:T(8,128)S(1)}, u32[]{:S(2)}, u32[]{:S(2)}) collective-permute-start(f32[48,256]{1,0:T(8,128)S(1)} %slice.141), channel_id=1, source_target_pairs={{0,1},{1,0},{2,3},{3,2},{4,5},{5,4},{6,7},{7,6},{8,9},{9,8},{10,11... | collective-permute-start | bytes 147464 | tf_op jit(solution)/shard_map/ppermute | solution.py:469
  (38 other events, 422.9 us)

commit v3 on v2

v3 whole, which is shorter than its diff:
```python
import functools

import jax
import jax.numpy as jnp
from jax import lax
from jax.experimental import pallas as pl
from jax.experimental.pallas import tpu as pltpu
from jax.sharding import PartitionSpec as P

NS = 128
L = 256
R = 512
SEQ_LEN = 2048
HEAD = 64
LANES = 128
MIB = 1024 * 1024

f32 = jnp.float32
bf16 = jnp.bfloat16
highest = lax.Precision.HIGHEST
eps = 1e-05

NN = (((1,), (0,)), ((), ()))
NT = (((1,), (1,)), ((), ()))
TN = (((0,), (0,)), ((), ()))


def mm(a, b, dims=NN, precision=None):
    return lax.dot_general(a, b, dims, precision=precision, preferred_element_type=f32)


def iota(shape, dim):
    return lax.broadcasted_iota(jnp.int32, shape, dim)


def lower_tri():
    return (iota((L, L), 0) >= iota((L, L), 1)).astype(bf16)


def upper_tri():
    return (iota((L, L), 0) <= iota((L, L), 1)).astype(bf16)


def expander(heads):
    rows = iota((LANES, heads * HEAD), 0)
    cols = iota((LANES, heads * HEAD), 1) // HEAD
    return ((rows % 16 == cols) & (rows < 48)).astype(bf16)


def collector(heads):
    rows = iota((heads * HEAD, LANES), 0) // HEAD
    cols = iota((heads * HEAD, LANES), 1)
    return ((cols % 16 == rows) & (cols < 48)).astype(bf16)


def split3(q):
    hi = q.astype(bf16).astype(f32)
    rest = q - hi
    mid = rest.astype(bf16).astype(f32)
    return hi, mid, rest - mid


def pack3(q):
    lane = iota(q.shape, 1)
    hi, mid, low = split3(q)
    return jnp.where(lane < 16, hi, jnp.where(lane < 32, mid, low)).astype(bf16)


def exact_mm(a, q):
    return sum(mm(a, part.astype(bf16)) for part in split3(q))


def turn(v):
    return v.astype(f32).T.astype(bf16)


def head_sums(q, col):
    hi = q.astype(bf16)
    lo = (q - hi.astype(f32)).astype(bf16)
    return mm(hi, col) + mm(lo, col)


def softplus(v):
    return jnp.maximum(v, 0.0) + jnp.log1p(jnp.exp(-jnp.abs(v)))


def sigmoid(v):
    return 0.5 * jnp.tanh(0.5 * v) + 0.5


def fold8(q):
    return jnp.sum(q.reshape(q.shape[0] // 8, 8, q.shape[1]), axis=0)


def packs(steps, within):
    tails = jnp.exp(within[L - 1 : L, :] - within)
    return pack3(steps), pack3(jnp.exp(within)), pack3(tails)


def load_rows(info, pieces, places, w, sem, cols=slice(None)):
    copies = []
    for piece, (offset, masks) in zip(pieces, places):
        count = piece.shape[1]
        for k, mask in enumerate(masks):
            slot = 0 if mask is None else (info[1] ^ mask)
            rows = pl.ds(pl.multiple_of(slot * count, 16), count)
            if cols == slice(None):
                src = piece.at[k]
                dst = w.at[rows, pl.ds(offset, piece.shape[2])]
            else:
                src = piece.at[k, :, cols]
                dst = w.at[rows, :]
            copies.append(pltpu.make_async_copy(src, dst, sem.at[len(copies)]))
    for copy in copies:
        copy.start()
    for copy in copies:
        copy.wait()


def store_rows(info, acc, outs, masks, count):
    each = len(masks) // len(outs)
    for at, mask in enumerate(masks):
        slot = 0 if mask is None else (info[1] ^ mask)
        rows = pl.ds(pl.multiple_of(slot * count, 16), count)
        start = at % each * count
        outs[at // each][start : start + count, :] = acc[rows, :].astype(bf16)


def row_products(acc, w, width):
    total = jnp.zeros((acc.shape[0], LANES), f32)
    for at in range(0, width, LANES):
        ps = slice(at, at + LANES)
        total += acc[:, ps] * w[:, ps].astype(f32)
    return total


def forward_kernel(
    places, info, own, oth, gin, conv, bias, dtb, rate, dsk, expand, tri_r, *rest
):
    count = len(places)
    pieces = rest[:count]
    (normed_o, xbc_o, act_o, dsilu_o, step_o, within_o, mixed_o, sin_o, state, buf, w, sem) = rest[
        count:
    ]
    c = pl.program_id(0)
    half = pl.num_programs(0) // 2
    width = dsk.shape[1]
    heads = width // HEAD
    cols = width + 2 * NS

    @pl.when(c == 0)
    def _():
        load_rows(info, pieces, places, w, sem)
        state[...] = jnp.zeros_like(state)
        buf[:, 0:8] = jnp.zeros((cols // LANES, 8, LANES), f32)

    mine = (c // half) == info[0]
    r = jnp.where(mine, own[...].astype(f32), oth[...].astype(f32))
    inv = lax.rsqrt(jnp.mean(r * r, axis=1, keepdims=True) + eps)
    normed = (r * inv * gin[...]).astype(bf16)
    normed_o[...] = normed
    step_raw = mm(normed, w[:, cols:])
    step_o[...] = step_raw
    steps = softplus(step_raw + dtb[...])
    within = exact_mm(tri_r[...], steps * rate[...])
    within_o[...] = within
    p_steps, p_grown, p_tails = packs(steps, within)
    within_t = within.T

    def conv_strip(cs):
        n = cs.start // LANES
        v = bias[:, cs] + conv[3:4, cs] * buf[n, 8 : 8 + L]
        for k in range(3):
            v = v + conv[k : k + 1, cs] * buf[n, 5 + k : 5 + k + L]
        buf[n, 0:8] = buf[n, L : L + 8]
        sig = sigmoid(v)
        value = v * sig
        dsilu_o[:, cs] = (sig + value * (1.0 - sig)).astype(bf16)
        act_o[:, cs] = value.astype(bf16)

    for at in range(cols - 2 * LANES, -1, -2 * LANES):
        ws = slice(at, at + 2 * LANES)
        xb = mm(normed, w[:, ws]).astype(bf16)
        xbc_o[:, ws] = xb
        xf = xb.astype(f32)
        buf[at // LANES, 8:] = xf[:, :LANES]
        buf[at // LANES + 1, 8:] = xf[:, LANES:]
        conv_strip(slice(at, at + LANES))
        conv_strip(slice(at + LANES, at + 2 * LANES))

    b = act_o[:, width : width + NS]
    cc = act_o[:, width + NS :]
    bt = turn(b)
    inter = mm(cc, b, NT)
    hl = L // 2
    tri = iota((hl, hl), 0) >= iota((hl, hl), 1)
    left = iota((L, LANES), 1) < HEAD
    zero = jnp.zeros((L, LANES), bf16)
    for quad in range(heads // 4):
        qs = slice(quad * 2 * LANES, (quad + 1) * 2 * LANES)
        steps_e = mm(p_steps, expand[:, qs])
        grown_e = mm(p_grown, expand[:, qs])
        tails_e = mm(p_tails, expand[:, qs])
        x = act_o[:, qs].astype(f32)
        scaled = x * steps_e
        scaled_b = scaled.astype(bf16)
        sin = state[:, qs]
        sin_o[0, :, qs] = sin
        base = mm(cc, sin.astype(bf16)) * grown_e + dsk[:, qs] * x
        state[:, qs] = sin * grown_e[L - 1 : L, :] + mm(bt, (scaled * tails_e).astype(bf16))
        for side in range(2):
            pair = 2 * quad + side
            ls = slice(side * LANES, (side + 1) * LANES)
            ps = slice(pair * LANES, (pair + 1) * LANES)
            x2 = scaled_b[:, ls]
            xe = jnp.where(left, x2, zero)
            xo = jnp.where(left, zero, x2)
            tops, bots = [], []
            for h in (2 * pair, 2 * pair + 1):
                wc = within[:, h : h + 1]
                wr = within_t[h : h + 1, :]
                d_tl = jnp.exp(jnp.where(tri, wc[:hl] - wr[:, :hl], -1e30))
                d_bl = jnp.exp(wc[hl:] - wr[:, :hl])
                d_br = jnp.exp(jnp.where(tri, wc[hl:] - wr[:, hl:], -1e30))
                tops.append((inter[:hl, :hl] * d_tl).astype(bf16))
                bots.append((inter[hl:, :hl] * d_bl).astype(bf16))
                bots.append((inter[hl:, hl:] * d_br).astype(bf16))
            top = mm(
                jnp.concatenate(tops, axis=1), jnp.concatenate([xe[:hl], xo[:hl]], axis=0)
            )
            bot = mm(jnp.concatenate(bots, axis=1), jnp.concatenate([xe, xo], axis=0))
            mixed_o[:hl, ps] = top + base[:hl, ls]
            mixed_o[hl:, ps] = bot + base[hl:, ls]


def gate_kernel(places, info, cown, coth, normed, mixed, gout, *rest):
    count = len(places)
    pieces = rest[:count]
    gate_o, gno_o, sums_o, w, sem = rest[count:]
    c = pl.program_id(0)
    half = pl.num_programs(0) // 2
    width = gout.shape[1]

    @pl.when(c == 0)
    def _():
        load_rows(info, pieces, places, w, sem)

    mine = (c // half) == info[0]
    cot = jnp.where(mine, cown[...].astype(f32), coth[...].astype(f32)).astype(bf16)
    squares = jnp.zeros((R, LANES), f32)
    products = jnp.zeros((R, LANES), f32)
    for at in range(0, width, 2 * LANES):
        gate = mm(normed[...], w[:, at : at + 2 * LANES]).astype(bf16)
        gno = mm(cot, w[:, width + at : width + at + 2 * LANES])
        gate_o[:, at : at + 2 * LANES] = gate
        gno_o[:, at : at + 2 * LANES] = gno
        for ls in (slice(0, LANES), slice(LANES, 2 * LANES)):
            ps = slice(at + ls.start, at + ls.stop)
            gf = gate[:, ls].astype(f32)
            gated = mixed[:, ps] * (gf * sigmoid(gf))
            squares += gated * gated
            products += gno[:, ls] * gout[:, ps] * gated
    sums_o[0:8, :] = jnp.broadcast_to(jnp.sum(squares.T, axis=0, keepdims=True), (8, R))
    sums_o[8:16, :] = jnp.broadcast_to(jnp.sum(products.T, axis=0, keepdims=True), (8, R))


def gate_back_kernel(
    places, masks, info, cown, coth, normed, mixed, gate, gno, sown, soth, gout, *rest
):
    count = len(places)
    pieces = rest[:count]
    rest = rest[count:]
    parts = len(rest) - 11
    (sent_o, kept_o, ggate_o, gm_o, ggo_o, gain_o) = rest[:6]
    gw_o = rest[6 : 6 + parts]
    acc, acc_g, w, nout, sem = rest[6 + parts :]
    c = pl.program_id(0)
    last = pl.num_programs(0) - 1
    half = pl.num_programs(0) // 2
    width = gout.shape[1]

    @pl.when(c == 0)
    def _():
        load_rows(info, pieces, places, w, sem)
        acc[...] = jnp.zeros_like(acc)
        acc_g[...] = jnp.zeros_like(acc_g)

    cot = jnp.where(c < half, coth[...].astype(f32), cown[...].astype(f32)).astype(bf16)
    inner_total = 2.0 * width
    s = sown[...] + soth[...]
    scale_r = lax.rsqrt(s[0:1] / inner_total + eps)
    coef_r = scale_r * scale_r * scale_r * (s[8:9] / inner_total)
    scale = jnp.broadcast_to(scale_r, (LANES, R)).T
    coef = jnp.broadcast_to(coef_r, (LANES, R)).T
    for at in range(0, width, LANES):
        ps = slice(at, at + LANES)
        gain = gout[:, ps]
        gf = gate[:, ps].astype(f32)
        sig = sigmoid(gf)
        silu = gf * sig
        mix = mixed[:, ps]
        gated = mix * silu
        grad = gno[:, ps]
        unit = gated * scale
        nout[:, ps] = (unit * gain).astype(bf16)
        acc_g[:, ps] += fold8(grad * unit)
        grad_gated = scale * (grad * gain) - gated * coef
        ggate_o[:, ps] = (grad_gated * mix * (sig + silu * (1.0 - sig))).astype(bf16)
        gm_o[:, ps] = (grad_gated * silu).astype(bf16)
    branch = mm(nout[...], w[:, width:], NT).astype(bf16)

    @pl.when(c < half)
    def _():
        sent_o[...] = branch

    @pl.when(c >= half)
    def _():
        kept_o[...] = branch

    acc[:, :width] += mm(normed[...], ggate_o[...], TN)
    acc[:, width:] += mm(cot, nout[...], TN)

    @pl.when(c == last)
    def _():
        store_rows(info, acc, gw_o, masks, acc.shape[0] // len(masks))
        ggo_o[...] = acc_g[...]
        gain_o[...] = row_products(acc, w, width)


def scan_back_kernel(
    masks, places, info, xbc, act_r, dsilu, step, within_r, mixed, sin_r, gm, normed, conv, dtb, rate, dsk,
    expand, collect, tri_r, ggo, gain_z, *rest,
):
    count = len(places)
    pieces = rest[:count]
    gx_o, small_o = rest[count : count + 2]
    gw_o = rest[count + 2 : -8]
    dstate, dvbuf, acc_w, acc_c, acc_s, acc_h, w, sem = rest[-8:]
    i = pl.program_id(0)
    last = pl.num_programs(0) - 1
    width = dsk.shape[1]
    heads = width // HEAD
    cols = width + 2 * NS

    @pl.when(i == 0)
    def _():
        load_rows(info, pieces, places, w, sem)
        dstate[...] = jnp.zeros_like(dstate)
        dvbuf[...] = jnp.zeros_like(dvbuf)
        acc_w[...] = jnp.zeros_like(acc_w)
        acc_c[...] = jnp.zeros_like(acc_c)
        acc_s[...] = jnp.zeros_like(acc_s)
        acc_h[...] = jnp.zeros_like(acc_h)

    def conv_strip(dpost, cs):
        dv = dpost * dsilu[:, cs].astype(f32)
        n = cs.start // LANES
        dvbuf[n, 0:L] = dv
        xin = xbc[:, cs].astype(f32)
        acc_c[4, :, cs] += fold8(dv)
        acc_c[3, :, cs] += fold8(dv * xin)
        dxin = conv[3:4, cs] * dv
        for k in range(3):
            ahead = dvbuf[n, 3 - k : 3 - k + L]
            acc_c[k, :, cs] += fold8(ahead * xin)
            dxin = dxin + conv[k : k + 1, cs] * ahead
        dvbuf[n, L : L + 8] = dv[0:8, :]
        gx_o[:, cs] = dxin.astype(bf16)

    b = act_r[:, width : width + NS]
    cc = act_r[:, width + NS :]
    ct = turn(cc)
    step_raw = step[...]
    within = within_r[...]
    steps = softplus(step_raw + dtb[...])
    p_steps, p_grown, p_tails = packs(steps, within)
    within_t = within.T
    inter_t = mm(b, cc, NT)
    hl = L // 2
    tri = iota((hl, hl), 0) <= iota((hl, hl), 1)
    left = iota((L, LANES), 1) < HEAD
    zero = jnp.zeros((L, LANES), bf16)
    dg_tl = jnp.zeros((hl, hl), f32)
    dg_tr = jnp.zeros((hl, hl), f32)
    dg_br = jnp.zeros((hl, hl), f32)
    dc = jnp.zeros((L, NS), f32)
    db = jnp.zeros((L, NS), f32)
    q_h = jnp.zeros((L, LANES), f32)
    s_h = jnp.zeros((L, LANES), f32)
    ends_h = jnp.zeros((8, LANES), f32)
    for quad in range(heads // 4):
        qs = slice(quad * 2 * LANES, (quad + 1) * 2 * LANES)
        steps_e = mm(p_steps, expand[:, qs])
        grown_e = mm(p_grown, expand[:, qs])
        tails_e = mm(p_tails, expand[:, qs])
        x = act_r[:, qs].astype(f32)
        scaled = x * steps_e
        scaled_b = scaled.astype(bf16)
        scaled_f = scaled_b.astype(f32)
        gmb = gm[:, qs]
        gmf = gmb.astype(f32)
        ds = dstate[:, qs]
        ds_b = ds.astype(bf16)
        sin = sin_r[0, :, qs]
        last_grown = grown_e[L - 1 : L, :]
        gm_grown = (gmf * grown_e).astype(bf16)
        dc += mm(gm_grown, sin.astype(bf16), NT)
        db += mm((scaled * tails_e).astype(bf16), ds_b, NT)
        dstate[:, qs] = ds * last_grown + mm(ct, gm_grown)
        state_part = mm(b, ds_b) * tails_e
        ends = jnp.sum(scaled_f * state_part, axis=0, keepdims=True) + last_grown * jnp.sum(
            sin * ds, axis=0, keepdims=True
        )
        collect_q = collect[qs, :]
        ends_h += head_sums(jnp.broadcast_to(ends, (8, 2 * LANES)), collect_q)
        his, los, prods = [], [], []
        for side in range(2):
            pair = 2 * quad + side
            ls = slice(side * LANES, (side + 1) * LANES)
            ps = slice(pair * LANES, (pair + 1) * LANES)
            x2 = scaled_b[:, ls]
            g2 = gmb[:, ls]
            ge = jnp.where(left, g2, zero)
            go = jnp.where(left, zero, g2)
            g_both = jnp.concatenate([ge, go], axis=0)
            g_bot = jnp.concatenate([ge[hl:], go[hl:]], axis=0)
            dm_top = mm(x2[:hl], g_both, NT)
            dm_bot = mm(x2[hl:], g_bot, NT)
            tops, bots = [], []
            for k, h in enumerate((2 * pair, 2 * pair + 1)):
                wc = within[:, h : h + 1]
                wr = within_t[h : h + 1, :]
                d_tl = jnp.exp(jnp.where(tri, wr[:, :hl] - wc[:hl], -1e30))
                d_tr = jnp.exp(wr[:, hl:] - wc[:hl])
                d_br = jnp.exp(jnp.where(tri, wr[:, hl:] - wc[hl:], -1e30))
                tops.append((inter_t[:hl, :hl] * d_tl).astype(bf16))
                tops.append((inter_t[:hl, hl:] * d_tr).astype(bf16))
                bots.append((inter_t[hl:, hl:] * d_br).astype(bf16))
                dg_tl += dm_top[:, k * L : k * L + hl] * d_tl
                dg_tr += dm_top[:, k * L + hl : (k + 1) * L] * d_tr
                dg_br += dm_bot[:, k * hl : (k + 1) * hl] * d_br
            top = mm(jnp.concatenate(tops, axis=1), g_both)
            bot = mm(jnp.concatenate(bots, axis=1), g_bot)
            dscaled = jnp.concatenate([top, bot], axis=0) + state_part[:, ls]
            xs = x[:, ls]
            gs = gmf[:, ls]
            y = mixed[:, ps] - dsk[:, ps] * xs
            q = gs * y - scaled_f[:, ls] * dscaled
            hi = q.astype(bf16)
            his.append(hi)
            los.append((q - hi.astype(f32)).astype(bf16))
            prods.append((dscaled * xs).astype(bf16))
            acc_s[:, ps] += fold8(gs * xs)
            conv_strip(dscaled * steps_e[:, ls] + dsk[:, ps] * gs, ps)
        q_h += mm(jnp.concatenate(his, axis=1), collect_q)
        q_h += mm(jnp.concatenate(los, axis=1), collect_q)
        s_h += mm(jnp.concatenate(prods, axis=1), collect_q)
    top = jnp.concatenate([dg_tl, dg_tr], axis=1)
    bot = jnp.concatenate([jnp.zeros((hl, hl), f32), dg_br], axis=1)
    dg = jnp.concatenate([top, bot], axis=0)
    dc += mm(dg.T.astype(bf16), b)
    db += mm(dg.astype(bf16), cc)
    conv_strip(db, slice(width, width + NS))
    conv_strip(dc, slice(width + NS, cols))
    d_rate = exact_mm(tri_r[...], q_h) + ends_h[0:1, :]
    d_steps = d_rate * rate[...] + s_h
    sig_s = sigmoid(step_raw + dtb[...])
    keep = iota((L, LANES), 1) < heads
    d_raw = jnp.where(keep, d_steps * sig_s, 0.0)
    acc_h[0:8, :] += fold8(d_raw)
    acc_h[8:16, :] += fold8(d_rate * steps * rate[...])
    gx_o[:, cols:] = d_raw.astype(bf16)
    acc_w[...] += mm(normed[...], gx_o[...], TN)

    @pl.when(i == last)
    def _():
        store_rows(info, acc_w, gw_o, masks, acc_w.shape[0] // len(masks))
        small_o[...] = jnp.zeros_like(small_o)
        for k in range(5):
            small_o[k : k + 1, :cols] = jnp.sum(acc_c[k], axis=0, keepdims=True)
        for k in range(2):
            head = acc_h[8 * k : 8 * k + 8, :]
            small_o[k : k + 1, cols:] = jnp.sum(head, axis=0, keepdims=True)
        small_o[5:6, :width] = jnp.sum(acc_s[...], axis=0, keepdims=True)
        small_o[6:7, :width] = jnp.sum(ggo[...], axis=0, keepdims=True)
        gains = row_products(acc_w, w, cols + LANES) + gain_z[...]
        small_o[7:8, : acc_w.shape[0]] = jnp.sum(gains.T, axis=0, keepdims=True)
        if len(gw_o) > 1:
            small = small_o[...]
            hi = small.astype(bf16).astype(f32)
            parts = jnp.concatenate([hi, small - hi], axis=0).astype(bf16)
            for out in gw_o:
                out[out.shape[0] - 16 :, :] = parts


def input_back_kernel(zplaces, xplaces, info, ggate, gx, *rest):
    zcount, xcount = len(zplaces), len(xplaces)
    zpieces = rest[:zcount]
    xpieces = rest[zcount : zcount + xcount]
    sent_o, kept_o, wz, wx, dnb, zsem, xsem = rest[zcount + xcount :]
    c = pl.program_id(0)
    half = pl.num_programs(0) // 2
    width = ggate.shape[1]

    @pl.when(c == 0)
    def _():
        load_rows(info, zpieces, zplaces, wz, zsem, pl.ds(0, width))
        load_rows(info, xpieces, xplaces, wx, xsem)

    dim = dnb.shape[1]
    for at in range(0, dim, 2 * LANES):
        ds = slice(at, at + 2 * LANES)
        dn = mm(ggate[...], wz[ds, :], NT) + mm(gx[...], wx[ds, :], NT)
        dnb[:, ds] = dn.astype(bf16)

    @pl.when(c < half)
    def _():
        sent_o[...] = dnb[...]

    @pl.when(c >= half)
    def _():
        kept_o[...] = dnb[...]


def finish_kernel(resid, cot, gin, dn_own, dn_oth, br_own, br_oth, out_o, gres_o):
    r = resid[...].astype(f32)
    inv = lax.rsqrt(jnp.mean(r * r, axis=1, keepdims=True) + eps)
    out_o[...] = (r + (br_own[...].astype(f32) + br_oth[...].astype(f32))).astype(bf16)
    u = (dn_own[...].astype(f32) + dn_oth[...].astype(f32)) * gin[...]
    mean = jnp.mean(u * r, axis=1, keepdims=True)
    gres_o[...] = cot[...].astype(f32) + inv * u - r * (inv * inv * inv * mean)


def swap(v, bit, axis):
    size = lax.axis_size(axis)
    return lax.ppermute(v, axis, [(i, i ^ bit) for i in range(size)])


NEAR = (0, 1, 2, 3)
FAR = (0, 4, 8, 12)


def direct(size, rows):
    return size == 16 and rows % 16 == 0


def gather_whole(v, bits):
    size = lax.axis_size("dp")
    me = lax.axis_index("dp")
    held = v[None]
    for bit in sorted(bits):
        got = swap(held, bit, "dp")
        upper = (me & bit) != 0
        held = jnp.where(
            upper, jnp.concatenate([got, held]), jnp.concatenate([held, got])
        )
    return held.reshape(1, size * v.shape[0], v.shape[1])


def whole_pieces(v, bits):
    return [gather_whole(v, bits)], [(0, (None,))]


def gather_far(v):
    return [swap(v, far, "dp") for far in FAR[1:]]


def gather_near(held):
    pieces = [held] + [swap(held, near, "dp") for near in NEAR[1:]]
    return pieces, [(0, tuple(near ^ far for far in FAR)) for near in NEAR]


def scatter_shapes(size, rows, cols, extra=0):
    if not direct(size, rows):
        return [jax.ShapeDtypeStruct((size * rows, cols), bf16)], (None,)
    masks = tuple(near ^ far for near in NEAR for far in FAR)
    return [jax.ShapeDtypeStruct((4 * rows + extra, cols), bf16)] * 4, masks


def both_parts(v):
    return v[-16:-8] + v[-8:]


def scatter_near(pieces):
    return [pieces[0]] + [swap(p, near, "dp") for p, near in zip(pieces[1:], NEAR[1:])]


def scatter_far(total, rows, extra=None):
    blocks = [total[k * rows : (k + 1) * rows] for k in range(4)]
    if extra is not None:
        hi = extra.astype(bf16).astype(f32)
        parts = jnp.concatenate([hi, (extra - hi).astype(bf16).astype(f32)])
        blocks = [jnp.concatenate([block, parts]) for block in blocks]
    sent = [swap(block.astype(bf16), far, "dp") for block, far in zip(blocks[1:], FAR[1:])]
    return blocks[:1] + sent


def sum_pieces(pieces):
    return sum(p.astype(f32) for p in pieces)


def scatter_whole(g, bits):
    me = lax.axis_index("dp")
    rows = g.shape[0] // lax.axis_size("dp")
    left = sorted(bits, reverse=True)
    cur = g.reshape([2] * len(left) + [rows, g.shape[1]])
    for bit in sorted(bits):
        dim = left.index(bit)
        mine = ((me & bit) != 0).astype(jnp.int32)
        send = lax.dynamic_index_in_dim(cur, 1 - mine, dim, keepdims=False)
        keep = lax.dynamic_index_in_dim(cur, mine, dim, keepdims=False)
        got = swap(send.astype(bf16), bit, "dp")
        cur = keep.astype(f32) + got.astype(f32)
        left.pop(dim)
    return cur.astype(f32)


def full(shape):
    zeros = (0,) * len(shape)
    return pl.BlockSpec(shape, lambda c, *_: zeros)


def rows_spec(count, width, index=lambda c, info: c):
    return pl.BlockSpec((count, width), lambda c, info: (index(c, info), 0))


def call(kernel, name, vmem, grid, ins, outs, scratch, info, *args, **more):
    specs = [spec for spec, _ in outs]
    shapes = [item for _, item in outs]
    return pl.pallas_call(
        kernel,
        grid_spec=pltpu.PrefetchScalarGridSpec(
            num_scalar_prefetch=1, grid=(grid,), in_specs=ins, out_specs=specs,
            scratch_shapes=scratch,
        ),
        out_shape=shapes,
        compiler_params=pltpu.CompilerParams(
            dimension_semantics=("arbitrary",), vmem_limit_bytes=vmem * MIB
        ),
        name=name,
        **more,
    )(info, *args)


def local(
    resid, gain_in, w_z, w_x, w_bc, w_dt, conv_x, bias_x, conv_bc, bias_bc, dt_bias, a_log, d_skip,
    gain_out, w_out, cotangent,
):
    size = lax.axis_size("dp")
    place = lax.axis_index("tensor")
    heads = a_log.shape[0]
    width = heads * HEAD
    dim = resid.shape[1]
    rows = w_z.shape[0]
    cols = width + 2 * NS
    half_rows = resid.shape[0]
    tokens = 2 * half_rows
    assert tokens == SEQ_LEN
    chunks = tokens // L
    half = chunks // 2
    shape = jax.ShapeDtypeStruct
    bits = [1 << k for k in range(size.bit_length() - 1)]

    def lanes3(v):
        pad = [(0, 0)] * (v.ndim - 1)
        group = jnp.pad(v, pad + [(0, 16 - heads)])
        return jnp.pad(jnp.concatenate([group] * 3, axis=-1), pad + [(0, LANES - 48)])

    first = jnp.concatenate([w_x, w_bc, lanes3(w_dt)], axis=1)
    second = jnp.concatenate([w_z, w_out.T], axis=1)
    conv = jnp.concatenate([conv_x, conv_bc], axis=1)
    bias = jnp.concatenate([bias_x, bias_bc])[None]
    dtb = lanes3(dt_bias[None])
    rate = lanes3(-jnp.exp(a_log)[None])
    dsk = jnp.repeat(d_skip, HEAD)[None]
    gin = gain_in[None]
    gout = gain_out[None]
    expand = expander(heads)
    if direct(size, rows):
        cut = first.shape[1]
        both = jnp.concatenate([first, second], axis=1)
        both, got, resid_in, cot_in, conv, bias, dtb, rate, dsk, gin, gout, expand = (
            lax.optimization_barrier(
                (
                    both, gather_far(both), resid, cotangent, conv, bias, dtb, rate, dsk, gin,
                    gout, expand,
                )
            )
        )
        held = [both] + got
        wx, wx_at = gather_near(jnp.stack([v[:, :cut] for v in held]))
        resid_oth = swap(resid_in, 1, "tensor")
        cot_oth = swap(cot_in, 1, "tensor")
        held, resid_oth, cot_oth, wx = lax.optimization_barrier((held, resid_oth, cot_oth, wx))
        wz, wz_at = gather_near(jnp.stack([v[:, cut:] for v in held]))
    else:
        resid_oth = swap(resid, 1, "tensor")
        cot_oth = swap(cotangent, 1, "tensor")
        wx, wx_at = whole_pieces(first, bits)
        wz, wz_at = whole_pieces(second, bits)

    info = jnp.stack([place, lax.axis_index("dp")]).astype(jnp.int32)
    anywhere = pl.BlockSpec(memory_space=pl.ANY)

    def copies(at):
        return pltpu.SemaphoreType.DMA((sum(len(masks) for _, masks in at),))

    def tok(width, dtype):
        return shape((tokens, width), dtype)

    own_spec = rows_spec(L, dim, lambda c, info: jnp.clip(c - half * info[0], 0, half - 1))
    oth_spec = rows_spec(L, dim, lambda c, info: jnp.clip(c - half * (1 - info[0]), 0, half - 1))
    wide = rows_spec(L, width)
    normed, xbc, act, dsilu, step_raw, within, mixed, sin = call(
        functools.partial(forward_kernel, wx_at),
        "mix_forward",
        52,
        chunks,
        [
            own_spec, oth_spec, full((1, dim)), full((4, cols)), full((1, cols)),
            full((1, LANES)), full((1, LANES)), full((1, width)), full((LANES, width)),
            full((L, L)),
        ]
        + [anywhere] * len(wx),
        [
            (rows_spec(L, dim), tok(dim, bf16)),
            (rows_spec(L, cols), tok(cols, bf16)),
            (rows_spec(L, cols), tok(cols, bf16)),
            (rows_spec(L, cols), tok(cols, bf16)),
            (rows_spec(L, LANES), tok(LANES, f32)),
            (rows_spec(L, LANES), tok(LANES, f32)),
            (wide, tok(width, f32)),
            (
                pl.BlockSpec((1, NS, width), lambda c, info: (c, 0, 0)),
                shape((chunks, NS, width), f32),
            ),
        ],
        [
            pltpu.VMEM((NS, width), f32), pltpu.VMEM((cols // LANES, L + 8, LANES), f32),
            pltpu.VMEM((dim, cols + LANES), bf16), copies(wx_at),
        ],
        info, resid, resid_oth, gin, conv, bias, dtb, rate, dsk, expand, lower_tri(), *wx,
    )

    steps = tokens // R
    rhalf = steps // 2

    def block(width, index=lambda c, info: c):
        return rows_spec(R, width, index)

    own_r = block(dim, lambda c, info: jnp.clip(c - rhalf * info[0], 0, rhalf - 1))
    oth_r = block(dim, lambda c, info: jnp.clip(c - rhalf * (1 - info[0]), 0, rhalf - 1))
    sums_shape = shape((steps * 16, R), f32)
    gate, gno, sums = call(
        functools.partial(gate_kernel, wz_at),
        "gate_forward",
        52,
        steps,
        [own_r, oth_r, block(dim), block(width), full((1, width))] + [anywhere] * len(wz),
        [
            (block(width), tok(width, bf16)), (block(width), tok(width, f32)),
            (rows_spec(16, R), sums_shape),
        ],
        [pltpu.VMEM((dim, 2 * width), bf16), copies(wz_at)],
        info, cotangent, cot_oth, normed, mixed, gout, *wz,
    )
    sums_oth = swap(sums, 1, "tensor")

    def turned(c, info):
        return jnp.where(c < rhalf, c + rhalf * (1 - info[0]), c - rhalf + rhalf * info[0])

    gw_shapes, masks = scatter_shapes(size, rows, 2 * width)
    twide = block(width, turned)
    lead = block(dim, lambda c, info: jnp.minimum(c, rhalf - 1))
    trail = block(dim, lambda c, info: jnp.maximum(c - rhalf, 0))
    half_shape = shape((half_rows, dim), bf16)
    branch_sent, branch_own, ggate, gm, g_gout, g_gin_z, *gw_zo = call(
        functools.partial(gate_back_kernel, wz_at, masks),
        "gate_backward",
        52,
        steps,
        [
            trail, lead, block(dim, turned), twide, twide, twide,
            rows_spec(16, R, turned), rows_spec(16, R, turned), full((1, width)),
        ]
        + [anywhere] * len(wz),
        [
            (lead, half_shape), (trail, half_shape), (twide, tok(width, bf16)),
            (twide, tok(width, bf16)), (full((8, width)), shape((8, width), f32)),
            (full((dim, LANES)), shape((dim, LANES), f32)),
        ]
        + [(full(item.shape), item) for item in gw_shapes],
        [
            pltpu.VMEM((dim, 2 * width), f32), pltpu.VMEM((8, width), f32),
            pltpu.VMEM((dim, 2 * width), bf16), pltpu.VMEM((R, width), bf16), copies(wz_at),
        ],
        info, cotangent, cot_oth, normed, mixed, gate, gno, sums, sums_oth, gout, *wz,
    )
    branch_oth = swap(branch_sent, 1, "tensor")
    sent_zo = scatter_near(gw_zo) if direct(size, rows) else gw_zo

    def back(c, info):
        return chunks - 1 - c

    rwide = rows_spec(L, width, back)
    rcols = rows_spec(L, cols, back)
    rlanes = rows_spec(L, LANES, back)
    gwx_shapes, masks = scatter_shapes(size, rows, cols + LANES, 16)
    gx, small, *gw_x = call(
        functools.partial(scan_back_kernel, masks, wx_at),
        "mix_backward",
        52,
        chunks,
        [
            rcols, rcols, rcols, rlanes, rlanes, rwide,
            pl.BlockSpec((1, NS, width), lambda c, info: (chunks - 1 - c, 0, 0)),
            rwide, rows_spec(L, dim, back), full((4, cols)), full((1, LANES)),
            full((1, LANES)), full((1, width)), full((LANES, width)), full((width, LANES)),
            full((L, L)), full((8, width)), full((dim, LANES)),
        ]
        + [anywhere] * len(wx),
        [
            (rows_spec(L, cols + LANES, back), tok(cols + LANES, bf16)),
            (full((8, cols + LANES)), shape((8, cols + LANES), f32)),
        ]
        + [(full(item.shape), item) for item in gwx_shapes],
        [
            pltpu.VMEM((NS, width), f32), pltpu.VMEM((cols // LANES, L + 8, LANES), f32),
            pltpu.VMEM((dim, cols + LANES), f32), pltpu.VMEM((5, 8, cols), f32),
            pltpu.VMEM((8, width), f32), pltpu.VMEM((16, LANES), f32),
            pltpu.VMEM((dim, cols + LANES), bf16), copies(wx_at),
        ],
        info, xbc, act, dsilu, step_raw, within, mixed, sin, gm, normed, conv, dtb, rate, dsk,
        expand, collector(heads), upper_tri(), g_gout, g_gin_z, *wx,
    )

    sent_zo, branch_oth, gx, gw_x, small = lax.optimization_barrier(
        (sent_zo, branch_oth, gx, gw_x, small)
    )
    if direct(size, rows):
        sent_x = scatter_near(gw_x)
        far_zo = scatter_far(sum_pieces(sent_zo), rows)

    dn_sent, dn_own = call(
        functools.partial(input_back_kernel, wz_at, wx_at),
        "input_backward",
        32,
        steps,
        [twide, block(cols + LANES, turned)]
        + [anywhere] * (len(wz) + len(wx)),
        [(lead, half_shape), (trail, half_shape)],
        [
            pltpu.VMEM((dim, width), bf16), pltpu.VMEM((dim, cols + LANES), bf16),
            pltpu.VMEM((R, dim), bf16), copies(wz_at), copies(wx_at),
        ],
        info, ggate, gx, *wz, *wx,
    )
    if direct(size, rows):
        sent_x, dn_own, dn_sent = lax.optimization_barrier((sent_x, dn_own, dn_sent))
    dn_oth = swap(dn_sent, 1, "tensor")
    if direct(size, rows):
        total_x = sum_pieces(sent_x)
        far_x = scatter_far(total_x, rows, both_parts(total_x))
        far_zo, dn_oth, dn_own = lax.optimization_barrier((far_zo, dn_oth, dn_own))
        sum_zo = sum_pieces(far_zo)

    dspec = rows_spec(L, dim)
    block_out, grad_resid = call(
        lambda info, *refs: finish_kernel(*refs),
        "finish",
        12,
        half,
        [dspec, dspec, full((1, dim)), dspec, dspec, dspec, dspec],
        [(dspec, half_shape), (dspec, shape((half_rows, dim), f32))],
        [],
        info, resid, cotangent, gin, dn_own, dn_oth, branch_own, branch_oth,
    )

    if direct(size, rows):
        block_out, grad_resid, far_x = lax.optimization_barrier((block_out, grad_resid, far_x))
        sum_x = sum_pieces(far_x)
        small = both_parts(sum_x)
    else:
        sum_zo = scatter_whole(sent_zo[0], bits)
        sum_x = scatter_whole(gw_x[0], bits)
        for bit in bits:
            small = small + swap(small, bit, "dp")
    grad_w_bc = sum_x[:rows, width:cols]
    pair = jnp.concatenate(
        [grad_w_bc.reshape(-1), small[:5, width:cols].reshape(-1), small[7, :dim]]
    )
    pair = pair + swap(pair, 1, "tensor")
    grad_w_bc, bc_g, gain_g = jnp.split(pair, [rows * 2 * NS, (rows + 5) * 2 * NS])
    bc_g = bc_g.reshape(5, 2 * NS)
    return (
        block_out, grad_resid, gain_g / gain_in, sum_zo[:, :width], sum_x[:rows, :width],
        grad_w_bc.reshape(rows, 2 * NS), sum_x[:rows, cols : cols + heads],
        small[:4, :width], small[4, :width], bc_g[:4], bc_g[4], small[0, cols : cols + heads],
        small[1, cols : cols + heads], small[5, :width].reshape(heads, HEAD).sum(axis=1),
        small[6, :width], sum_zo[:, width:].T,
    )


def solution(mesh):
    in_specs = (
        P(("dp", "tensor"), None),
        P(),
        P("dp", "tensor"),
        P("dp", "tensor"),
        P("dp", None),
        P("dp", "tensor"),
        P(None, "tensor"),
        P("tensor"),
        P(),
        P(),
        P("tensor"),
        P("tensor"),
        P("tensor"),
        P("tensor"),
        P("tensor", "dp"),
        P(("dp", "tensor"), None),
    )
    out_specs = (
        P(("dp", "tensor"), None),
        P(("dp", "tensor"), None),
        P(),
        P("dp", "tensor"),
        P("dp", "tensor"),
        P("dp", None),
        P("dp", "tensor"),
        P(None, "tensor"),
        P("tensor"),
        P(),
        P(),
        P("tensor"),
        P("tensor"),
        P("tensor"),
        P("tensor"),
        P("tensor", "dp"),
    )
    return jax.shard_map(local, mesh=mesh, in_specs=in_specs, out_specs=out_specs, check_vma=False)
```

time: 252 us -> 234 us (0.929)
  starting transfers between devices: 46.4 us -> 33.9 us
  waiting for transfers between devices: 31.1 us -> 41.5 us
  Pallas kernels: 141 us -> 132 us
  other arithmetic: 10.6 us -> 5.43 us
    ppermute x37 -> x27, starting transfers between devices: 46.4 us -> 33.9 us  [swap(): return lax.ppermute(v, axis, [(i, i ^ bit) for i in range(size)])]
    ppermute x37 -> x27, waiting for transfers between devices: 31.1 us -> 41.5 us  [swap(): return lax.ppermute(v, axis, [(i, i ^ bit) for i in range(size)])]
    pallas_call x6, Pallas kernels: 141 us -> 132 us  [call(): pl.pallas_call(kernel, grid_spec=pltpu.PrefetchScalarGridSpec(num_scalar_...]
    unnamed x68 -> x51, local copies, waits for them, and re-layouts: 8.17 us -> 10 us
  transfers between devices with their start and end apart: 37 -> 27, of which waited for: 10 -> 7; matrix products, arithmetic and copies ran while one was open for 7% -> 4% of each run, Pallas kernels for 40% -> 39%
where the time goes in v3:
time: 234 us; the launch traced here: 233 us
  Pallas kernels  132 us (56%)
  waiting for transfers between devices  41.5 us (18%)
  starting transfers between devices  33.9 us (14%)
  local copies, waits for them, and re-layouts  19 us (8%)
  other arithmetic  5.43 us (2%)
    pallas_call x6, Pallas kernels, call(): pl.pallas_call(kernel, grid_spec=pltpu.PrefetchScalarGridSpec(num_scalar_...  132 us
    ppermute x27, waiting for transfers between devices, swap(): return lax.ppermute(v, axis, [(i, i ^ bit) for i in range(size)])  41.5 us
    ppermute x27, starting transfers between devices, swap(): return lax.ppermute(v, axis, [(i, i ^ bit) for i in range(size)])  33.9 us
    unnamed x51, local copies, waits for them, and re-layouts  10 us
  transfers between devices with their start and end apart: 27, of which 7 were waited for; matrix products, arithmetic and copies ran while one was open for 4% of the time, Pallas kernels for 39%

profile of v3, /device:TPU:0, one launch (start us, length us, event | category | flops | bytes accessed | tf_op | source)
XLA Modules:
  0.0 232.7 jit_solution(5232519904692782497)
XLA Ops:
  4.9 3.0 %collective-permute-start = (bf16[48,2688]{1,0:T(8,128)(2,1)S(1)}, bf16[48,2688]{1,0:T(8,128)(2,1)S(1)}, u32[]{:S(2)}, u32[]{:S(2)}) collective-permute-start(bf16[48,2688]{1,0:T(8,128)(2,1)S(1)} %bitcast_dynamic-update-slice_fusion), channel_id=1, source_target_pairs={{0,8},{2,10},{4,12},{6,14},{8,0},{10,2},{12,4},{14,6},{16,24},{18,... | collective-permute-start | bytes 774152 | tf_op jit(solution)/shard_map/ppermute | solution.py:536
  8.0 2.6 %collective-permute-start.1 = (bf16[48,2688]{1,0:T(8,128)(2,1)S(1)}, bf16[48,2688]{1,0:T(8,128)(2,1)S(1)}, u32[]{:S(2)}, u32[]{:S(2)}) collective-permute-start(bf16[48,2688]{1,0:T(8,128)(2,1)S(1)} %bitcast_dynamic-update-slice_fusion), channel_id=1, source_target_pairs={{0,16},{2,18},{4,20},{6,22},{8,24},{10,26},{12,28},{14,30},{16,0},... | collective-permute-start | bytes 774152 | tf_op jit(solution)/shard_map/ppermute | solution.py:536
  15.8 3.2 %collective-permute-done = bf16[48,2688]{1,0:T(8,128)(2,1)S(1)} collective-permute-done((bf16[48,2688]{1,0:T(8,128)(2,1)S(1)}, bf16[48,2688]{1,0:T(8,128)(2,1)S(1)}, u32[]{:S(2)}, u32[]{:S(2)}) %collective-permute-start) | collective-permute-done | bytes 258080 | tf_op jit(solution)/shard_map/ppermute | solution.py:536
  18.9 10.1 %collective-permute-done.1 = bf16[48,2688]{1,0:T(8,128)(2,1)S(1)} collective-permute-done((bf16[48,2688]{1,0:T(8,128)(2,1)S(1)}, bf16[48,2688]{1,0:T(8,128)(2,1)S(1)}, u32[]{:S(2)}, u32[]{:S(2)}) %collective-permute-start.1) | collective-permute-done | bytes 258080 | tf_op jit(solution)/shard_map/ppermute | solution.py:536
  29.8 1.6 collective-permute-start.5
  31.4 1.5 collective-permute-start.6
  33.3 9.5 %collective-permute-done.5.rest_1_.rest_5_ = bf16[4,48,1152]{2,1,0:T(8,128)(2,1)S(1)} collective-permute-done((bf16[4,48,1152]{2,1,0:T(8,128)(2,1)S(1)}, bf16[4,48,1152]{2,1,0:T(8,128)(2,1)S(1)}, u32[]{:S(2)}, u32[]{:S(2)}) %collective-permute-start.5) | collective-permute-done | bytes 442400 | tf_op jit(solution)/shard_map/ppermute | solution.py:536
  42.9 9.8 %collective-permute-done.6.rest_2_.rest_6_ = bf16[4,48,1152]{2,1,0:T(8,128)(2,1)S(1)} collective-permute-done((bf16[4,48,1152]{2,1,0:T(8,128)(2,1)S(1)}, bf16[4,48,1152]{2,1,0:T(8,128)(2,1)S(1)}, u32[]{:S(2)}, u32[]{:S(2)}) %collective-permute-start.6) | collective-permute-done | bytes 442400 | tf_op jit(solution)/shard_map/ppermute | solution.py:536
  52.8 1.1 copy-done.19
  54.8 1.6 collective-permute-start.10
  56.3 1.5 collective-permute-start.8
  58.4 1.0 copy-done.12
  59.4 30.1 %mix_forward.1 = (bf16[2048,768]{1,0:T(8,128)(2,1)}, bf16[2048,1024]{1,0:T(8,128)(2,1)}, bf16[2048,1024]{1,0:T(8,128)(2,1)}, bf16[2048,1024]{1,0:T(8,128)(2,1)},...) custom-call(s32[2]{0:T(128)S(1)} %pad_add_fusion.info, ...), custom_call_target="tpu_custom_call" | custom-call | tf_op jit(solution)/shard_map/mix_forward/pallas_call | solution.py:630
  90.3 15.8 %gate_forward.1 = (bf16[2048,768]{1,0:T(8,128)(2,1)}, f32[2048,768]{1,0:T(8,128)}, f32[64,512]{1,0:T(8,128)S(1)}) custom-call(s32[2]{0:T(128)S(1)} %pad_add_fusion.info, bf16[1024,768]{1,0:T(8,128)(2,1)} %refs_1_.1, bf16[1024,768]{1,0:T(8,128)(2,1)} %copy-done.18, bf16[2048,768]{1,0:T(8,128)(2,1)} %get-tuple-element.117.normed, ...), custom_call_target="tpu_custom_call" | custom-call | tf_op jit(solution)/shard_map/gate_forward/pallas_call | solution.py:630
  106.2 1.3 collective-permute-done.11.soth
  107.5 25.8 %gate_backward.1 = (bf16[1024,768]{1,0:T(8,128)(2,1)}, bf16[1024,768]{1,0:T(8,128)(2,1)}, bf16[2048,768]{1,0:T(8,128)(2,1)}, bf16[2048,768]{1,0:T(8,128)(2,1)}, ...) custom-call(s32[2]{0:T(128)S(1)} %pad_add_fusion.info, ...), custom_call_target="tpu_custom_call" | custom-call | tf_op jit(solution)/shard_map/gate_backward/pallas_call | solution.py:630
  133.4 1.1 collective-permute-start.12
  135.5 1.4 collective-permute-start.14
  137.7 44.6 %mix_backward.1 = (bf16[2048,1152]{1,0:T(8,128)(2,1)}, f32[8,1152]{1,0:T(8,128)}, bf16[208,1152]{1,0:T(8,128)(2,1)}, bf16[208,1152]{1,0:T(8,128)(2,1)}, bf16[208...) custom-call(s32[2]{0:T(128)S(1)} %pad_add_fusion.info, bf16[2048,1024]{1,0:T(8,128)(2,1)} %get-tuple-element.132.xbc, ...), custom_call_target="tpu_custom_call" | custom-call | tf_op jit(solution)/shard_map/mix_backward/pallas_call | solution.py:630
  182.4 1.1 collective-permute-start.19
  184.5 1.5 collective-permute-start.21
  186.3 4.7 %collective-permute-start.16 = (bf16[48,1536]{1,0:T(8,128)(2,1)S(1)}, bf16[48,1536]{1,0:T(8,128)(2,1)S(1)}, u32[]{:S(2)}, u32[]{:S(2)}) collective-permute-start(bf16[48,1536]{1,0:T(8,128)(2,1)S(1)} %get-tuple-element.210), channel_id=1, source_target_pairs={{0,8},{2,10},{4,12},{6,14},{8,0},{10,2},{12,4},{14,6},{16,24},{18,... | collective-permute-start | bytes 442376 | tf_op jit(solution)/shard_map/ppermute | solution.py:536
  191.0 1.1 collective-permute-start.17
  192.2 2.3 %copy-done.10 = bf16[2048,1152]{1,0:T(8,128)(2,1)S(1)} copy-done((bf16[2048,1152]{1,0:T(8,128)(2,1)S(1)}, bf16[2048,1152]{1,0:T(8,128)(2,1)}, u32[]{:S(2)}) %copy-start.10) | copy-done | bytes 4718616
  194.6 11.5 %input_backward.1 = (bf16[1024,768]{1,0:T(8,128)(2,1)S(1)}, bf16[1024,768]{1,0:T(8,128)(2,1)S(1)}) custom-call(s32[2]{0:T(128)S(1)} %pad_add_fusion.info, bf16[2048,768]{1,0:T(8,128)(2,1)S(1)} %copy-done.16, bf16[2048,1152]{1,0:T(8,128)(2,1)S(1)} %copy-done.10, bf16[4,48,1536]{2,1,0:T(8,128)(2,1)S(1)} %copy-done.2, bf16[4,48,1536]{2,1,0:T(8,128)(2,1)S(1)} %copy-done.7, ...), custom_call_target="tpu_custom_call" | custom-call | tf_op jit(solution)/shard_map/input_backward/pallas_call | solution.py:630
  206.1 1.5 collective-permute-start.18
  208.0 3.5 %collective-permute-start.23 = (bf16[64,1152]{1,0:T(8,128)(2,1)S(1)}, bf16[64,1152]{1,0:T(8,128)(2,1)S(1)}, u32[]{:S(2)}, u32[]{:S(2)}) collective-permute-start(bf16[64,1152]{1,0:T(8,128)(2,1)S(1)} %get-tuple-element.219), channel_id=1, source_target_pairs={{0,8},{2,10},{4,12},{6,14},{8,0},{10,2},{12,4},{14,6},{16,24},{18,... | collective-permute-start | bytes 442376 | tf_op jit(solution)/shard_map/ppermute | solution.py:536
  211.5 1.1 collective-permute-start.24
  212.6 1.4 collective-permute-start.25
  214.1 3.9 %finish.1 = (bf16[1024,768]{1,0:T(8,128)(2,1)}, f32[1024,768]{1,0:T(8,128)}) custom-call(s32[2]{0:T(128)S(1)} %pad_add_fusion.info, bf16[1024,768]{1,0:T(8,128)(2,1)S(1)} %copy-done.3, bf16[1024,768]{1,0:T(8,128)(2,1)S(1)} %copy-done, f32[1,768]{1,0:T(1,128)S(1)} %broadcast_in_dim.19.gin.refs_2_, bf16[1024,768]{1,0:T(8,128)(2,1)S(1)} %get-tuple-element.160.refs_3_, ...), custom_call_target="tpu_custom_call" | custom-call | tf_op jit(solution)/shard_map/finish/pallas_call | solution.py:630
  218.0 1.1 collective-permute-done.23
  219.1 6.3 %collective-permute-done.24 = bf16[64,1152]{1,0:T(8,128)(2,1)S(1)} collective-permute-done((bf16[64,1152]{1,0:T(8,128)(2,1)S(1)}, bf16[64,1152]{1,0:T(8,128)(2,1)S(1)}, u32[]{:S(2)}, u32[]{:S(2)}) %collective-permute-start.24) | collective-permute-done | bytes 147488 | tf_op jit(solution)/shard_map/ppermute | solution.py:536
  (142 shorter events, 23.7 us)
Async XLA Ops:
  4.9 14.0 %collective-permute-start = (bf16[48,2688]{1,0:T(8,128)(2,1)S(1)}, bf16[48,2688]{1,0:T(8,128)(2,1)S(1)}, u32[]{:S(2)}, u32[]{:S(2)}) collective-permute-start(bf16[48,2688]{1,0:T(8,128)(2,1)S(1)} %bitcast_dynamic-update-slice_fusion), channel_id=1, source_target_pairs={{0,8},{2,10},{4,12},{6,14},{8,0},{10,2},{12,4},{14,6},{16,24},{18,... | collective-permute-start | bytes 774152 | tf_op jit(solution)/shard_map/ppermute | solution.py:536
  8.0 21.1 %collective-permute-start.1 = (bf16[48,2688]{1,0:T(8,128)(2,1)S(1)}, bf16[48,2688]{1,0:T(8,128)(2,1)S(1)}, u32[]{:S(2)}, u32[]{:S(2)}) collective-permute-start(bf16[48,2688]{1,0:T(8,128)(2,1)S(1)} %bitcast_dynamic-update-slice_fusion), channel_id=1, source_target_pairs={{0,16},{2,18},{4,20},{6,22},{8,24},{10,26},{12,28},{14,30},{16,0},... | collective-permute-start | bytes 774152 | tf_op jit(solution)/shard_map/ppermute | solution.py:536
  10.6 18.5 %collective-permute-start.2 = (bf16[48,2688]{1,0:T(8,128)(2,1)S(1)}, bf16[48,2688]{1,0:T(8,128)(2,1)S(1)}, u32[]{:S(2)}, u32[]{:S(2)}) collective-permute-start(bf16[48,2688]{1,0:T(8,128)(2,1)S(1)} %bitcast_dynamic-update-slice_fusion), channel_id=1, source_target_pairs={{0,24},{2,26},{4,28},{6,30},{8,16},{10,18},{12,20},{14,22},{16,8},... | collective-permute-start | bytes 774152 | tf_op jit(solution)/shard_map/ppermute | solution.py:536
  29.1 23.6 %collective-permute-start.3 = (bf16[1024,768]{1,0:T(8,128)(2,1)}, bf16[1024,768]{1,0:T(8,128)(2,1)S(1)}, u32[]{:S(2)}, u32[]{:S(2)}) collective-permute-start(bf16[1024,768]{1,0:T(8,128)(2,1)} %refs_0_.1), channel_id=1, source_target_pairs={{0,1},{1,0},{2,3},{3,2},{4,5},{5,4},{6,7},{7,6},{8,9},{9,8},{10,11... | collective-permute-start | bytes 4718600 | tf_op jit(solution)/shard_map/ppermute | solution.py:536
  29.2 23.5 %collective-permute-start.4 = (bf16[1024,768]{1,0:T(8,128)(2,1)}, bf16[1024,768]{1,0:T(8,128)(2,1)S(1)}, u32[]{:S(2)}, u32[]{:S(2)}) collective-permute-start(bf16[1024,768]{1,0:T(8,128)(2,1)} %refs_1_.1), channel_id=1, source_target_pairs={{0,1},{1,0},{2,3},{3,2},{4,5},{5,4},{6,7},{7,6},{8,9},{9,8},{10,11... | collective-permute-start | bytes 4718600 | tf_op jit(solution)/shard_map/ppermute | solution.py:536
  29.8 13.1 %collective-permute-start.5 = (bf16[4,48,1152]{2,1,0:T(8,128)(2,1)S(1)}, bf16[4,48,1152]{2,1,0:T(8,128)(2,1)S(1)}, u32[]{:S(2)}, u32[]{:S(2)}) collective-permute-start(bf16[4,48,1152]{2,1,0:T(8,128)(2,1)S(1)} %pad_maximum_fusion.1.rest_0_.rest_4_), channel_id=1, source_target_pairs={{0,2},{2,0},{4,6},{6,4},{8,10},{10,8},{12,14},{14,12},{16,18},{18,... | collective-permute-start | bytes 1327112 | tf_op jit(solution)/shard_map/ppermute | solution.py:536
  31.4 21.4 %collective-permute-start.6 = (bf16[4,48,1152]{2,1,0:T(8,128)(2,1)S(1)}, bf16[4,48,1152]{2,1,0:T(8,128)(2,1)S(1)}, u32[]{:S(2)}, u32[]{:S(2)}) collective-permute-start(bf16[4,48,1152]{2,1,0:T(8,128)(2,1)S(1)} %pad_maximum_fusion.1.rest_0_.rest_4_), channel_id=1, source_target_pairs={{0,4},{2,6},{4,0},{6,2},{8,12},{10,14},{12,8},{14,10},{16,20},{18,... | collective-permute-start | bytes 1327112 | tf_op jit(solution)/shard_map/ppermute | solution.py:536
  32.9 19.8 %collective-permute-start.7 = (bf16[4,48,1152]{2,1,0:T(8,128)(2,1)S(1)}, bf16[4,48,1152]{2,1,0:T(8,128)(2,1)S(1)}, u32[]{:S(2)}, u32[]{:S(2)}) collective-permute-start(bf16[4,48,1152]{2,1,0:T(8,128)(2,1)S(1)} %pad_maximum_fusion.1.rest_0_.rest_4_), channel_id=1, source_target_pairs={{0,6},{2,4},{4,2},{6,0},{8,14},{10,12},{12,10},{14,8},{16,22},{18,... | collective-permute-start | bytes 1327112 | tf_op jit(solution)/shard_map/ppermute | solution.py:536
  54.7 34.8 %copy-start.1 = (bf16[4,48,1536]{2,1,0:T(8,128)(2,1)}, bf16[4,48,1536]{2,1,0:T(8,128)(2,1)S(1)}, u32[]{:S(2)}) copy-start(bf16[4,48,1536]{2,1,0:T(8,128)(2,1)S(1)} %pad_maximum_fusion.rest_0_) | copy-start | bytes 1769476
  54.8 34.7 %collective-permute-start.10 = (bf16[4,48,1536]{2,1,0:T(8,128)(2,1)S(1)}, bf16[4,48,1536]{2,1,0:T(8,128)(2,1)S(1)}, u32[]{:S(2)}, u32[]{:S(2)}) collective-permute-start(bf16[4,48,1536]{2,1,0:T(8,128)(2,1)S(1)} %pad_maximum_fusion.rest_0_), channel_id=1, source_target_pairs={{0,6},{2,4},{4,2},{6,0},{8,14},{10,12},{12,10},{14,8},{16,22},{18,... | collective-permute-start | bytes 1769480 | tf_op jit(solution)/shard_map/ppermute | solution.py:536
  56.3 33.2 %collective-permute-start.8 = (bf16[4,48,1536]{2,1,0:T(8,128)(2,1)S(1)}, bf16[4,48,1536]{2,1,0:T(8,128)(2,1)S(1)}, u32[]{:S(2)}, u32[]{:S(2)}) collective-permute-start(bf16[4,48,1536]{2,1,0:T(8,128)(2,1)S(1)} %pad_maximum_fusion.rest_0_), channel_id=1, source_target_pairs={{0,2},{2,0},{4,6},{6,4},{8,10},{10,8},{12,14},{14,12},{16,18},{18,... | collective-permute-start | bytes 1769480 | tf_op jit(solution)/shard_map/ppermute | solution.py:536
  57.8 31.7 %collective-permute-start.9 = (bf16[4,48,1536]{2,1,0:T(8,128)(2,1)S(1)}, bf16[4,48,1536]{2,1,0:T(8,128)(2,1)S(1)}, u32[]{:S(2)}, u32[]{:S(2)}) collective-permute-start(bf16[4,48,1536]{2,1,0:T(8,128)(2,1)S(1)} %pad_maximum_fusion.rest_0_), channel_id=1, source_target_pairs={{0,4},{2,6},{4,0},{6,2},{8,12},{10,14},{12,8},{14,10},{16,20},{18,... | collective-permute-start | bytes 1769480 | tf_op jit(solution)/shard_map/ppermute | solution.py:536
  89.5 16.6 %copy-start.6 = (bf16[4,48,1536]{2,1,0:T(8,128)(2,1)}, bf16[4,48,1536]{2,1,0:T(8,128)(2,1)S(1)}, u32[]{:S(2)}) copy-start(bf16[4,48,1536]{2,1,0:T(8,128)(2,1)S(1)} %collective-permute-done.8.rest_1_) | copy-start | bytes 1769476
  89.5 16.5 %copy-start.8 = (bf16[4,48,1536]{2,1,0:T(8,128)(2,1)}, bf16[4,48,1536]{2,1,0:T(8,128)(2,1)S(1)}, u32[]{:S(2)}) copy-start(bf16[4,48,1536]{2,1,0:T(8,128)(2,1)S(1)} %collective-permute-done.9.rest_2_) | copy-start | bytes 1769476
  106.1 1.4 collective-permute-start.11
  133.3 49.1 %collective-permute-start.15 = (bf16[1024,768]{1,0:T(8,128)(2,1)}, bf16[1024,768]{1,0:T(8,128)(2,1)S(1)}, u32[]{:S(2)}, u32[]{:S(2)}) collective-permute-start(bf16[1024,768]{1,0:T(8,128)(2,1)} %get-tuple-element.131), channel_id=1, source_target_pairs={{0,1},{1,0},{2,3},{3,2},{4,5},{5,4},{6,7},{7,6},{8,9},{9,8},{10,11... | collective-permute-start | bytes 4718600 | tf_op jit(solution)/shard_map/ppermute | solution.py:536
  133.4 48.9 %collective-permute-start.12 = (bf16[192,1536]{1,0:T(8,128)(2,1)S(1)}, bf16[192,1536]{1,0:T(8,128)(2,1)S(1)}, u32[]{:S(2)}, u32[]{:S(2)}) collective-permute-start(bf16[192,1536]{1,0:T(8,128)(2,1)S(1)} %get-tuple-element.128), channel_id=1, source_target_pairs={{0,2},{2,0},{4,6},{6,4},{8,10},{10,8},{12,14},{14,12},{16,18},{18,... | collective-permute-start | bytes 1769480 | tf_op jit(solution)/shard_map/ppermute | solution.py:536
  134.5 47.8 %collective-permute-start.13 = (bf16[192,1536]{1,0:T(8,128)(2,1)}, bf16[192,1536]{1,0:T(8,128)(2,1)S(1)}, u32[]{:S(2)}, u32[]{:S(2)}) collective-permute-start(bf16[192,1536]{1,0:T(8,128)(2,1)} %get-tuple-element.129), channel_id=1, source_target_pairs={{0,4},{2,6},{4,0},{6,2},{8,12},{10,14},{12,8},{14,10},{16,20},{18,... | collective-permute-start | bytes 1769480 | tf_op jit(solution)/shard_map/ppermute | solution.py:536
  135.5 46.9 %collective-permute-start.14 = (bf16[192,1536]{1,0:T(8,128)(2,1)}, bf16[192,1536]{1,0:T(8,128)(2,1)S(1)}, u32[]{:S(2)}, u32[]{:S(2)}) collective-permute-start(bf16[192,1536]{1,0:T(8,128)(2,1)} %get-tuple-element.130), channel_id=1, source_target_pairs={{0,6},{2,4},{4,2},{6,0},{8,14},{10,12},{12,10},{14,8},{16,22},{18,... | collective-permute-start | bytes 1769480 | tf_op jit(solution)/shard_map/ppermute | solution.py:536
  137.7 54.5 %copy-start.16 = (bf16[2048,768]{1,0:T(8,128)(2,1)S(1)}, bf16[2048,768]{1,0:T(8,128)(2,1)}, u32[]{:S(2)}) copy-start(bf16[2048,768]{1,0:T(8,128)(2,1)} %get-tuple-element.154.ggate) | copy-start | bytes 9437188
  182.4 23.7 %collective-permute-start.19 = (bf16[208,1152]{1,0:T(8,128)(2,1)}, bf16[208,1152]{1,0:T(8,128)(2,1)S(1)}, u32[]{:S(2)}, u32[]{:S(2)}) collective-permute-start(bf16[208,1152]{1,0:T(8,128)(2,1)} %get-tuple-element.151), channel_id=1, source_target_pairs={{0,2},{2,0},{4,6},{6,4},{8,10},{10,8},{12,14},{14,12},{16,18},{18,... | collective-permute-start | bytes 1437704 | tf_op jit(solution)/shard_map/ppermute | solution.py:536
  183.5 24.0 %collective-permute-start.20 = (bf16[208,1152]{1,0:T(8,128)(2,1)}, bf16[208,1152]{1,0:T(8,128)(2,1)S(1)}, u32[]{:S(2)}, u32[]{:S(2)}) collective-permute-start(bf16[208,1152]{1,0:T(8,128)(2,1)} %get-tuple-element.152), channel_id=1, source_target_pairs={{0,4},{2,6},{4,0},{6,2},{8,12},{10,14},{12,8},{14,10},{16,20},{18,... | collective-permute-start | bytes 1437704 | tf_op jit(solution)/shard_map/ppermute | solution.py:536
  184.5 23.1 %collective-permute-start.21 = (bf16[208,1152]{1,0:T(8,128)(2,1)}, bf16[208,1152]{1,0:T(8,128)(2,1)S(1)}, u32[]{:S(2)}, u32[]{:S(2)}) collective-permute-start(bf16[208,1152]{1,0:T(8,128)(2,1)} %get-tuple-element.153), channel_id=1, source_target_pairs={{0,6},{2,4},{4,2},{6,0},{8,14},{10,12},{12,10},{14,8},{16,22},{18,... | collective-permute-start | bytes 1437704 | tf_op jit(solution)/shard_map/ppermute | solution.py:536
  186.3 25.2 %collective-permute-start.16 = (bf16[48,1536]{1,0:T(8,128)(2,1)S(1)}, bf16[48,1536]{1,0:T(8,128)(2,1)S(1)}, u32[]{:S(2)}, u32[]{:S(2)}) collective-permute-start(bf16[48,1536]{1,0:T(8,128)(2,1)S(1)} %get-tuple-element.210), channel_id=1, source_target_pairs={{0,8},{2,10},{4,12},{6,14},{8,0},{10,2},{12,4},{14,6},{16,24},{18,... | collective-permute-start | bytes 442376 | tf_op jit(solution)/shard_map/ppermute | solution.py:536
  191.0 21.5 %collective-permute-start.17 = (bf16[48,1536]{1,0:T(8,128)(2,1)S(1)}, bf16[48,1536]{1,0:T(8,128)(2,1)S(1)}, u32[]{:S(2)}, u32[]{:S(2)}) collective-permute-start(bf16[48,1536]{1,0:T(8,128)(2,1)S(1)} %get-tuple-element.209), channel_id=1, source_target_pairs={{0,16},{2,18},{4,20},{6,22},{8,24},{10,26},{12,28},{14,30},{16,0},... | collective-permute-start | bytes 442376 | tf_op jit(solution)/shard_map/ppermute | solution.py:536
  194.6 13.0 %copy-start.20 = (bf16[208,1152]{1,0:T(8,128)(2,1)S(1)}, bf16[208,1152]{1,0:T(8,128)(2,1)}, u32[]{:S(2)}) copy-start(bf16[208,1152]{1,0:T(8,128)(2,1)} %get-tuple-element.166) | copy-start | bytes 1437700
  206.1 8.0 %collective-permute-start.18 = (bf16[48,1536]{1,0:T(8,128)(2,1)S(1)}, bf16[48,1536]{1,0:T(8,128)(2,1)S(1)}, u32[]{:S(2)}, u32[]{:S(2)}) collective-permute-start(bf16[48,1536]{1,0:T(8,128)(2,1)S(1)} %get-tuple-element.208), channel_id=1, source_target_pairs={{0,24},{2,26},{4,28},{6,30},{8,16},{10,18},{12,20},{14,22},{16,8},... | collective-permute-start | bytes 442376 | tf_op jit(solution)/shard_map/ppermute | solution.py:536
  207.6 6.5 %collective-permute-start.22 = (bf16[1024,768]{1,0:T(8,128)(2,1)S(1)}, bf16[1024,768]{1,0:T(8,128)(2,1)S(1)}, u32[]{:S(2)}, u32[]{:S(2)}) collective-permute-start(bf16[1024,768]{1,0:T(8,128)(2,1)S(1)} %get-tuple-element.158), channel_id=1, source_target_pairs={{0,1},{1,0},{2,3},{3,2},{4,5},{5,4},{6,7},{7,6},{8,9},{9,8},{10,11... | collective-permute-start | bytes 4718600 | tf_op jit(solution)/shard_map/ppermute | solution.py:536
  208.0 11.1 %collective-permute-start.23 = (bf16[64,1152]{1,0:T(8,128)(2,1)S(1)}, bf16[64,1152]{1,0:T(8,128)(2,1)S(1)}, u32[]{:S(2)}, u32[]{:S(2)}) collective-permute-start(bf16[64,1152]{1,0:T(8,128)(2,1)S(1)} %get-tuple-element.219), channel_id=1, source_target_pairs={{0,8},{2,10},{4,12},{6,14},{8,0},{10,2},{12,4},{14,6},{16,24},{18,... | collective-permute-start | bytes 442376 | tf_op jit(solution)/shard_map/ppermute | solution.py:536
  211.5 13.9 %collective-permute-start.24 = (bf16[64,1152]{1,0:T(8,128)(2,1)S(1)}, bf16[64,1152]{1,0:T(8,128)(2,1)S(1)}, u32[]{:S(2)}, u32[]{:S(2)}) collective-permute-start(bf16[64,1152]{1,0:T(8,128)(2,1)S(1)} %get-tuple-element.220), channel_id=1, source_target_pairs={{0,16},{2,18},{4,20},{6,22},{8,24},{10,26},{12,28},{14,30},{16,0},... | collective-permute-start | bytes 442376 | tf_op jit(solution)/shard_map/ppermute | solution.py:536
  212.6 12.9 %collective-permute-start.25 = (bf16[64,1152]{1,0:T(8,128)(2,1)S(1)}, bf16[64,1152]{1,0:T(8,128)(2,1)S(1)}, u32[]{:S(2)}, u32[]{:S(2)}) collective-permute-start(bf16[64,1152]{1,0:T(8,128)(2,1)S(1)} %get-tuple-element.218), channel_id=1, source_target_pairs={{0,24},{2,26},{4,28},{6,30},{8,16},{10,18},{12,20},{14,22},{16,8},... | collective-permute-start | bytes 442376 | tf_op jit(solution)/shard_map/ppermute | solution.py:536
  227.0 3.3 %collective-permute-start.26 = (f32[14336]{0:T(1024)S(1)}, f32[14336]{0:T(1024)S(1)}, u32[]{:S(2)}, u32[]{:S(2)}) collective-permute-start(f32[14336]{0:T(1024)S(1)} %pad_maximum_fusion.9), channel_id=1, source_target_pairs={{0,1},{1,0},{2,3},{3,2},{4,5},{5,4},{6,7},{7,6},{8,9},{9,8},{10,11... | collective-permute-start | bytes 172040 | tf_op jit(solution)/shard_map/ppermute | solution.py:536
  (17 other events, 71.8 us)

commit v4 on v3

--- a/solution.py
+++ b/solution.py
@@ -95,6 +95,20 @@
 def packs(steps, within):
     tails = jnp.exp(within[L - 1 : L, :] - within)
     return pack3(steps), pack3(jnp.exp(within)), pack3(tails)
+
+
+CONV, BIAS, GIN, GOUT, DSK, DTB, RATE = 0, 4, 5, 6, 7, 8, 9
+
+
+class vector:
+    def __init__(self, ref, at, width, count=1):
+        self.ref, self.at, self.width, self.count = ref, at, width, count
+
+    def __getitem__(self, key):
+        rows, cols = (slice(None), slice(None)) if key is Ellipsis else key
+        start, stop, _ = rows.indices(self.count)
+        left, right, _ = cols.indices(self.width)
+        return self.ref[self.at + start : self.at + stop, left:right]
 
 
 def load_rows(info, pieces, places, w, sem, cols=slice(None)):
@@ -135,21 +149,26 @@
 
 
 def forward_kernel(
-    places, info, own, oth, gin, conv, bias, dtb, rate, dsk, expand, tri_r, *rest
+    places, info, own, oth, consts, tri_r, *rest
 ):
     count = len(places)
     pieces = rest[:count]
-    (normed_o, xbc_o, act_o, dsilu_o, step_o, within_o, mixed_o, sin_o, state, buf, w, sem) = rest[
-        count:
-    ]
+    (
+        normed_o, xbc_o, act_o, dsilu_o, step_o, within_o, mixed_o, sin_o, state, buf, w, expand,
+        sem,
+    ) = rest[count:]
     c = pl.program_id(0)
     half = pl.num_programs(0) // 2
-    width = dsk.shape[1]
+    width = expand.shape[1]
     heads = width // HEAD
     cols = width + 2 * NS
+    conv, bias = vector(consts, CONV, cols, 4), vector(consts, BIAS, cols)
+    gin, dsk = vector(consts, GIN, own.shape[1]), vector(consts, DSK, width)
+    dtb, rate = vector(consts, DTB, LANES), vector(consts, RATE, LANES)
 
     @pl.when(c == 0)
     def _():
+        expand[...] = expander(heads)
         load_rows(info, pieces, places, w, sem)
         state[...] = jnp.zeros_like(state)
         buf[:, 0:8] = jnp.zeros((cols // LANES, 8, LANES), f32)
@@ -233,13 +252,14 @@
             mixed_o[hl:, ps] = bot + base[hl:, ls]
 
 
-def gate_kernel(places, info, cown, coth, normed, mixed, gout, *rest):
+def gate_kernel(places, info, cown, coth, normed, mixed, consts, *rest):
     count = len(places)
     pieces = rest[:count]
     gate_o, gno_o, sums_o, w, sem = rest[count:]
     c = pl.program_id(0)
     half = pl.num_programs(0) // 2
-    width = gout.shape[1]
+    width = gate_o.shape[1]
+    gout = vector(consts, GOUT, width)
 
     @pl.when(c == 0)
     def _():
@@ -265,7 +285,7 @@
 
 
 def gate_back_kernel(
-    places, masks, info, cown, coth, normed, mixed, gate, gno, sown, soth, gout, *rest
+    places, masks, info, cown, coth, normed, mixed, gate, gno, sown, soth, consts, *rest
 ):
     count = len(places)
     pieces = rest[:count]
@@ -277,7 +297,8 @@
     c = pl.program_id(0)
     last = pl.num_programs(0) - 1
     half = pl.num_programs(0) // 2
-    width = gout.shape[1]
+    width = gm_o.shape[1]
+    gout = vector(consts, GOUT, width)
 
     @pl.when(c == 0)
     def _():
@@ -328,22 +349,26 @@
 
 
 def scan_back_kernel(
-    masks, places, info, xbc, act_r, dsilu, step, within_r, mixed, sin_r, gm, normed, conv, dtb, rate, dsk,
-    expand, collect, tri_r, ggo, gain_z, *rest,
+    masks, places, info, xbc, act_r, dsilu, step, within_r, mixed, sin_r, gm, normed, consts,
+    tri_r, ggo, gain_z, *rest,
 ):
     count = len(places)
     pieces = rest[:count]
     gx_o, small_o = rest[count : count + 2]
-    gw_o = rest[count + 2 : -8]
-    dstate, dvbuf, acc_w, acc_c, acc_s, acc_h, w, sem = rest[-8:]
+    gw_o = rest[count + 2 : -10]
+    dstate, dvbuf, acc_w, acc_c, acc_s, acc_h, w, expand, collect, sem = rest[-10:]
     i = pl.program_id(0)
     last = pl.num_programs(0) - 1
-    width = dsk.shape[1]
+    width = expand.shape[1]
     heads = width // HEAD
     cols = width + 2 * NS
+    conv, dsk = vector(consts, CONV, cols, 4), vector(consts, DSK, width)
+    dtb, rate = vector(consts, DTB, LANES), vector(consts, RATE, LANES)
 
     @pl.when(i == 0)
     def _():
+        expand[...] = expander(heads)
+        collect[...] = collector(heads)
         load_rows(info, pieces, places, w, sem)
         dstate[...] = jnp.zeros_like(dstate)
         dvbuf[...] = jnp.zeros_like(dvbuf)
@@ -522,11 +547,12 @@
         kept_o[...] = dnb[...]
 
 
-def finish_kernel(resid, cot, gin, dn_own, dn_oth, br_own, br_oth, out_o, gres_o):
+def finish_kernel(resid, cot, consts, dn_own, dn_oth, br_own, br_oth, out_o, gres_o):
     r = resid[...].astype(f32)
     inv = lax.rsqrt(jnp.mean(r * r, axis=1, keepdims=True) + eps)
     out_o[...] = (r + (br_own[...].astype(f32) + br_oth[...].astype(f32))).astype(bf16)
-    u = (dn_own[...].astype(f32) + dn_oth[...].astype(f32)) * gin[...]
+    gin = consts[GIN : GIN + 1, : r.shape[1]]
+    u = (dn_own[...].astype(f32) + dn_oth[...].astype(f32)) * gin
     mean = jnp.mean(u * r, axis=1, keepdims=True)
     gres_o[...] = cot[...].astype(f32) + inv * u - r * (inv * inv * inv * mean)
 
@@ -668,31 +694,39 @@
 
     first = jnp.concatenate([w_x, w_bc, lanes3(w_dt)], axis=1)
     second = jnp.concatenate([w_z, w_out.T], axis=1)
-    conv = jnp.concatenate([conv_x, conv_bc], axis=1)
-    bias = jnp.concatenate([bias_x, bias_bc])[None]
-    dtb = lanes3(dt_bias[None])
-    rate = lanes3(-jnp.exp(a_log)[None])
-    dsk = jnp.repeat(d_skip, HEAD)[None]
-    gin = gain_in[None]
-    gout = gain_out[None]
-    expand = expander(heads)
+    def row(v):
+        return jnp.pad(v, ((0, 0), (0, cols - v.shape[1])))
+
+    consts = jnp.concatenate(
+        [
+            jnp.concatenate([conv_x, conv_bc], axis=1),
+            jnp.concatenate([bias_x, bias_bc])[None],
+            row(gain_in[None]),
+            row(gain_out[None]),
+            row(jnp.repeat(d_skip, HEAD)[None]),
+            row(lanes3(dt_bias[None])),
+            row(lanes3(-jnp.exp(a_log)[None])),
+            jnp.zeros((6, cols), f32),
+        ]
+    )
     if direct(size, rows):
-        cut = first.shape[1]
-        both = jnp.concatenate([first, second], axis=1)
-        both, got, resid_in, cot_in, conv, bias, dtb, rate, dsk, gin, gout, expand = (
-            lax.optimization_barrier(
-                (
-                    both, gather_far(both), resid, cotangent, conv, bias, dtb, rate, dsk, gin,
-                    gout, expand,
-                )
-            )
+        many = jnp.concatenate([first[:, :width], second], axis=1)
+        few = first[:, width:]
+        got_many = gather_far(many)
+        got_few = [swap(few, near, "dp") for near in NEAR[1:]]
+        many, got_many, few, got_few, resid_in, cot_in, consts = lax.optimization_barrier(
+            (many, got_many, few, got_few, resid, cotangent, consts)
         )
-        held = [both] + got
-        wx, wx_at = gather_near(jnp.stack([v[:, :cut] for v in held]))
+        held = [many] + got_many
+        few = jnp.stack([few] + got_few)
+        wx = [few] + [swap(few, far, "dp") for far in FAR[1:]]
+        wx_at = [(width, tuple(near ^ far for near in NEAR)) for far in FAR]
+        near_x, near_at = gather_near(jnp.stack([v[:, :width] for v in held]))
+        wx, wx_at = near_x + wx, near_at + wx_at
         resid_oth = swap(resid_in, 1, "tensor")
         cot_oth = swap(cot_in, 1, "tensor")
         held, resid_oth, cot_oth, wx = lax.optimization_barrier((held, resid_oth, cot_oth, wx))
-        wz, wz_at = gather_near(jnp.stack([v[:, cut:] for v in held]))
+        wz, wz_at = gather_near(jnp.stack([v[:, width:] for v in held]))
     else:
         resid_oth = swap(resid, 1, "tensor")
         cot_oth = swap(cotangent, 1, "tensor")
@@ -700,7 +734,7 @@
         wz, wz_at = whole_pieces(second, bits)
 
     info = jnp.stack([place, lax.axis_index("dp")]).astype(jnp.int32)
-    anywhere = pl.BlockSpec(memory_space=pl.ANY)
+    anywhere = pl.BlockSpec(memory_space=pltpu.HBM)
 
     def copies(at):
         return pltpu.SemaphoreType.DMA((sum(len(masks) for _, masks in at),))
@@ -717,9 +751,7 @@
         52,
         chunks,
         [
-            own_spec, oth_spec, full((1, dim)), full((4, cols)), full((1, cols)),
-            full((1, LANES)), full((1, LANES)), full((1, width)), full((LANES, width)),
-            full((L, L)),
+            own_spec, oth_spec, full((16, cols)), full((L, L)),
         ]
         + [anywhere] * len(wx),
         [
@@ -737,9 +769,10 @@
         ],
         [
             pltpu.VMEM((NS, width), f32), pltpu.VMEM((cols // LANES, L + 8, LANES), f32),
-            pltpu.VMEM((dim, cols + LANES), bf16), copies(wx_at),
+            pltpu.VMEM((dim, cols + LANES), bf16), pltpu.VMEM((LANES, width), bf16),
+            copies(wx_at),
         ],
-        info, resid, resid_oth, gin, conv, bias, dtb, rate, dsk, expand, lower_tri(), *wx,
+        info, resid, resid_oth, consts, lower_tri(), *wx,
     )
 
     steps = tokens // R
@@ -756,13 +789,13 @@
         "gate_forward",
         52,
         steps,
-        [own_r, oth_r, block(dim), block(width), full((1, width))] + [anywhere] * len(wz),
+        [own_r, oth_r, block(dim), block(width), full((16, cols))] + [anywhere] * len(wz),
         [
             (block(width), tok(width, bf16)), (block(width), tok(width, f32)),
             (rows_spec(16, R), sums_shape),
         ],
         [pltpu.VMEM((dim, 2 * width), bf16), copies(wz_at)],
-        info, cotangent, cot_oth, normed, mixed, gout, *wz,
+        info, cotangent, cot_oth, normed, mixed, consts, *wz,
     )
     sums_oth = swap(sums, 1, "tensor")
 
@@ -781,7 +814,7 @@
         steps,
         [
             trail, lead, block(dim, turned), twide, twide, twide,
-            rows_spec(16, R, turned), rows_spec(16, R, turned), full((1, width)),
+            rows_spec(16, R, turned), rows_spec(16, R, turned), full((16, cols)),
         ]
         + [anywhere] * len(wz),
         [
@@ -794,7 +827,7 @@
             pltpu.VMEM((dim, 2 * width), f32), pltpu.VMEM((8, width), f32),
             pltpu.VMEM((dim, 2 * width), bf16), pltpu.VMEM((R, width), bf16), copies(wz_at),
         ],
-        info, cotangent, cot_oth, normed, mixed, gate, gno, sums, sums_oth, gout, *wz,
+        info, cotangent, cot_oth, normed, mixed, gate, gno, sums, sums_oth, consts, *wz,
     )
     branch_oth = swap(branch_sent, 1, "tensor")
     sent_zo = scatter_near(gw_zo) if direct(size, rows) else gw_zo
@@ -814,8 +847,7 @@
         [
             rcols, rcols, rcols, rlanes, rlanes, rwide,
             pl.BlockSpec((1, NS, width), lambda c, info: (chunks - 1 - c, 0, 0)),
-            rwide, rows_spec(L, dim, back), full((4, cols)), full((1, LANES)),
-            full((1, LANES)), full((1, width)), full((LANES, width)), full((width, LANES)),
+            rwide, rows_spec(L, dim, back), full((16, cols)),
             full((L, L)), full((8, width)), full((dim, LANES)),
         ]
         + [anywhere] * len(wx),
@@ -828,10 +860,11 @@
             pltpu.VMEM((NS, width), f32), pltpu.VMEM((cols // LANES, L + 8, LANES), f32),
             pltpu.VMEM((dim, cols + LANES), f32), pltpu.VMEM((5, 8, cols), f32),
             pltpu.VMEM((8, width), f32), pltpu.VMEM((16, LANES), f32),
-            pltpu.VMEM((dim, cols + LANES), bf16), copies(wx_at),
+            pltpu.VMEM((dim, cols + LANES), bf16), pltpu.VMEM((LANES, width), bf16),
+            pltpu.VMEM((width, LANES), bf16), copies(wx_at),
         ],
-        info, xbc, act, dsilu, step_raw, within, mixed, sin, gm, normed, conv, dtb, rate, dsk,
-        expand, collector(heads), upper_tri(), g_gout, g_gin_z, *wx,
+        info, xbc, act, dsilu, step_raw, within, mixed, sin, gm, normed, consts,
+        upper_tri(), g_gout, g_gin_z, *wx,
     )
 
     sent_zo, branch_oth, gx, gw_x, small = lax.optimization_barrier(
@@ -870,10 +903,10 @@
         "finish",
         12,
         half,
-        [dspec, dspec, full((1, dim)), dspec, dspec, dspec, dspec],
+        [dspec, dspec, full((16, cols)), dspec, dspec, dspec, dspec],
         [(dspec, half_shape), (dspec, shape((half_rows, dim), f32))],
         [],
-        info, resid, cotangent, gin, dn_own, dn_oth, branch_own, branch_oth,
+        info, resid, cotangent, consts, dn_own, dn_oth, branch_own, branch_oth,
     )
 
     if direct(size, rows):

time: 234 us -> 229 us (0.979)
  waiting for transfers between devices: 41.5 us -> 30.7 us
  starting transfers between devices: 33.9 us -> 42.3 us
  Pallas kernels: 132 us -> 126 us
    ppermute x27 -> x33, waiting for transfers between devices: 41.5 us -> 30.7 us  [swap(): return lax.ppermute(v, axis, [(i, i ^ bit) for i in range(size)])]
    ppermute x27 -> x33, starting transfers between devices: 33.9 us -> 42.3 us  [swap(): return lax.ppermute(v, axis, [(i, i ^ bit) for i in range(size)])]
    pallas_call x6, Pallas kernels: 132 us -> 126 us  [call(): pl.pallas_call(kernel, grid_spec=pltpu.PrefetchScalarGridSpec(num_scalar_...]
    unnamed x51 -> x66, local copies, waits for them, and re-layouts: 10 us -> 11.1 us
  transfers between devices with their start and end apart: 27 -> 33, of which waited for: 7 -> 12; matrix products, arithmetic and copies ran while one was open for 4% -> 5% of each run, Pallas kernels for 39% -> 37%
where the time goes in v4:
time: 229 us; the launch traced here: 227 us
  Pallas kernels  126 us (55%)
  starting transfers between devices  42.3 us (18%)
  waiting for transfers between devices  30.7 us (13%)
  local copies, waits for them, and re-layouts  20.4 us (9%)
  other arithmetic  6.36 us (3%)
    pallas_call x6, Pallas kernels, call(): pl.pallas_call(kernel, grid_spec=pltpu.PrefetchScalarGridSpec(num_scalar_...  126 us
    ppermute x33, starting transfers between devices, swap(): return lax.ppermute(v, axis, [(i, i ^ bit) for i in range(size)])  42.3 us
    ppermute x33, waiting for transfers between devices, swap(): return lax.ppermute(v, axis, [(i, i ^ bit) for i in range(size)])  30.7 us
    unnamed x66, local copies, waits for them, and re-layouts  11.1 us
  transfers between devices with their start and end apart: 33, of which 12 were waited for; matrix products, arithmetic and copies ran while one was open for 5% of the time, Pallas kernels for 37%

profile of v4, /device:TPU:0, one launch (start us, length us, event | category | flops | bytes accessed | tf_op | source)
XLA Modules:
  0.0 227.1 jit_solution(17736094184871057472)
XLA Ops:
  1.6 3.1 %collective-permute-start = (bf16[48,2304]{1,0:T(8,128)(2,1)S(1)}, bf16[48,2304]{1,0:T(8,128)(2,1)S(1)}, u32[]{:S(2)}, u32[]{:S(2)}) collective-permute-start(bf16[48,2304]{1,0:T(8,128)(2,1)S(1)} %pad_maximum_fusion.9), channel_id=1, source_target_pairs={{0,8},{2,10},{4,12},{6,14},{8,0},{10,2},{12,4},{14,6},{16,24},{18,... | collective-permute-start | bytes 663560 | tf_op jit(solution)/shard_map/ppermute | solution.py:562
  4.7 2.6 %collective-permute-start.1 = (bf16[48,2304]{1,0:T(8,128)(2,1)S(1)}, bf16[48,2304]{1,0:T(8,128)(2,1)S(1)}, u32[]{:S(2)}, u32[]{:S(2)}) collective-permute-start(bf16[48,2304]{1,0:T(8,128)(2,1)S(1)} %pad_maximum_fusion.9), channel_id=1, source_target_pairs={{0,16},{2,18},{4,20},{6,22},{8,24},{10,26},{12,28},{14,30},{16,0},... | collective-permute-start | bytes 663560 | tf_op jit(solution)/shard_map/ppermute | solution.py:562
  8.9 1.7 collective-permute-start.3
  10.6 1.5 collective-permute-start.4
  19.9 3.6 %collective-permute-done.1 = bf16[48,2304]{1,0:T(8,128)(2,1)S(1)} collective-permute-done((bf16[48,2304]{1,0:T(8,128)(2,1)S(1)}, bf16[48,2304]{1,0:T(8,128)(2,1)S(1)}, u32[]{:S(2)}, u32[]{:S(2)}) %collective-permute-start.1) | collective-permute-done | bytes 221216 | tf_op jit(solution)/shard_map/ppermute | solution.py:562
  24.0 3.9 %collective-permute-start.11 = (bf16[4,48,384]{2,1,0:T(8,128)(2,1)S(1)}, bf16[4,48,384]{2,1,0:T(8,128)(2,1)S(1)}, u32[]{:S(2)}, u32[]{:S(2)}) collective-permute-start(bf16[4,48,384]{2,1,0:T(8,128)(2,1)S(1)} %pad_maximum_fusion.10.rest_4_.rest_8_), channel_id=1, source_target_pairs={{0,8},{2,10},{4,12},{6,14},{8,0},{10,2},{12,4},{14,6},{16,24},{18,... | collective-permute-start | bytes 442376 | tf_op jit(solution)/shard_map/ppermute | solution.py:562
  29.0 1.4 collective-permute-start.13
  30.5 3.7 %collective-permute-done.11.rest_5_.rest_9_ = bf16[4,48,384]{2,1,0:T(8,128)(2,1)S(1)} collective-permute-done((bf16[4,48,384]{2,1,0:T(8,128)(2,1)S(1)}, bf16[4,48,384]{2,1,0:T(8,128)(2,1)S(1)}, u32[]{:S(2)}, u32[]{:S(2)}) %collective-permute-start.11) | collective-permute-done | bytes 147488 | tf_op jit(solution)/shard_map/ppermute | solution.py:562
  34.2 2.4 %collective-permute-start.10 = (bf16[4,48,768]{2,1,0:T(8,128)(2,1)S(1)}, bf16[4,48,768]{2,1,0:T(8,128)(2,1)S(1)}, u32[]{:S(2)}, u32[]{:S(2)}) collective-permute-start(bf16[4,48,768]{2,1,0:T(8,128)(2,1)S(1)} %pad_maximum_fusion.1.rest_0_.rest_4_), channel_id=1, source_target_pairs={{0,6},{2,4},{4,2},{6,0},{8,14},{10,12},{12,10},{14,8},{16,22},{18,... | collective-permute-start | bytes 884744 | tf_op jit(solution)/shard_map/ppermute | solution.py:562
  36.6 5.3 %collective-permute-done.12.rest_6_.rest_10_ = bf16[4,48,384]{2,1,0:T(8,128)(2,1)S(1)} collective-permute-done((bf16[4,48,384]{2,1,0:T(8,128)(2,1)S(1)}, bf16[4,48,384]{2,1,0:T(8,128)(2,1)S(1)}, u32[]{:S(2)}, u32[]{:S(2)}) %collective-permute-start.12) | collective-permute-done | bytes 147488 | tf_op jit(solution)/shard_map/ppermute | solution.py:562
  41.9 1.5 collective-permute-start.8
  43.4 1.5 collective-permute-start.9
  45.0 4.6 %collective-permute-done.8.rest_1_.rest_5_ = bf16[4,48,768]{2,1,0:T(8,128)(2,1)S(1)} collective-permute-done((bf16[4,48,768]{2,1,0:T(8,128)(2,1)S(1)}, bf16[4,48,768]{2,1,0:T(8,128)(2,1)S(1)}, u32[]{:S(2)}, u32[]{:S(2)}) %collective-permute-start.8) | collective-permute-done | bytes 294944 | tf_op jit(solution)/shard_map/ppermute | solution.py:562
  51.4 1.4 collective-permute-start.14
  52.8 1.5 collective-permute-start.15
  59.6 27.9 %mix_forward.1 = (bf16[2048,768]{1,0:T(8,128)(2,1)}, bf16[2048,1024]{1,0:T(8,128)(2,1)}, bf16[2048,1024]{1,0:T(8,128)(2,1)}, bf16[2048,1024]{1,0:T(8,128)(2,1)},...) custom-call(s32[2]{0:T(128)S(1)} %pad_add_fusion.info, ...), custom_call_target="tpu_custom_call" | custom-call | tf_op jit(solution)/shard_map/mix_forward/pallas_call | solution.py:656
  88.4 15.7 %gate_forward.1 = (bf16[2048,768]{1,0:T(8,128)(2,1)}, f32[2048,768]{1,0:T(8,128)}, f32[64,512]{1,0:T(8,128)S(1)}) custom-call(s32[2]{0:T(128)S(1)} %pad_add_fusion.info, bf16[1024,768]{1,0:T(8,128)(2,1)} %refs_1_.1, bf16[1024,768]{1,0:T(8,128)(2,1)} %copy-done.27, bf16[2048,768]{1,0:T(8,128)(2,1)} %get-tuple-element.120.normed, ...), custom_call_target="tpu_custom_call" | custom-call | tf_op jit(solution)/shard_map/gate_forward/pallas_call | solution.py:656
  104.2 1.3 collective-permute-done.17.soth
  105.6 25.8 %gate_backward.1 = (bf16[1024,768]{1,0:T(8,128)(2,1)}, bf16[1024,768]{1,0:T(8,128)(2,1)}, bf16[2048,768]{1,0:T(8,128)(2,1)}, bf16[2048,768]{1,0:T(8,128)(2,1)}, ...) custom-call(s32[2]{0:T(128)S(1)} %pad_add_fusion.info, ...), custom_call_target="tpu_custom_call" | custom-call | tf_op jit(solution)/shard_map/gate_backward/pallas_call | solution.py:656
  133.6 1.5 collective-permute-start.19
  135.8 43.2 %mix_backward.1 = (bf16[2048,1152]{1,0:T(8,128)(2,1)}, f32[8,1152]{1,0:T(8,128)}, bf16[208,1152]{1,0:T(8,128)(2,1)}, bf16[208,1152]{1,0:T(8,128)(2,1)}, bf16[208...) custom-call(s32[2]{0:T(128)S(1)} %pad_add_fusion.info, bf16[2048,1024]{1,0:T(8,128)(2,1)} %get-tuple-element.134.xbc, ...), custom_call_target="tpu_custom_call" | custom-call | tf_op jit(solution)/shard_map/mix_backward/pallas_call | solution.py:656
  179.1 1.4 collective-permute-start.25
  180.4 1.5 collective-permute-start.26
  183.0 2.1 collective-permute-start.22
  186.4 2.3 %copy-done.10 = bf16[2048,1152]{1,0:T(8,128)(2,1)S(1)} copy-done((bf16[2048,1152]{1,0:T(8,128)(2,1)S(1)}, bf16[2048,1152]{1,0:T(8,128)(2,1)}, u32[]{:S(2)}) %copy-start.10) | copy-done | bytes 4718616
  188.7 9.4 %input_backward.1 = (bf16[1024,768]{1,0:T(8,128)(2,1)S(1)}, bf16[1024,768]{1,0:T(8,128)(2,1)S(1)}) custom-call(s32[2]{0:T(128)S(1)} %pad_add_fusion.info, bf16[2048,768]{1,0:T(8,128)(2,1)S(1)} %copy-done.11, bf16[2048,1152]{1,0:T(8,128)(2,1)S(1)} %copy-done.10, bf16[4,48,1536]{2,1,0:T(8,128)(2,1)S(1)} %copy-done.2, bf16[4,48,1536]{2,1,0:T(8,128)(2,1)S(1)} %copy-done.5, ...), custom_call_target="tpu_custom_call" | custom-call | tf_op jit(solution)/shard_map/input_backward/pallas_call | solution.py:656
  198.1 1.5 collective-permute-start.24
  199.6 2.7 %collective-permute-done.26 = bf16[208,1152]{1,0:T(8,128)(2,1)S(1)} collective-permute-done((bf16[208,1152]{1,0:T(8,128)(2,1)}, bf16[208,1152]{1,0:T(8,128)(2,1)S(1)}, u32[]{:S(2)}, u32[]{:S(2)}) %collective-permute-start.26) | collective-permute-done | bytes 479264 | tf_op jit(solution)/shard_map/ppermute | solution.py:562
  203.5 2.3 %collective-permute-start.29 = (bf16[64,1152]{1,0:T(8,128)(2,1)S(1)}, bf16[64,1152]{1,0:T(8,128)(2,1)S(1)}, u32[]{:S(2)}, u32[]{:S(2)}) collective-permute-start(bf16[64,1152]{1,0:T(8,128)(2,1)S(1)} %get-tuple-element.221), channel_id=1, source_target_pairs={{0,8},{2,10},{4,12},{6,14},{8,0},{10,2},{12,4},{14,6},{16,24},{18,... | collective-permute-start | bytes 442376 | tf_op jit(solution)/shard_map/ppermute | solution.py:562
  207.0 1.4 collective-permute-start.31
  208.6 3.9 %finish.1 = (bf16[1024,768]{1,0:T(8,128)(2,1)}, f32[1024,768]{1,0:T(8,128)}) custom-call(s32[2]{0:T(128)S(1)} %pad_add_fusion.info, bf16[1024,768]{1,0:T(8,128)(2,1)S(1)} %copy-done.3, bf16[1024,768]{1,0:T(8,128)(2,1)S(1)} %copy-done, f32[16,1024]{1,0:T(8,128)S(1)} %copy-done.12, bf16[1024,768]{1,0:T(8,128)(2,1)S(1)} %get-tuple-element.162.refs_3_, ...), custom_call_target="tpu_custom_call" | custom-call | tf_op jit(solution)/shard_map/finish/pallas_call | solution.py:656
  213.1 6.7 %collective-permute-done.30 = bf16[64,1152]{1,0:T(8,128)(2,1)S(1)} collective-permute-done((bf16[64,1152]{1,0:T(8,128)(2,1)S(1)}, bf16[64,1152]{1,0:T(8,128)(2,1)S(1)}, u32[]{:S(2)}, u32[]{:S(2)}) %collective-permute-start.30) | collective-permute-done | bytes 147488 | tf_op jit(solution)/shard_map/ppermute | solution.py:562
  (171 shorter events, 35.4 us)
Async XLA Ops:
  1.6 18.3 %collective-permute-start = (bf16[48,2304]{1,0:T(8,128)(2,1)S(1)}, bf16[48,2304]{1,0:T(8,128)(2,1)S(1)}, u32[]{:S(2)}, u32[]{:S(2)}) collective-permute-start(bf16[48,2304]{1,0:T(8,128)(2,1)S(1)} %pad_maximum_fusion.9), channel_id=1, source_target_pairs={{0,8},{2,10},{4,12},{6,14},{8,0},{10,2},{12,4},{14,6},{16,24},{18,... | collective-permute-start | bytes 663560 | tf_op jit(solution)/shard_map/ppermute | solution.py:562
  4.7 18.7 %collective-permute-start.1 = (bf16[48,2304]{1,0:T(8,128)(2,1)S(1)}, bf16[48,2304]{1,0:T(8,128)(2,1)S(1)}, u32[]{:S(2)}, u32[]{:S(2)}) collective-permute-start(bf16[48,2304]{1,0:T(8,128)(2,1)S(1)} %pad_maximum_fusion.9), channel_id=1, source_target_pairs={{0,16},{2,18},{4,20},{6,22},{8,24},{10,26},{12,28},{14,30},{16,0},... | collective-permute-start | bytes 663560 | tf_op jit(solution)/shard_map/ppermute | solution.py:562
  7.3 16.1 %collective-permute-start.2 = (bf16[48,2304]{1,0:T(8,128)(2,1)S(1)}, bf16[48,2304]{1,0:T(8,128)(2,1)S(1)}, u32[]{:S(2)}, u32[]{:S(2)}) collective-permute-start(bf16[48,2304]{1,0:T(8,128)(2,1)S(1)} %pad_maximum_fusion.9), channel_id=1, source_target_pairs={{0,24},{2,26},{4,28},{6,30},{8,16},{10,18},{12,20},{14,22},{16,8},... | collective-permute-start | bytes 663560 | tf_op jit(solution)/shard_map/ppermute | solution.py:562
  8.9 6.1 %collective-permute-start.3 = (bf16[48,384]{1,0:T(8,128)(2,1)S(1)}, bf16[48,384]{1,0:T(8,128)(2,1)S(1)}, u32[]{:S(2)}, u32[]{:S(2)}) collective-permute-start(bf16[48,384]{1,0:T(8,128)(2,1)S(1)} %pad_maximum_fusion.12), channel_id=1, source_target_pairs={{0,2},{2,0},{4,6},{6,4},{8,10},{10,8},{12,14},{14,12},{16,18},{18,... | collective-permute-start | bytes 110600 | tf_op jit(solution)/shard_map/ppermute | solution.py:562
  10.6 8.5 %collective-permute-start.4 = (bf16[48,384]{1,0:T(8,128)(2,1)S(1)}, bf16[48,384]{1,0:T(8,128)(2,1)S(1)}, u32[]{:S(2)}, u32[]{:S(2)}) collective-permute-start(bf16[48,384]{1,0:T(8,128)(2,1)S(1)} %pad_maximum_fusion.12), channel_id=1, source_target_pairs={{0,4},{2,6},{4,0},{6,2},{8,12},{10,14},{12,8},{14,10},{16,20},{18,... | collective-permute-start | bytes 110600 | tf_op jit(solution)/shard_map/ppermute | solution.py:562
  15.0 4.9 %collective-permute-start.5 = (bf16[48,384]{1,0:T(8,128)(2,1)S(1)}, bf16[48,384]{1,0:T(8,128)(2,1)S(1)}, u32[]{:S(2)}, u32[]{:S(2)}) collective-permute-start(bf16[48,384]{1,0:T(8,128)(2,1)S(1)} %pad_maximum_fusion.12), channel_id=1, source_target_pairs={{0,6},{2,4},{4,2},{6,0},{8,14},{10,12},{12,10},{14,8},{16,22},{18,... | collective-permute-start | bytes 110600 | tf_op jit(solution)/shard_map/ppermute | solution.py:562
  23.5 26.7 %collective-permute-start.6 = (bf16[1024,768]{1,0:T(8,128)(2,1)}, bf16[1024,768]{1,0:T(8,128)(2,1)S(1)}, u32[]{:S(2)}, u32[]{:S(2)}) collective-permute-start(bf16[1024,768]{1,0:T(8,128)(2,1)} %refs_0_.1), channel_id=1, source_target_pairs={{0,1},{1,0},{2,3},{3,2},{4,5},{5,4},{6,7},{7,6},{8,9},{9,8},{10,11... | collective-permute-start | bytes 4718600 | tf_op jit(solution)/shard_map/ppermute | solution.py:562
  23.5 26.7 %collective-permute-start.7 = (bf16[1024,768]{1,0:T(8,128)(2,1)}, bf16[1024,768]{1,0:T(8,128)(2,1)S(1)}, u32[]{:S(2)}, u32[]{:S(2)}) collective-permute-start(bf16[1024,768]{1,0:T(8,128)(2,1)} %refs_1_.1), channel_id=1, source_target_pairs={{0,1},{1,0},{2,3},{3,2},{4,5},{5,4},{6,7},{7,6},{8,9},{9,8},{10,11... | collective-permute-start | bytes 4718600 | tf_op jit(solution)/shard_map/ppermute | solution.py:562
  24.0 10.2 %collective-permute-start.11 = (bf16[4,48,384]{2,1,0:T(8,128)(2,1)S(1)}, bf16[4,48,384]{2,1,0:T(8,128)(2,1)S(1)}, u32[]{:S(2)}, u32[]{:S(2)}) collective-permute-start(bf16[4,48,384]{2,1,0:T(8,128)(2,1)S(1)} %pad_maximum_fusion.10.rest_4_.rest_8_), channel_id=1, source_target_pairs={{0,8},{2,10},{4,12},{6,14},{8,0},{10,2},{12,4},{14,6},{16,24},{18,... | collective-permute-start | bytes 442376 | tf_op jit(solution)/shard_map/ppermute | solution.py:562
  27.9 14.0 %collective-permute-start.12 = (bf16[4,48,384]{2,1,0:T(8,128)(2,1)S(1)}, bf16[4,48,384]{2,1,0:T(8,128)(2,1)S(1)}, u32[]{:S(2)}, u32[]{:S(2)}) collective-permute-start(bf16[4,48,384]{2,1,0:T(8,128)(2,1)S(1)} %pad_maximum_fusion.10.rest_4_.rest_8_), channel_id=1, source_target_pairs={{0,16},{2,18},{4,20},{6,22},{8,24},{10,26},{12,28},{14,30},{16,0},... | collective-permute-start | bytes 442376 | tf_op jit(solution)/shard_map/ppermute | solution.py:562
  29.0 14.4 %collective-permute-start.13 = (bf16[4,48,384]{2,1,0:T(8,128)(2,1)S(1)}, bf16[4,48,384]{2,1,0:T(8,128)(2,1)S(1)}, u32[]{:S(2)}, u32[]{:S(2)}) collective-permute-start(bf16[4,48,384]{2,1,0:T(8,128)(2,1)S(1)} %pad_maximum_fusion.10.rest_4_.rest_8_), channel_id=1, source_target_pairs={{0,24},{2,26},{4,28},{6,30},{8,16},{10,18},{12,20},{14,22},{16,8},... | collective-permute-start | bytes 442376 | tf_op jit(solution)/shard_map/ppermute | solution.py:562
  34.2 10.8 %collective-permute-start.10 = (bf16[4,48,768]{2,1,0:T(8,128)(2,1)S(1)}, bf16[4,48,768]{2,1,0:T(8,128)(2,1)S(1)}, u32[]{:S(2)}, u32[]{:S(2)}) collective-permute-start(bf16[4,48,768]{2,1,0:T(8,128)(2,1)S(1)} %pad_maximum_fusion.1.rest_0_.rest_4_), channel_id=1, source_target_pairs={{0,6},{2,4},{4,2},{6,0},{8,14},{10,12},{12,10},{14,8},{16,22},{18,... | collective-permute-start | bytes 884744 | tf_op jit(solution)/shard_map/ppermute | solution.py:562
  41.9 7.7 %collective-permute-start.8 = (bf16[4,48,768]{2,1,0:T(8,128)(2,1)S(1)}, bf16[4,48,768]{2,1,0:T(8,128)(2,1)S(1)}, u32[]{:S(2)}, u32[]{:S(2)}) collective-permute-start(bf16[4,48,768]{2,1,0:T(8,128)(2,1)S(1)} %pad_maximum_fusion.1.rest_0_.rest_4_), channel_id=1, source_target_pairs={{0,2},{2,0},{4,6},{6,4},{8,10},{10,8},{12,14},{14,12},{16,18},{18,... | collective-permute-start | bytes 884744 | tf_op jit(solution)/shard_map/ppermute | solution.py:562
  43.4 6.7 %collective-permute-start.9 = (bf16[4,48,768]{2,1,0:T(8,128)(2,1)S(1)}, bf16[4,48,768]{2,1,0:T(8,128)(2,1)S(1)}, u32[]{:S(2)}, u32[]{:S(2)}) collective-permute-start(bf16[4,48,768]{2,1,0:T(8,128)(2,1)S(1)} %pad_maximum_fusion.1.rest_0_.rest_4_), channel_id=1, source_target_pairs={{0,4},{2,6},{4,0},{6,2},{8,12},{10,14},{12,8},{14,10},{16,20},{18,... | collective-permute-start | bytes 884744 | tf_op jit(solution)/shard_map/ppermute | solution.py:562
  51.4 36.0 %collective-permute-start.14 = (bf16[4,48,1536]{2,1,0:T(8,128)(2,1)S(1)}, bf16[4,48,1536]{2,1,0:T(8,128)(2,1)S(1)}, u32[]{:S(2)}, u32[]{:S(2)}) collective-permute-start(bf16[4,48,1536]{2,1,0:T(8,128)(2,1)S(1)} %pad_maximum_fusion.rest_0_), channel_id=1, source_target_pairs={{0,2},{2,0},{4,6},{6,4},{8,10},{10,8},{12,14},{14,12},{16,18},{18,... | collective-permute-start | bytes 1769480 | tf_op jit(solution)/shard_map/ppermute | solution.py:562
  52.8 34.7 %collective-permute-start.15 = (bf16[4,48,1536]{2,1,0:T(8,128)(2,1)S(1)}, bf16[4,48,1536]{2,1,0:T(8,128)(2,1)S(1)}, u32[]{:S(2)}, u32[]{:S(2)}) collective-permute-start(bf16[4,48,1536]{2,1,0:T(8,128)(2,1)S(1)} %pad_maximum_fusion.rest_0_), channel_id=1, source_target_pairs={{0,4},{2,6},{4,0},{6,2},{8,12},{10,14},{12,8},{14,10},{16,20},{18,... | collective-permute-start | bytes 1769480 | tf_op jit(solution)/shard_map/ppermute | solution.py:562
  54.3 33.2 %collective-permute-start.16 = (bf16[4,48,1536]{2,1,0:T(8,128)(2,1)S(1)}, bf16[4,48,1536]{2,1,0:T(8,128)(2,1)S(1)}, u32[]{:S(2)}, u32[]{:S(2)}) collective-permute-start(bf16[4,48,1536]{2,1,0:T(8,128)(2,1)S(1)} %pad_maximum_fusion.rest_0_), channel_id=1, source_target_pairs={{0,6},{2,4},{4,2},{6,0},{8,14},{10,12},{12,10},{14,8},{16,22},{18,... | collective-permute-start | bytes 1769480 | tf_op jit(solution)/shard_map/ppermute | solution.py:562
  132.2 46.9 %collective-permute-start.21 = (bf16[1024,768]{1,0:T(8,128)(2,1)}, bf16[1024,768]{1,0:T(8,128)(2,1)S(1)}, u32[]{:S(2)}, u32[]{:S(2)}) collective-permute-start(bf16[1024,768]{1,0:T(8,128)(2,1)} %get-tuple-element.133), channel_id=1, source_target_pairs={{0,1},{1,0},{2,3},{3,2},{4,5},{5,4},{6,7},{7,6},{8,9},{9,8},{10,11... | collective-permute-start | bytes 4718600 | tf_op jit(solution)/shard_map/ppermute | solution.py:562
  132.3 46.8 %collective-permute-start.18 = (bf16[192,1536]{1,0:T(8,128)(2,1)S(1)}, bf16[192,1536]{1,0:T(8,128)(2,1)S(1)}, u32[]{:S(2)}, u32[]{:S(2)}) collective-permute-start(bf16[192,1536]{1,0:T(8,128)(2,1)S(1)} %get-tuple-element.130), channel_id=1, source_target_pairs={{0,2},{2,0},{4,6},{6,4},{8,10},{10,8},{12,14},{14,12},{16,18},{18,... | collective-permute-start | bytes 1769480 | tf_op jit(solution)/shard_map/ppermute | solution.py:562
  133.6 45.5 %collective-permute-start.19 = (bf16[192,1536]{1,0:T(8,128)(2,1)}, bf16[192,1536]{1,0:T(8,128)(2,1)S(1)}, u32[]{:S(2)}, u32[]{:S(2)}) collective-permute-start(bf16[192,1536]{1,0:T(8,128)(2,1)} %get-tuple-element.131), channel_id=1, source_target_pairs={{0,4},{2,6},{4,0},{6,2},{8,12},{10,14},{12,8},{14,10},{16,20},{18,... | collective-permute-start | bytes 1769480 | tf_op jit(solution)/shard_map/ppermute | solution.py:562
  135.1 44.0 %collective-permute-start.20 = (bf16[192,1536]{1,0:T(8,128)(2,1)}, bf16[192,1536]{1,0:T(8,128)(2,1)S(1)}, u32[]{:S(2)}, u32[]{:S(2)}) collective-permute-start(bf16[192,1536]{1,0:T(8,128)(2,1)} %get-tuple-element.132), channel_id=1, source_target_pairs={{0,6},{2,4},{4,2},{6,0},{8,14},{10,12},{12,10},{14,8},{16,22},{18,... | collective-permute-start | bytes 1769480 | tf_op jit(solution)/shard_map/ppermute | solution.py:562
  179.1 19.0 %collective-permute-start.25 = (bf16[208,1152]{1,0:T(8,128)(2,1)}, bf16[208,1152]{1,0:T(8,128)(2,1)S(1)}, u32[]{:S(2)}, u32[]{:S(2)}) collective-permute-start(bf16[208,1152]{1,0:T(8,128)(2,1)} %get-tuple-element.153), channel_id=1, source_target_pairs={{0,2},{2,0},{4,6},{6,4},{8,10},{10,8},{12,14},{14,12},{16,18},{18,... | collective-permute-start | bytes 1437704 | tf_op jit(solution)/shard_map/ppermute | solution.py:562
  180.4 21.8 %collective-permute-start.26 = (bf16[208,1152]{1,0:T(8,128)(2,1)}, bf16[208,1152]{1,0:T(8,128)(2,1)S(1)}, u32[]{:S(2)}, u32[]{:S(2)}) collective-permute-start(bf16[208,1152]{1,0:T(8,128)(2,1)} %get-tuple-element.154), channel_id=1, source_target_pairs={{0,4},{2,6},{4,0},{6,2},{8,12},{10,14},{12,8},{14,10},{16,20},{18,... | collective-permute-start | bytes 1437704 | tf_op jit(solution)/shard_map/ppermute | solution.py:562
  181.9 21.2 %collective-permute-start.27 = (bf16[208,1152]{1,0:T(8,128)(2,1)}, bf16[208,1152]{1,0:T(8,128)(2,1)S(1)}, u32[]{:S(2)}, u32[]{:S(2)}) collective-permute-start(bf16[208,1152]{1,0:T(8,128)(2,1)} %get-tuple-element.155), channel_id=1, source_target_pairs={{0,6},{2,4},{4,2},{6,0},{8,14},{10,12},{12,10},{14,8},{16,22},{18,... | collective-permute-start | bytes 1437704 | tf_op jit(solution)/shard_map/ppermute | solution.py:562
  183.0 22.9 %collective-permute-start.22 = (bf16[48,1536]{1,0:T(8,128)(2,1)S(1)}, bf16[48,1536]{1,0:T(8,128)(2,1)S(1)}, u32[]{:S(2)}, u32[]{:S(2)}) collective-permute-start(bf16[48,1536]{1,0:T(8,128)(2,1)S(1)} %get-tuple-element.212), channel_id=1, source_target_pairs={{0,8},{2,10},{4,12},{6,14},{8,0},{10,2},{12,4},{14,6},{16,24},{18,... | collective-permute-start | bytes 442376 | tf_op jit(solution)/shard_map/ppermute | solution.py:562
  185.1 21.9 %collective-permute-start.23 = (bf16[48,1536]{1,0:T(8,128)(2,1)S(1)}, bf16[48,1536]{1,0:T(8,128)(2,1)S(1)}, u32[]{:S(2)}, u32[]{:S(2)}) collective-permute-start(bf16[48,1536]{1,0:T(8,128)(2,1)S(1)} %get-tuple-element.211), channel_id=1, source_target_pairs={{0,16},{2,18},{4,20},{6,22},{8,24},{10,26},{12,28},{14,30},{16,0},... | collective-permute-start | bytes 442376 | tf_op jit(solution)/shard_map/ppermute | solution.py:562
  198.1 10.4 %collective-permute-start.24 = (bf16[48,1536]{1,0:T(8,128)(2,1)S(1)}, bf16[48,1536]{1,0:T(8,128)(2,1)S(1)}, u32[]{:S(2)}, u32[]{:S(2)}) collective-permute-start(bf16[48,1536]{1,0:T(8,128)(2,1)S(1)} %get-tuple-element.210), channel_id=1, source_target_pairs={{0,24},{2,26},{4,28},{6,30},{8,16},{10,18},{12,20},{14,22},{16,8},... | collective-permute-start | bytes 442376 | tf_op jit(solution)/shard_map/ppermute | solution.py:562
  203.1 5.4 %collective-permute-start.28 = (bf16[1024,768]{1,0:T(8,128)(2,1)S(1)}, bf16[1024,768]{1,0:T(8,128)(2,1)S(1)}, u32[]{:S(2)}, u32[]{:S(2)}) collective-permute-start(bf16[1024,768]{1,0:T(8,128)(2,1)S(1)} %get-tuple-element.160), channel_id=1, source_target_pairs={{0,1},{1,0},{2,3},{3,2},{4,5},{5,4},{6,7},{7,6},{8,9},{9,8},{10,11... | collective-permute-start | bytes 4718600 | tf_op jit(solution)/shard_map/ppermute | solution.py:562
  203.5 9.6 %collective-permute-start.29 = (bf16[64,1152]{1,0:T(8,128)(2,1)S(1)}, bf16[64,1152]{1,0:T(8,128)(2,1)S(1)}, u32[]{:S(2)}, u32[]{:S(2)}) collective-permute-start(bf16[64,1152]{1,0:T(8,128)(2,1)S(1)} %get-tuple-element.221), channel_id=1, source_target_pairs={{0,8},{2,10},{4,12},{6,14},{8,0},{10,2},{12,4},{14,6},{16,24},{18,... | collective-permute-start | bytes 442376 | tf_op jit(solution)/shard_map/ppermute | solution.py:562
  205.9 14.0 %collective-permute-start.30 = (bf16[64,1152]{1,0:T(8,128)(2,1)S(1)}, bf16[64,1152]{1,0:T(8,128)(2,1)S(1)}, u32[]{:S(2)}, u32[]{:S(2)}) collective-permute-start(bf16[64,1152]{1,0:T(8,128)(2,1)S(1)} %get-tuple-element.222), channel_id=1, source_target_pairs={{0,16},{2,18},{4,20},{6,22},{8,24},{10,26},{12,28},{14,30},{16,0},... | collective-permute-start | bytes 442376 | tf_op jit(solution)/shard_map/ppermute | solution.py:562
  207.0 12.8 %collective-permute-start.31 = (bf16[64,1152]{1,0:T(8,128)(2,1)S(1)}, bf16[64,1152]{1,0:T(8,128)(2,1)S(1)}, u32[]{:S(2)}, u32[]{:S(2)}) collective-permute-start(bf16[64,1152]{1,0:T(8,128)(2,1)S(1)} %get-tuple-element.220), channel_id=1, source_target_pairs={{0,24},{2,26},{4,28},{6,30},{8,16},{10,18},{12,20},{14,22},{16,8},... | collective-permute-start | bytes 442376 | tf_op jit(solution)/shard_map/ppermute | solution.py:562
  221.4 3.3 %collective-permute-start.32 = (f32[14336]{0:T(1024)S(1)}, f32[14336]{0:T(1024)S(1)}, u32[]{:S(2)}, u32[]{:S(2)}) collective-permute-start(f32[14336]{0:T(1024)S(1)} %pad_maximum_fusion.11), channel_id=1, source_target_pairs={{0,1},{1,0},{2,3},{3,2},{4,5},{5,4},{6,7},{7,6},{8,9},{9,8},{10,11... | collective-permute-start | bytes 172040 | tf_op jit(solution)/shard_map/ppermute | solution.py:562
  (32 other events, 314.7 us)

commit v5 on v4

--- a/solution.py
+++ b/solution.py
@@ -290,59 +290,70 @@
     count = len(places)
     pieces = rest[:count]
     rest = rest[count:]
-    parts = len(rest) - 11
+    parts = len(rest) - 14
     (sent_o, kept_o, ggate_o, gm_o, ggo_o, gain_o) = rest[:6]
     gw_o = rest[6 : 6 + parts]
-    acc, acc_g, w, nout, sem = rest[6 + parts :]
+    acc, acc_g, w, nout, gates, normed_t, cot_t, sem = rest[6 + parts :]
     c = pl.program_id(0)
     last = pl.num_programs(0) - 1
     half = pl.num_programs(0) // 2
     width = gm_o.shape[1]
     gout = vector(consts, GOUT, width)
+    dim = acc.shape[0]
 
     @pl.when(c == 0)
     def _():
         load_rows(info, pieces, places, w, sem)
-        acc[...] = jnp.zeros_like(acc)
-        acc_g[...] = jnp.zeros_like(acc_g)
-
-    cot = jnp.where(c < half, coth[...].astype(f32), cown[...].astype(f32)).astype(bf16)
+        for ref in (acc, acc_g, nout, gates, normed_t, cot_t):
+            ref[...] = jnp.zeros_like(ref)
+
+    now = c % 2
+    before = 1 - now
+    cot = jnp.where(c < half, coth[...].astype(f32), cown[...].astype(f32))
     inner_total = 2.0 * width
     s = sown[...] + soth[...]
     scale_r = lax.rsqrt(s[0:1] / inner_total + eps)
     coef_r = scale_r * scale_r * scale_r * (s[8:9] / inner_total)
-    scale = jnp.broadcast_to(scale_r, (LANES, R)).T
-    coef = jnp.broadcast_to(coef_r, (LANES, R)).T
-    for at in range(0, width, LANES):
-        ps = slice(at, at + LANES)
-        gain = gout[:, ps]
-        gf = gate[:, ps].astype(f32)
-        sig = sigmoid(gf)
-        silu = gf * sig
-        mix = mixed[:, ps]
-        gated = mix * silu
-        grad = gno[:, ps]
-        unit = gated * scale
-        nout[:, ps] = (unit * gain).astype(bf16)
-        acc_g[:, ps] += fold8(grad * unit)
-        grad_gated = scale * (grad * gain) - gated * coef
-        ggate_o[:, ps] = (grad_gated * mix * (sig + silu * (1.0 - sig))).astype(bf16)
-        gm_o[:, ps] = (grad_gated * silu).astype(bf16)
-    branch = mm(nout[...], w[:, width:], NT).astype(bf16)
+    scale = jnp.broadcast_to(scale_r, (LANES, L)).T
+    coef = jnp.broadcast_to(coef_r, (LANES, L)).T
+    branch = jnp.zeros((L, dim), f32)
+    for at in range(0, width, 2 * LANES):
+        ws = slice(at, at + 2 * LANES)
+        acc[:, ws] += mm(normed_t[before], gates[before, :, ws])
+        for ps in (slice(at, at + LANES), slice(at + LANES, at + 2 * LANES)):
+            gain = gout[:, ps]
+            gf = gate[:, ps].astype(f32)
+            sig = jax.nn.sigmoid(gf)
+            silu = gf * sig
+            mix = mixed[:, ps]
+            gated = mix * silu
+            grad = gno[:, ps].astype(f32)
+            unit = gated * scale
+            nout[now, :, ps] = (unit * gain).astype(bf16)
+            acc_g[:, ps] += fold8(grad * unit)
+            grad_gated = scale * (grad * gain) - gated * coef
+            grad_gate = (grad_gated * mix * (sig + silu * (1.0 - sig))).astype(bf16)
+            gates[now, :, ps] = grad_gate
+            ggate_o[:, ps] = grad_gate
+            gm_o[:, ps] = (grad_gated * silu).astype(bf16)
+        acc[:, width + at : width + at + 2 * LANES] += mm(cot_t[before], nout[before, :, ws])
+        branch += mm(nout[now, :, ws], w[:, width + at : width + at + 2 * LANES], NT)
+    normed_t[now] = turn(normed[...])
+    cot_t[now] = cot.T.astype(bf16)
+    branch_b = branch.astype(bf16)
 
     @pl.when(c < half)
     def _():
-        sent_o[...] = branch
+        sent_o[...] = branch_b
 
     @pl.when(c >= half)
     def _():
-        kept_o[...] = branch
-
-    acc[:, :width] += mm(normed[...], ggate_o[...], TN)
-    acc[:, width:] += mm(cot, nout[...], TN)
+        kept_o[...] = branch_b
 
     @pl.when(c == last)
     def _():
+        acc[:, :width] += mm(normed_t[now], gates[now])
+        acc[:, width:] += mm(cot_t[now], nout[now])
         store_rows(info, acc, gw_o, masks, acc.shape[0] // len(masks))
         ggo_o[...] = acc_g[...]
         gain_o[...] = row_products(acc, w, width)
@@ -719,8 +730,8 @@
         )
         held = [many] + got_many
         few = jnp.stack([few] + got_few)
-        wx = [few] + [swap(few, far, "dp") for far in FAR[1:]]
-        wx_at = [(width, tuple(near ^ far for near in NEAR)) for far in FAR]
+        wx = [jnp.concatenate([few] + [swap(few, far, "dp") for far in FAR[1:]])]
+        wx_at = [(width, tuple(near ^ far for far in FAR for near in NEAR))]
         near_x, near_at = gather_near(jnp.stack([v[:, :width] for v in held]))
         wx, wx_at = near_x + wx, near_at + wx_at
         resid_oth = swap(resid_in, 1, "tensor")
@@ -803,18 +814,25 @@
         return jnp.where(c < rhalf, c + rhalf * (1 - info[0]), c - rhalf + rhalf * info[0])
 
     gw_shapes, masks = scatter_shapes(size, rows, 2 * width)
-    twide = block(width, turned)
-    lead = block(dim, lambda c, info: jnp.minimum(c, rhalf - 1))
-    trail = block(dim, lambda c, info: jnp.maximum(c - rhalf, 0))
+
+    def turned_l(c, info):
+        return jnp.where(c < half, c + half * (1 - info[0]), c - half + half * info[0])
+
+    twide = rows_spec(L, width, turned_l)
+    lead = rows_spec(L, dim, lambda c, info: jnp.minimum(c, half - 1))
+    trail = rows_spec(L, dim, lambda c, info: jnp.maximum(c - half, 0))
+    sums_spec = pl.BlockSpec(
+        (16, L), lambda c, info: (turned_l(c, info) // (R // L), turned_l(c, info) % (R // L))
+    )
     half_shape = shape((half_rows, dim), bf16)
     branch_sent, branch_own, ggate, gm, g_gout, g_gin_z, *gw_zo = call(
         functools.partial(gate_back_kernel, wz_at, masks),
         "gate_backward",
         52,
-        steps,
-        [
-            trail, lead, block(dim, turned), twide, twide, twide,
-            rows_spec(16, R, turned), rows_spec(16, R, turned), full((16, cols)),
+        chunks,
+        [
+            trail, lead, rows_spec(L, dim, turned_l), twide, twide, twide,
+            sums_spec, sums_spec, full((16, cols)),
         ]
         + [anywhere] * len(wz),
         [
@@ -825,7 +843,9 @@
         + [(full(item.shape), item) for item in gw_shapes],
         [
             pltpu.VMEM((dim, 2 * width), f32), pltpu.VMEM((8, width), f32),
-            pltpu.VMEM((dim, 2 * width), bf16), pltpu.VMEM((R, width), bf16), copies(wz_at),
+            pltpu.VMEM((dim, 2 * width), bf16), pltpu.VMEM((2, L, width), bf16),
+            pltpu.VMEM((2, L, width), bf16), pltpu.VMEM((2, dim, L), bf16),
+            pltpu.VMEM((2, dim, L), bf16), copies(wz_at),
         ],
         info, cotangent, cot_oth, normed, mixed, gate, gno, sums, sums_oth, consts, *wz,
     )
@@ -874,14 +894,16 @@
         sent_x = scatter_near(gw_x)
         far_zo = scatter_far(sum_pieces(sent_zo), rows)
 
+    lead_r = block(dim, lambda c, info: jnp.minimum(c, rhalf - 1))
+    trail_r = block(dim, lambda c, info: jnp.maximum(c - rhalf, 0))
     dn_sent, dn_own = call(
         functools.partial(input_back_kernel, wz_at, wx_at),
         "input_backward",
         32,
         steps,
-        [twide, block(cols + LANES, turned)]
+        [block(width, turned), block(cols + LANES, turned)]
         + [anywhere] * (len(wz) + len(wx)),
-        [(lead, half_shape), (trail, half_shape)],
+        [(lead_r, half_shape), (trail_r, half_shape)],
         [
             pltpu.VMEM((dim, width), bf16), pltpu.VMEM((dim, cols + LANES), bf16),
             pltpu.VMEM((R, dim), bf16), copies(wz_at), copies(wx_at),
@@ -910,11 +932,14 @@
     )
 
     if direct(size, rows):
-        block_out, grad_resid, far_x = lax.optimization_barrier((block_out, grad_resid, far_x))
+        block_out, grad_resid, far_x, grad_w_z, grad_w_out = lax.optimization_barrier(
+            (block_out, grad_resid, far_x, sum_zo[:, :width], sum_zo[:, width:].T)
+        )
         sum_x = sum_pieces(far_x)
         small = both_parts(sum_x)
     else:
         sum_zo = scatter_whole(sent_zo[0], bits)
+        grad_w_z, grad_w_out = sum_zo[:, :width], sum_zo[:, width:].T
         sum_x = scatter_whole(gw_x[0], bits)
         for bit in bits:
             small = small + swap(small, bit, "dp")
@@ -926,11 +951,11 @@
     grad_w_bc, bc_g, gain_g = jnp.split(pair, [rows * 2 * NS, (rows + 5) * 2 * NS])
     bc_g = bc_g.reshape(5, 2 * NS)
     return (
-        block_out, grad_resid, gain_g / gain_in, sum_zo[:, :width], sum_x[:rows, :width],
+        block_out, grad_resid, gain_g / gain_in, grad_w_z, sum_x[:rows, :width],
         grad_w_bc.reshape(rows, 2 * NS), sum_x[:rows, cols : cols + heads],
         small[:4, :width], small[4, :width], bc_g[:4], bc_g[4], small[0, cols : cols + heads],
         small[1, cols : cols + heads], small[5, :width].reshape(heads, HEAD).sum(axis=1),
-        small[6, :width], sum_zo[:, width:].T,
+        small[6, :width], grad_w_out,
     )
 
 

time: 229 us -> 223 us (0.974)
  waiting for transfers between devices: 30.7 us -> 27.8 us
    ppermute x33, waiting for transfers between devices: 30.7 us -> 27.8 us  [swap(): return lax.ppermute(v, axis, [(i, i ^ bit) for i in range(size)])]
    unnamed x66 -> x62, local copies, waits for them, and re-layouts: 11.1 us -> 9.25 us
  transfers between devices with their start and end apart: 33 -> 33, of which waited for: 12 -> 10; matrix products, arithmetic and copies ran while one was open for 5% -> 6% of each run, Pallas kernels for 37% -> 38%
where the time goes in v5:
time: 223 us; the launch traced here: 221 us
  Pallas kernels  124 us (56%)
  starting transfers between devices  43 us (19%)
  waiting for transfers between devices  27.8 us (12%)
  local copies, waits for them, and re-layouts  18.6 us (8%)
  other arithmetic  6.35 us (3%)
    pallas_call x6, Pallas kernels, call(): pl.pallas_call(kernel, grid_spec=pltpu.PrefetchScalarGridSpec(num_scalar_...  124 us
    ppermute x33, starting transfers between devices, swap(): return lax.ppermute(v, axis, [(i, i ^ bit) for i in range(size)])  43 us
    ppermute x33, waiting for transfers between devices, swap(): return lax.ppermute(v, axis, [(i, i ^ bit) for i in range(size)])  27.8 us
    unnamed x62, local copies, waits for them, and re-layouts  9.25 us
  transfers between devices with their start and end apart: 33, of which 10 were waited for; matrix products, arithmetic and copies ran while one was open for 6% of the time, Pallas kernels for 38%

profile of v5, /device:TPU:0, one launch (start us, length us, event | category | flops | bytes accessed | tf_op | source)
XLA Modules:
  0.0 221.1 jit_solution(14215353569790609737)
XLA Ops:
  1.6 3.1 %collective-permute-start = (bf16[48,2304]{1,0:T(8,128)(2,1)S(1)}, bf16[48,2304]{1,0:T(8,128)(2,1)S(1)}, u32[]{:S(2)}, u32[]{:S(2)}) collective-permute-start(bf16[48,2304]{1,0:T(8,128)(2,1)S(1)} %pad_maximum_fusion.9), channel_id=1, source_target_pairs={{0,8},{2,10},{4,12},{6,14},{8,0},{10,2},{12,4},{14,6},{16,24},{18,... | collective-permute-start | bytes 663560 | tf_op jit(solution)/shard_map/ppermute | solution.py:573
  4.7 2.6 %collective-permute-start.1 = (bf16[48,2304]{1,0:T(8,128)(2,1)S(1)}, bf16[48,2304]{1,0:T(8,128)(2,1)S(1)}, u32[]{:S(2)}, u32[]{:S(2)}) collective-permute-start(bf16[48,2304]{1,0:T(8,128)(2,1)S(1)} %pad_maximum_fusion.9), channel_id=1, source_target_pairs={{0,16},{2,18},{4,20},{6,22},{8,24},{10,26},{12,28},{14,30},{16,0},... | collective-permute-start | bytes 663560 | tf_op jit(solution)/shard_map/ppermute | solution.py:573
  8.9 1.7 collective-permute-start.3
  10.6 1.5 collective-permute-start.4
  19.9 3.6 %collective-permute-done.1 = bf16[48,2304]{1,0:T(8,128)(2,1)S(1)} collective-permute-done((bf16[48,2304]{1,0:T(8,128)(2,1)S(1)}, bf16[48,2304]{1,0:T(8,128)(2,1)S(1)}, u32[]{:S(2)}, u32[]{:S(2)}) %collective-permute-start.1) | collective-permute-done | bytes 221216 | tf_op jit(solution)/shard_map/ppermute | solution.py:573
  23.5 3.9 %collective-permute-start.11 = (bf16[4,48,384]{2,1,0:T(8,128)(2,1)S(1)}, bf16[4,48,384]{2,1,0:T(8,128)(2,1)S(1)}, u32[]{:S(2)}, u32[]{:S(2)}) collective-permute-start(bf16[4,48,384]{2,1,0:T(8,128)(2,1)S(1)} %pad_maximum_fusion.10), channel_id=1, source_target_pairs={{0,8},{2,10},{4,12},{6,14},{8,0},{10,2},{12,4},{14,6},{16,24},{18,... | collective-permute-start | bytes 442376 | tf_op jit(solution)/shard_map/ppermute | solution.py:573
  30.5 1.6 collective-permute-done.11
  32.2 2.4 %collective-permute-start.10 = (bf16[4,48,768]{2,1,0:T(8,128)(2,1)S(1)}, bf16[4,48,768]{2,1,0:T(8,128)(2,1)S(1)}, u32[]{:S(2)}, u32[]{:S(2)}) collective-permute-start(bf16[4,48,768]{2,1,0:T(8,128)(2,1)S(1)} %pad_maximum_fusion.1.rest_0_.rest_4_), channel_id=1, source_target_pairs={{0,6},{2,4},{4,2},{6,0},{8,14},{10,12},{12,10},{14,8},{16,22},{18,... | collective-permute-start | bytes 884744 | tf_op jit(solution)/shard_map/ppermute | solution.py:573
  34.6 5.8 %collective-permute-done.12 = bf16[4,48,384]{2,1,0:T(8,128)(2,1)S(1)} collective-permute-done((bf16[4,48,384]{2,1,0:T(8,128)(2,1)S(1)}, bf16[4,48,384]{2,1,0:T(8,128)(2,1)S(1)}, u32[]{:S(2)}, u32[]{:S(2)}) %collective-permute-start.12) | collective-permute-done | bytes 147488 | tf_op jit(solution)/shard_map/ppermute | solution.py:573
  40.4 1.5 collective-permute-start.8
  41.9 1.5 collective-permute-start.9
  43.6 3.6 %collective-permute-done.8.rest_1_.rest_5_ = bf16[4,48,768]{2,1,0:T(8,128)(2,1)S(1)} collective-permute-done((bf16[4,48,768]{2,1,0:T(8,128)(2,1)S(1)}, bf16[4,48,768]{2,1,0:T(8,128)(2,1)S(1)}, u32[]{:S(2)}, u32[]{:S(2)}) %collective-permute-start.8) | collective-permute-done | bytes 294944 | tf_op jit(solution)/shard_map/ppermute | solution.py:573
  47.2 1.5 collective-permute-done.9.rest_2_.rest_6_
  51.1 1.5 collective-permute-start.15
  52.6 1.4 collective-permute-start.16
  56.9 27.9 %mix_forward.1 = (bf16[2048,768]{1,0:T(8,128)(2,1)}, bf16[2048,1024]{1,0:T(8,128)(2,1)}, bf16[2048,1024]{1,0:T(8,128)(2,1)}, bf16[2048,1024]{1,0:T(8,128)(2,1)},...) custom-call(s32[2]{0:T(128)S(1)} %pad_add_fusion.info, ...), custom_call_target="tpu_custom_call" | custom-call | tf_op jit(solution)/shard_map/mix_forward/pallas_call | solution.py:667
  85.7 15.8 %gate_forward.1 = (bf16[2048,768]{1,0:T(8,128)(2,1)}, f32[2048,768]{1,0:T(8,128)}, f32[64,512]{1,0:T(8,128)S(1)}) custom-call(s32[2]{0:T(128)S(1)} %pad_add_fusion.info, bf16[1024,768]{1,0:T(8,128)(2,1)} %refs_1_.1, bf16[1024,768]{1,0:T(8,128)(2,1)} %copy-done.22, bf16[2048,768]{1,0:T(8,128)(2,1)} %get-tuple-element.116.normed, ...), custom_call_target="tpu_custom_call" | custom-call | tf_op jit(solution)/shard_map/gate_forward/pallas_call | solution.py:667
  102.9 23.7 %gate_backward.1 = (bf16[1024,768]{1,0:T(8,128)(2,1)}, bf16[1024,768]{1,0:T(8,128)(2,1)}, bf16[2048,768]{1,0:T(8,128)(2,1)}, bf16[2048,768]{1,0:T(8,128)(2,1)}, ...) custom-call(s32[2]{0:T(128)S(1)} %pad_add_fusion.info, ...), custom_call_target="tpu_custom_call" | custom-call | tf_op jit(solution)/shard_map/gate_backward/pallas_call | solution.py:667
  127.5 1.5 collective-permute-start.19
  130.5 43.5 %mix_backward.1 = (bf16[2048,1152]{1,0:T(8,128)(2,1)}, f32[8,1152]{1,0:T(8,128)}, bf16[208,1152]{1,0:T(8,128)(2,1)}, bf16[208,1152]{1,0:T(8,128)(2,1)}, bf16[208...) custom-call(s32[2]{0:T(128)S(1)} %pad_add_fusion.info, bf16[2048,1024]{1,0:T(8,128)(2,1)} %get-tuple-element.130.xbc, ...), custom_call_target="tpu_custom_call" | custom-call | tf_op jit(solution)/shard_map/mix_backward/pallas_call | solution.py:667
  174.6 1.5 collective-permute-start.26
  176.2 1.4 collective-permute-start.27
  177.9 2.1 collective-permute-start.22
  181.5 2.3 %copy-done.12 = bf16[2048,1152]{1,0:T(8,128)(2,1)S(1)} copy-done((bf16[2048,1152]{1,0:T(8,128)(2,1)S(1)}, bf16[2048,1152]{1,0:T(8,128)(2,1)}, u32[]{:S(2)}) %copy-start.12) | copy-done | bytes 4718616
  183.8 9.4 %input_backward.1 = (bf16[1024,768]{1,0:T(8,128)(2,1)S(1)}, bf16[1024,768]{1,0:T(8,128)(2,1)S(1)}) custom-call(s32[2]{0:T(128)S(1)} %pad_add_fusion.info, bf16[2048,768]{1,0:T(8,128)(2,1)S(1)} %copy-done.13, bf16[2048,1152]{1,0:T(8,128)(2,1)S(1)} %copy-done.12, bf16[4,48,1536]{2,1,0:T(8,128)(2,1)S(1)} %copy-done.2, bf16[4,48,1536]{2,1,0:T(8,128)(2,1)S(1)} %copy-done.7, ...), custom_call_target="tpu_custom_call" | custom-call | tf_op jit(solution)/shard_map/input_backward/pallas_call | solution.py:667
  193.2 1.5 collective-permute-start.24
  194.7 1.6 collective-permute-done.26
  196.3 1.5 collective-permute-done.27
  198.2 2.4 %collective-permute-start.29 = (bf16[64,1152]{1,0:T(8,128)(2,1)S(1)}, bf16[64,1152]{1,0:T(8,128)(2,1)S(1)}, u32[]{:S(2)}, u32[]{:S(2)}) collective-permute-start(bf16[64,1152]{1,0:T(8,128)(2,1)S(1)} %get-tuple-element.219), channel_id=1, source_target_pairs={{0,8},{2,10},{4,12},{6,14},{8,0},{10,2},{12,4},{14,6},{16,24},{18,... | collective-permute-start | bytes 442376 | tf_op jit(solution)/shard_map/ppermute | solution.py:573
  202.0 1.5 collective-permute-start.31
  203.6 3.9 %finish.1 = (bf16[1024,768]{1,0:T(8,128)(2,1)}, f32[1024,768]{1,0:T(8,128)}) custom-call(s32[2]{0:T(128)S(1)} %pad_add_fusion.info, bf16[1024,768]{1,0:T(8,128)(2,1)S(1)} %copy-done.3, bf16[1024,768]{1,0:T(8,128)(2,1)S(1)} %copy-done, f32[16,1024]{1,0:T(8,128)S(1)} %copy-done.20, bf16[1024,768]{1,0:T(8,128)(2,1)S(1)} %get-tuple-element.158.refs_3_, ...), custom_call_target="tpu_custom_call" | custom-call | tf_op jit(solution)/shard_map/finish/pallas_call | solution.py:667
  208.2 6.4 %collective-permute-done.30 = bf16[64,1152]{1,0:T(8,128)(2,1)S(1)} collective-permute-done((bf16[64,1152]{1,0:T(8,128)(2,1)S(1)}, bf16[64,1152]{1,0:T(8,128)(2,1)S(1)}, u32[]{:S(2)}, u32[]{:S(2)}) %collective-permute-start.30) | collective-permute-done | bytes 147488 | tf_op jit(solution)/shard_map/ppermute | solution.py:573
  (168 shorter events, 34.6 us)
Async XLA Ops:
  1.6 18.3 %collective-permute-start = (bf16[48,2304]{1,0:T(8,128)(2,1)S(1)}, bf16[48,2304]{1,0:T(8,128)(2,1)S(1)}, u32[]{:S(2)}, u32[]{:S(2)}) collective-permute-start(bf16[48,2304]{1,0:T(8,128)(2,1)S(1)} %pad_maximum_fusion.9), channel_id=1, source_target_pairs={{0,8},{2,10},{4,12},{6,14},{8,0},{10,2},{12,4},{14,6},{16,24},{18,... | collective-permute-start | bytes 663560 | tf_op jit(solution)/shard_map/ppermute | solution.py:573
  4.7 18.7 %collective-permute-start.1 = (bf16[48,2304]{1,0:T(8,128)(2,1)S(1)}, bf16[48,2304]{1,0:T(8,128)(2,1)S(1)}, u32[]{:S(2)}, u32[]{:S(2)}) collective-permute-start(bf16[48,2304]{1,0:T(8,128)(2,1)S(1)} %pad_maximum_fusion.9), channel_id=1, source_target_pairs={{0,16},{2,18},{4,20},{6,22},{8,24},{10,26},{12,28},{14,30},{16,0},... | collective-permute-start | bytes 663560 | tf_op jit(solution)/shard_map/ppermute | solution.py:573
  7.3 16.1 %collective-permute-start.2 = (bf16[48,2304]{1,0:T(8,128)(2,1)S(1)}, bf16[48,2304]{1,0:T(8,128)(2,1)S(1)}, u32[]{:S(2)}, u32[]{:S(2)}) collective-permute-start(bf16[48,2304]{1,0:T(8,128)(2,1)S(1)} %pad_maximum_fusion.9), channel_id=1, source_target_pairs={{0,24},{2,26},{4,28},{6,30},{8,16},{10,18},{12,20},{14,22},{16,8},... | collective-permute-start | bytes 663560 | tf_op jit(solution)/shard_map/ppermute | solution.py:573
  8.9 6.1 %collective-permute-start.3 = (bf16[48,384]{1,0:T(8,128)(2,1)S(1)}, bf16[48,384]{1,0:T(8,128)(2,1)S(1)}, u32[]{:S(2)}, u32[]{:S(2)}) collective-permute-start(bf16[48,384]{1,0:T(8,128)(2,1)S(1)} %pad_maximum_fusion.12), channel_id=1, source_target_pairs={{0,2},{2,0},{4,6},{6,4},{8,10},{10,8},{12,14},{14,12},{16,18},{18,... | collective-permute-start | bytes 110600 | tf_op jit(solution)/shard_map/ppermute | solution.py:573
  10.6 8.5 %collective-permute-start.4 = (bf16[48,384]{1,0:T(8,128)(2,1)S(1)}, bf16[48,384]{1,0:T(8,128)(2,1)S(1)}, u32[]{:S(2)}, u32[]{:S(2)}) collective-permute-start(bf16[48,384]{1,0:T(8,128)(2,1)S(1)} %pad_maximum_fusion.12), channel_id=1, source_target_pairs={{0,4},{2,6},{4,0},{6,2},{8,12},{10,14},{12,8},{14,10},{16,20},{18,... | collective-permute-start | bytes 110600 | tf_op jit(solution)/shard_map/ppermute | solution.py:573
  15.0 4.9 %collective-permute-start.5 = (bf16[48,384]{1,0:T(8,128)(2,1)S(1)}, bf16[48,384]{1,0:T(8,128)(2,1)S(1)}, u32[]{:S(2)}, u32[]{:S(2)}) collective-permute-start(bf16[48,384]{1,0:T(8,128)(2,1)S(1)} %pad_maximum_fusion.12), channel_id=1, source_target_pairs={{0,6},{2,4},{4,2},{6,0},{8,14},{10,12},{12,10},{14,8},{16,22},{18,... | collective-permute-start | bytes 110600 | tf_op jit(solution)/shard_map/ppermute | solution.py:573
  23.5 8.7 %collective-permute-start.11 = (bf16[4,48,384]{2,1,0:T(8,128)(2,1)S(1)}, bf16[4,48,384]{2,1,0:T(8,128)(2,1)S(1)}, u32[]{:S(2)}, u32[]{:S(2)}) collective-permute-start(bf16[4,48,384]{2,1,0:T(8,128)(2,1)S(1)} %pad_maximum_fusion.10), channel_id=1, source_target_pairs={{0,8},{2,10},{4,12},{6,14},{8,0},{10,2},{12,4},{14,6},{16,24},{18,... | collective-permute-start | bytes 442376 | tf_op jit(solution)/shard_map/ppermute | solution.py:573
  27.4 13.0 %collective-permute-start.12 = (bf16[4,48,384]{2,1,0:T(8,128)(2,1)S(1)}, bf16[4,48,384]{2,1,0:T(8,128)(2,1)S(1)}, u32[]{:S(2)}, u32[]{:S(2)}) collective-permute-start(bf16[4,48,384]{2,1,0:T(8,128)(2,1)S(1)} %pad_maximum_fusion.10), channel_id=1, source_target_pairs={{0,16},{2,18},{4,20},{6,22},{8,24},{10,26},{12,28},{14,30},{16,0},... | collective-permute-start | bytes 442376 | tf_op jit(solution)/shard_map/ppermute | solution.py:573
  28.5 13.4 %collective-permute-start.13 = (bf16[4,48,384]{2,1,0:T(8,128)(2,1)S(1)}, bf16[4,48,384]{2,1,0:T(8,128)(2,1)S(1)}, u32[]{:S(2)}, u32[]{:S(2)}) collective-permute-start(bf16[4,48,384]{2,1,0:T(8,128)(2,1)S(1)} %pad_maximum_fusion.10), channel_id=1, source_target_pairs={{0,24},{2,26},{4,28},{6,30},{8,16},{10,18},{12,20},{14,22},{16,8},... | collective-permute-start | bytes 442376 | tf_op jit(solution)/shard_map/ppermute | solution.py:573
  29.9 18.8 %collective-permute-start.6 = (bf16[1024,768]{1,0:T(8,128)(2,1)}, bf16[1024,768]{1,0:T(8,128)(2,1)S(1)}, u32[]{:S(2)}, u32[]{:S(2)}) collective-permute-start(bf16[1024,768]{1,0:T(8,128)(2,1)} %refs_0_.1), channel_id=1, source_target_pairs={{0,1},{1,0},{2,3},{3,2},{4,5},{5,4},{6,7},{7,6},{8,9},{9,8},{10,11... | collective-permute-start | bytes 4718600 | tf_op jit(solution)/shard_map/ppermute | solution.py:573
  29.9 18.8 %collective-permute-start.7 = (bf16[1024,768]{1,0:T(8,128)(2,1)}, bf16[1024,768]{1,0:T(8,128)(2,1)S(1)}, u32[]{:S(2)}, u32[]{:S(2)}) collective-permute-start(bf16[1024,768]{1,0:T(8,128)(2,1)} %refs_1_.1), channel_id=1, source_target_pairs={{0,1},{1,0},{2,3},{3,2},{4,5},{5,4},{6,7},{7,6},{8,9},{9,8},{10,11... | collective-permute-start | bytes 4718600 | tf_op jit(solution)/shard_map/ppermute | solution.py:573
  32.2 11.4 %collective-permute-start.10 = (bf16[4,48,768]{2,1,0:T(8,128)(2,1)S(1)}, bf16[4,48,768]{2,1,0:T(8,128)(2,1)S(1)}, u32[]{:S(2)}, u32[]{:S(2)}) collective-permute-start(bf16[4,48,768]{2,1,0:T(8,128)(2,1)S(1)} %pad_maximum_fusion.1.rest_0_.rest_4_), channel_id=1, source_target_pairs={{0,6},{2,4},{4,2},{6,0},{8,14},{10,12},{12,10},{14,8},{16,22},{18,... | collective-permute-start | bytes 884744 | tf_op jit(solution)/shard_map/ppermute | solution.py:573
  40.4 6.7 %collective-permute-start.8 = (bf16[4,48,768]{2,1,0:T(8,128)(2,1)S(1)}, bf16[4,48,768]{2,1,0:T(8,128)(2,1)S(1)}, u32[]{:S(2)}, u32[]{:S(2)}) collective-permute-start(bf16[4,48,768]{2,1,0:T(8,128)(2,1)S(1)} %pad_maximum_fusion.1.rest_0_.rest_4_), channel_id=1, source_target_pairs={{0,2},{2,0},{4,6},{6,4},{8,10},{10,8},{12,14},{14,12},{16,18},{18,... | collective-permute-start | bytes 884744 | tf_op jit(solution)/shard_map/ppermute | solution.py:573
  41.9 6.7 %collective-permute-start.9 = (bf16[4,48,768]{2,1,0:T(8,128)(2,1)S(1)}, bf16[4,48,768]{2,1,0:T(8,128)(2,1)S(1)}, u32[]{:S(2)}, u32[]{:S(2)}) collective-permute-start(bf16[4,48,768]{2,1,0:T(8,128)(2,1)S(1)} %pad_maximum_fusion.1.rest_0_.rest_4_), channel_id=1, source_target_pairs={{0,4},{2,6},{4,0},{6,2},{8,12},{10,14},{12,8},{14,10},{16,20},{18,... | collective-permute-start | bytes 884744 | tf_op jit(solution)/shard_map/ppermute | solution.py:573
  50.5 34.3 %collective-permute-start.14 = (bf16[4,48,1536]{2,1,0:T(8,128)(2,1)S(1)}, bf16[4,48,1536]{2,1,0:T(8,128)(2,1)S(1)}, u32[]{:S(2)}, u32[]{:S(2)}) collective-permute-start(bf16[4,48,1536]{2,1,0:T(8,128)(2,1)S(1)} %pad_maximum_fusion.rest_0_), channel_id=1, source_target_pairs={{0,2},{2,0},{4,6},{6,4},{8,10},{10,8},{12,14},{14,12},{16,18},{18,... | collective-permute-start | bytes 1769480 | tf_op jit(solution)/shard_map/ppermute | solution.py:573
  51.1 33.7 %collective-permute-start.15 = (bf16[4,48,1536]{2,1,0:T(8,128)(2,1)S(1)}, bf16[4,48,1536]{2,1,0:T(8,128)(2,1)S(1)}, u32[]{:S(2)}, u32[]{:S(2)}) collective-permute-start(bf16[4,48,1536]{2,1,0:T(8,128)(2,1)S(1)} %pad_maximum_fusion.rest_0_), channel_id=1, source_target_pairs={{0,4},{2,6},{4,0},{6,2},{8,12},{10,14},{12,8},{14,10},{16,20},{18,... | collective-permute-start | bytes 1769480 | tf_op jit(solution)/shard_map/ppermute | solution.py:573
  52.6 32.2 %collective-permute-start.16 = (bf16[4,48,1536]{2,1,0:T(8,128)(2,1)S(1)}, bf16[4,48,1536]{2,1,0:T(8,128)(2,1)S(1)}, u32[]{:S(2)}, u32[]{:S(2)}) collective-permute-start(bf16[4,48,1536]{2,1,0:T(8,128)(2,1)S(1)} %pad_maximum_fusion.rest_0_), channel_id=1, source_target_pairs={{0,6},{2,4},{4,2},{6,0},{8,14},{10,12},{12,10},{14,8},{16,22},{18,... | collective-permute-start | bytes 1769480 | tf_op jit(solution)/shard_map/ppermute | solution.py:573
  126.6 47.4 %collective-permute-start.21 = (bf16[1024,768]{1,0:T(8,128)(2,1)}, bf16[1024,768]{1,0:T(8,128)(2,1)S(1)}, u32[]{:S(2)}, u32[]{:S(2)}) collective-permute-start(bf16[1024,768]{1,0:T(8,128)(2,1)} %get-tuple-element.129), channel_id=1, source_target_pairs={{0,1},{1,0},{2,3},{3,2},{4,5},{5,4},{6,7},{7,6},{8,9},{9,8},{10,11... | collective-permute-start | bytes 4718600 | tf_op jit(solution)/shard_map/ppermute | solution.py:573
  126.9 47.0 %collective-permute-start.18 = (bf16[192,1536]{1,0:T(8,128)(2,1)S(1)}, bf16[192,1536]{1,0:T(8,128)(2,1)S(1)}, u32[]{:S(2)}, u32[]{:S(2)}) collective-permute-start(bf16[192,1536]{1,0:T(8,128)(2,1)S(1)} %get-tuple-element.126), channel_id=1, source_target_pairs={{0,2},{2,0},{4,6},{6,4},{8,10},{10,8},{12,14},{14,12},{16,18},{18,... | collective-permute-start | bytes 1769480 | tf_op jit(solution)/shard_map/ppermute | solution.py:573
  127.5 46.5 %collective-permute-start.19 = (bf16[192,1536]{1,0:T(8,128)(2,1)}, bf16[192,1536]{1,0:T(8,128)(2,1)S(1)}, u32[]{:S(2)}, u32[]{:S(2)}) collective-permute-start(bf16[192,1536]{1,0:T(8,128)(2,1)} %get-tuple-element.127), channel_id=1, source_target_pairs={{0,4},{2,6},{4,0},{6,2},{8,12},{10,14},{12,8},{14,10},{16,20},{18,... | collective-permute-start | bytes 1769480 | tf_op jit(solution)/shard_map/ppermute | solution.py:573
  129.0 45.0 %collective-permute-start.20 = (bf16[192,1536]{1,0:T(8,128)(2,1)}, bf16[192,1536]{1,0:T(8,128)(2,1)S(1)}, u32[]{:S(2)}, u32[]{:S(2)}) collective-permute-start(bf16[192,1536]{1,0:T(8,128)(2,1)} %get-tuple-element.128), channel_id=1, source_target_pairs={{0,6},{2,4},{4,2},{6,0},{8,14},{10,12},{12,10},{14,8},{16,22},{18,... | collective-permute-start | bytes 1769480 | tf_op jit(solution)/shard_map/ppermute | solution.py:573
  174.0 19.2 %collective-permute-start.25 = (bf16[208,1152]{1,0:T(8,128)(2,1)}, bf16[208,1152]{1,0:T(8,128)(2,1)S(1)}, u32[]{:S(2)}, u32[]{:S(2)}) collective-permute-start(bf16[208,1152]{1,0:T(8,128)(2,1)} %get-tuple-element.149), channel_id=1, source_target_pairs={{0,2},{2,0},{4,6},{6,4},{8,10},{10,8},{12,14},{14,12},{16,18},{18,... | collective-permute-start | bytes 1437704 | tf_op jit(solution)/shard_map/ppermute | solution.py:573
  174.6 21.7 %collective-permute-start.26 = (bf16[208,1152]{1,0:T(8,128)(2,1)}, bf16[208,1152]{1,0:T(8,128)(2,1)S(1)}, u32[]{:S(2)}, u32[]{:S(2)}) collective-permute-start(bf16[208,1152]{1,0:T(8,128)(2,1)} %get-tuple-element.150), channel_id=1, source_target_pairs={{0,4},{2,6},{4,0},{6,2},{8,12},{10,14},{12,8},{14,10},{16,20},{18,... | collective-permute-start | bytes 1437704 | tf_op jit(solution)/shard_map/ppermute | solution.py:573
  176.2 21.7 %collective-permute-start.27 = (bf16[208,1152]{1,0:T(8,128)(2,1)}, bf16[208,1152]{1,0:T(8,128)(2,1)S(1)}, u32[]{:S(2)}, u32[]{:S(2)}) collective-permute-start(bf16[208,1152]{1,0:T(8,128)(2,1)} %get-tuple-element.151), channel_id=1, source_target_pairs={{0,6},{2,4},{4,2},{6,0},{8,14},{10,12},{12,10},{14,8},{16,22},{18,... | collective-permute-start | bytes 1437704 | tf_op jit(solution)/shard_map/ppermute | solution.py:573
  177.9 22.7 %collective-permute-start.22 = (bf16[48,1536]{1,0:T(8,128)(2,1)S(1)}, bf16[48,1536]{1,0:T(8,128)(2,1)S(1)}, u32[]{:S(2)}, u32[]{:S(2)}) collective-permute-start(bf16[48,1536]{1,0:T(8,128)(2,1)S(1)} %get-tuple-element.210), channel_id=1, source_target_pairs={{0,8},{2,10},{4,12},{6,14},{8,0},{10,2},{12,4},{14,6},{16,24},{18,... | collective-permute-start | bytes 442376 | tf_op jit(solution)/shard_map/ppermute | solution.py:573
  180.0 21.9 %collective-permute-start.23 = (bf16[48,1536]{1,0:T(8,128)(2,1)S(1)}, bf16[48,1536]{1,0:T(8,128)(2,1)S(1)}, u32[]{:S(2)}, u32[]{:S(2)}) collective-permute-start(bf16[48,1536]{1,0:T(8,128)(2,1)S(1)} %get-tuple-element.209), channel_id=1, source_target_pairs={{0,16},{2,18},{4,20},{6,22},{8,24},{10,26},{12,28},{14,30},{16,0},... | collective-permute-start | bytes 442376 | tf_op jit(solution)/shard_map/ppermute | solution.py:573
  193.2 10.3 %collective-permute-start.24 = (bf16[48,1536]{1,0:T(8,128)(2,1)S(1)}, bf16[48,1536]{1,0:T(8,128)(2,1)S(1)}, u32[]{:S(2)}, u32[]{:S(2)}) collective-permute-start(bf16[48,1536]{1,0:T(8,128)(2,1)S(1)} %get-tuple-element.208), channel_id=1, source_target_pairs={{0,24},{2,26},{4,28},{6,30},{8,16},{10,18},{12,20},{14,22},{16,8},... | collective-permute-start | bytes 442376 | tf_op jit(solution)/shard_map/ppermute | solution.py:573
  197.8 5.7 %collective-permute-start.28 = (bf16[1024,768]{1,0:T(8,128)(2,1)S(1)}, bf16[1024,768]{1,0:T(8,128)(2,1)S(1)}, u32[]{:S(2)}, u32[]{:S(2)}) collective-permute-start(bf16[1024,768]{1,0:T(8,128)(2,1)S(1)} %get-tuple-element.156), channel_id=1, source_target_pairs={{0,1},{1,0},{2,3},{3,2},{4,5},{5,4},{6,7},{7,6},{8,9},{9,8},{10,11... | collective-permute-start | bytes 4718600 | tf_op jit(solution)/shard_map/ppermute | solution.py:573
  198.2 10.0 %collective-permute-start.29 = (bf16[64,1152]{1,0:T(8,128)(2,1)S(1)}, bf16[64,1152]{1,0:T(8,128)(2,1)S(1)}, u32[]{:S(2)}, u32[]{:S(2)}) collective-permute-start(bf16[64,1152]{1,0:T(8,128)(2,1)S(1)} %get-tuple-element.219), channel_id=1, source_target_pairs={{0,8},{2,10},{4,12},{6,14},{8,0},{10,2},{12,4},{14,6},{16,24},{18,... | collective-permute-start | bytes 442376 | tf_op jit(solution)/shard_map/ppermute | solution.py:573
  200.6 14.0 %collective-permute-start.30 = (bf16[64,1152]{1,0:T(8,128)(2,1)S(1)}, bf16[64,1152]{1,0:T(8,128)(2,1)S(1)}, u32[]{:S(2)}, u32[]{:S(2)}) collective-permute-start(bf16[64,1152]{1,0:T(8,128)(2,1)S(1)} %get-tuple-element.220), channel_id=1, source_target_pairs={{0,16},{2,18},{4,20},{6,22},{8,24},{10,26},{12,28},{14,30},{16,0},... | collective-permute-start | bytes 442376 | tf_op jit(solution)/shard_map/ppermute | solution.py:573
  202.0 12.7 %collective-permute-start.31 = (bf16[64,1152]{1,0:T(8,128)(2,1)S(1)}, bf16[64,1152]{1,0:T(8,128)(2,1)S(1)}, u32[]{:S(2)}, u32[]{:S(2)}) collective-permute-start(bf16[64,1152]{1,0:T(8,128)(2,1)S(1)} %get-tuple-element.218), channel_id=1, source_target_pairs={{0,24},{2,26},{4,28},{6,30},{8,16},{10,18},{12,20},{14,22},{16,8},... | collective-permute-start | bytes 442376 | tf_op jit(solution)/shard_map/ppermute | solution.py:573
  215.4 3.3 %collective-permute-start.32 = (f32[14336]{0:T(1024)S(1)}, f32[14336]{0:T(1024)S(1)}, u32[]{:S(2)}, u32[]{:S(2)}) collective-permute-start(f32[14336]{0:T(1024)S(1)} %pad_maximum_fusion.11), channel_id=1, source_target_pairs={{0,1},{1,0},{2,3},{3,2},{4,5},{5,4},{6,7},{7,6},{8,9},{9,8},{10,11... | collective-permute-start | bytes 172040 | tf_op jit(solution)/shard_map/ppermute | solution.py:573
  (27 other events, 290.8 us)

commit v6 on v5

--- a/solution.py
+++ b/solution.py
@@ -625,15 +625,15 @@
 def scatter_far(total, rows, extra=None):
     blocks = [total[k * rows : (k + 1) * rows] for k in range(4)]
     if extra is not None:
-        hi = extra.astype(bf16).astype(f32)
-        parts = jnp.concatenate([hi, (extra - hi).astype(bf16).astype(f32)])
-        blocks = [jnp.concatenate([block, parts]) for block in blocks]
-    sent = [swap(block.astype(bf16), far, "dp") for block, far in zip(blocks[1:], FAR[1:])]
+        rounded = extra.astype(bf16).astype(f32)
+        blocks = [jnp.concatenate([block, rounded]) for block in blocks]
+    sent = [swap(blocks[k].astype(bf16), FAR[k], "dp") for k in (3, 2, 1)]
     return blocks[:1] + sent
 
 
 def sum_pieces(pieces):
-    return sum(p.astype(f32) for p in pieces)
+    a, b, c, d = (p.astype(f32) for p in pieces)
+    return (a + b) + (c + d)
 
 
 def scatter_whole(g, bits):
@@ -936,7 +936,7 @@
             (block_out, grad_resid, far_x, sum_zo[:, :width], sum_zo[:, width:].T)
         )
         sum_x = sum_pieces(far_x)
-        small = both_parts(sum_x)
+        small = sum_x[rows:]
     else:
         sum_zo = scatter_whole(sent_zo[0], bits)
         grad_w_z, grad_w_out = sum_zo[:, :width], sum_zo[:, width:].T

time: 223 us -> 222 us (level)
  no operation moved by 1% of the time
where the time goes in v6:
time: 222 us; the launch traced here: 221 us
  Pallas kernels  124 us (56%)
  starting transfers between devices  41.9 us (19%)
  waiting for transfers between devices  28.4 us (13%)
  local copies, waits for them, and re-layouts  18.7 us (8%)
  other arithmetic  6.31 us (3%)
    pallas_call x6, Pallas kernels, call(): pl.pallas_call(kernel, grid_spec=pltpu.PrefetchScalarGridSpec(num_scalar_...  124 us
    ppermute x33, starting transfers between devices, swap(): return lax.ppermute(v, axis, [(i, i ^ bit) for i in range(size)])  41.9 us
    ppermute x33, waiting for transfers between devices, swap(): return lax.ppermute(v, axis, [(i, i ^ bit) for i in range(size)])  28.4 us
    unnamed x62, local copies, waits for them, and re-layouts  9.25 us
  transfers between devices with their start and end apart: 33, of which 10 were waited for; matrix products, arithmetic and copies ran while one was open for 6% of the time, Pallas kernels for 38%

profile of v6, /device:TPU:0, one launch (start us, length us, event | category | flops | bytes accessed | tf_op | source)
XLA Modules:
  0.0 220.7 jit_solution(5218326635158638930)
XLA Ops:
  1.6 3.1 %collective-permute-start = (bf16[48,2304]{1,0:T(8,128)(2,1)S(1)}, bf16[48,2304]{1,0:T(8,128)(2,1)S(1)}, u32[]{:S(2)}, u32[]{:S(2)}) collective-permute-start(bf16[48,2304]{1,0:T(8,128)(2,1)S(1)} %pad_maximum_fusion.3), channel_id=1, source_target_pairs={{0,8},{2,10},{4,12},{6,14},{8,0},{10,2},{12,4},{14,6},{16,24},{18,... | collective-permute-start | bytes 663560 | tf_op jit(solution)/shard_map/ppermute | solution.py:573
  4.7 2.6 %collective-permute-start.1 = (bf16[48,2304]{1,0:T(8,128)(2,1)S(1)}, bf16[48,2304]{1,0:T(8,128)(2,1)S(1)}, u32[]{:S(2)}, u32[]{:S(2)}) collective-permute-start(bf16[48,2304]{1,0:T(8,128)(2,1)S(1)} %pad_maximum_fusion.3), channel_id=1, source_target_pairs={{0,16},{2,18},{4,20},{6,22},{8,24},{10,26},{12,28},{14,30},{16,0},... | collective-permute-start | bytes 663560 | tf_op jit(solution)/shard_map/ppermute | solution.py:573
  8.9 1.7 collective-permute-start.3
  10.6 1.5 collective-permute-start.4
  19.9 3.6 %collective-permute-done.1 = bf16[48,2304]{1,0:T(8,128)(2,1)S(1)} collective-permute-done((bf16[48,2304]{1,0:T(8,128)(2,1)S(1)}, bf16[48,2304]{1,0:T(8,128)(2,1)S(1)}, u32[]{:S(2)}, u32[]{:S(2)}) %collective-permute-start.1) | collective-permute-done | bytes 221216 | tf_op jit(solution)/shard_map/ppermute | solution.py:573
  23.5 3.9 %collective-permute-start.11 = (bf16[4,48,384]{2,1,0:T(8,128)(2,1)S(1)}, bf16[4,48,384]{2,1,0:T(8,128)(2,1)S(1)}, u32[]{:S(2)}, u32[]{:S(2)}) collective-permute-start(bf16[4,48,384]{2,1,0:T(8,128)(2,1)S(1)} %pad_maximum_fusion.7), channel_id=1, source_target_pairs={{0,8},{2,10},{4,12},{6,14},{8,0},{10,2},{12,4},{14,6},{16,24},{18,... | collective-permute-start | bytes 442376 | tf_op jit(solution)/shard_map/ppermute | solution.py:573
  30.5 1.6 collective-permute-done.11
  32.2 2.4 %collective-permute-start.10 = (bf16[4,48,768]{2,1,0:T(8,128)(2,1)S(1)}, bf16[4,48,768]{2,1,0:T(8,128)(2,1)S(1)}, u32[]{:S(2)}, u32[]{:S(2)}) collective-permute-start(bf16[4,48,768]{2,1,0:T(8,128)(2,1)S(1)} %pad_maximum_fusion.1.rest_0_.rest_4_), channel_id=1, source_target_pairs={{0,6},{2,4},{4,2},{6,0},{8,14},{10,12},{12,10},{14,8},{16,22},{18,... | collective-permute-start | bytes 884744 | tf_op jit(solution)/shard_map/ppermute | solution.py:573
  34.6 5.8 %collective-permute-done.12 = bf16[4,48,384]{2,1,0:T(8,128)(2,1)S(1)} collective-permute-done((bf16[4,48,384]{2,1,0:T(8,128)(2,1)S(1)}, bf16[4,48,384]{2,1,0:T(8,128)(2,1)S(1)}, u32[]{:S(2)}, u32[]{:S(2)}) %collective-permute-start.12) | collective-permute-done | bytes 147488 | tf_op jit(solution)/shard_map/ppermute | solution.py:573
  40.4 1.5 collective-permute-start.8
  41.9 1.5 collective-permute-start.9
  43.6 3.6 %collective-permute-done.8.rest_1_.rest_5_ = bf16[4,48,768]{2,1,0:T(8,128)(2,1)S(1)} collective-permute-done((bf16[4,48,768]{2,1,0:T(8,128)(2,1)S(1)}, bf16[4,48,768]{2,1,0:T(8,128)(2,1)S(1)}, u32[]{:S(2)}, u32[]{:S(2)}) %collective-permute-start.8) | collective-permute-done | bytes 294944 | tf_op jit(solution)/shard_map/ppermute | solution.py:573
  47.2 1.5 collective-permute-done.9.rest_2_.rest_6_
  51.1 1.5 collective-permute-start.15
  56.9 27.9 %mix_forward.1 = (bf16[2048,768]{1,0:T(8,128)(2,1)}, bf16[2048,1024]{1,0:T(8,128)(2,1)}, bf16[2048,1024]{1,0:T(8,128)(2,1)}, bf16[2048,1024]{1,0:T(8,128)(2,1)},...) custom-call(s32[2]{0:T(128)S(1)} %pad_add_fusion.info, ...), custom_call_target="tpu_custom_call" | custom-call | tf_op jit(solution)/shard_map/mix_forward/pallas_call | solution.py:667
  85.7 15.8 %gate_forward.1 = (bf16[2048,768]{1,0:T(8,128)(2,1)}, f32[2048,768]{1,0:T(8,128)}, f32[64,512]{1,0:T(8,128)S(1)}) custom-call(s32[2]{0:T(128)S(1)} %pad_add_fusion.info, bf16[1024,768]{1,0:T(8,128)(2,1)} %refs_1_.1, bf16[1024,768]{1,0:T(8,128)(2,1)} %copy-done.22, bf16[2048,768]{1,0:T(8,128)(2,1)} %get-tuple-element.116.normed, ...), custom_call_target="tpu_custom_call" | custom-call | tf_op jit(solution)/shard_map/gate_forward/pallas_call | solution.py:667
  103.0 23.7 %gate_backward.1 = (bf16[1024,768]{1,0:T(8,128)(2,1)}, bf16[1024,768]{1,0:T(8,128)(2,1)}, bf16[2048,768]{1,0:T(8,128)(2,1)}, bf16[2048,768]{1,0:T(8,128)(2,1)}, ...) custom-call(s32[2]{0:T(128)S(1)} %pad_add_fusion.info, ...), custom_call_target="tpu_custom_call" | custom-call | tf_op jit(solution)/shard_map/gate_backward/pallas_call | solution.py:667
  127.5 1.5 collective-permute-start.19
  129.0 1.4 collective-permute-start.20
  130.5 43.5 %mix_backward.1 = (bf16[2048,1152]{1,0:T(8,128)(2,1)}, f32[8,1152]{1,0:T(8,128)}, bf16[208,1152]{1,0:T(8,128)(2,1)}, bf16[208,1152]{1,0:T(8,128)(2,1)}, bf16[208...) custom-call(s32[2]{0:T(128)S(1)} %pad_add_fusion.info, bf16[2048,1024]{1,0:T(8,128)(2,1)} %get-tuple-element.130.xbc, ...), custom_call_target="tpu_custom_call" | custom-call | tf_op jit(solution)/shard_map/mix_backward/pallas_call | solution.py:667
  174.6 1.5 collective-permute-start.26
  176.1 1.4 collective-permute-start.27
  177.9 2.0 collective-permute-start.22
  179.9 1.5 collective-permute-start.23
  181.6 2.3 %copy-done.12 = bf16[2048,1152]{1,0:T(8,128)(2,1)S(1)} copy-done((bf16[2048,1152]{1,0:T(8,128)(2,1)S(1)}, bf16[2048,1152]{1,0:T(8,128)(2,1)}, u32[]{:S(2)}) %copy-start.12) | copy-done | bytes 4718616
  183.9 9.4 %input_backward.1 = (bf16[1024,768]{1,0:T(8,128)(2,1)S(1)}, bf16[1024,768]{1,0:T(8,128)(2,1)S(1)}) custom-call(s32[2]{0:T(128)S(1)} %pad_add_fusion.info, bf16[2048,768]{1,0:T(8,128)(2,1)S(1)} %copy-done.13, bf16[2048,1152]{1,0:T(8,128)(2,1)S(1)} %copy-done.12, bf16[4,48,1536]{2,1,0:T(8,128)(2,1)S(1)} %copy-done.2, bf16[4,48,1536]{2,1,0:T(8,128)(2,1)S(1)} %copy-done.7, ...), custom_call_target="tpu_custom_call" | custom-call | tf_op jit(solution)/shard_map/input_backward/pallas_call | solution.py:667
  194.3 2.0 collective-permute-done.26
  196.3 1.5 collective-permute-done.27
  198.2 2.0 collective-permute-start.29
  200.3 1.9 collective-permute-start.30
  202.9 3.9 %finish.1 = (bf16[1024,768]{1,0:T(8,128)(2,1)}, f32[1024,768]{1,0:T(8,128)}) custom-call(s32[2]{0:T(128)S(1)} %pad_add_fusion.info, bf16[1024,768]{1,0:T(8,128)(2,1)S(1)} %copy-done.3, bf16[1024,768]{1,0:T(8,128)(2,1)S(1)} %copy-done, f32[16,1024]{1,0:T(8,128)S(1)} %copy-done.20, bf16[1024,768]{1,0:T(8,128)(2,1)S(1)} %get-tuple-element.158.refs_3_, ...), custom_call_target="tpu_custom_call" | custom-call | tf_op jit(solution)/shard_map/finish/pallas_call | solution.py:667
  207.5 6.7 %collective-permute-done.30 = bf16[56,1152]{1,0:T(8,128)(2,1)S(1)} collective-permute-done((bf16[56,1152]{1,0:T(8,128)(2,1)S(1)}, bf16[56,1152]{1,0:T(8,128)(2,1)S(1)}, u32[]{:S(2)}, u32[]{:S(2)}) %collective-permute-start.30) | collective-permute-done | bytes 129056 | tf_op jit(solution)/shard_map/ppermute | solution.py:573
  (166 shorter events, 33.5 us)
Async XLA Ops:
  1.6 18.3 %collective-permute-start = (bf16[48,2304]{1,0:T(8,128)(2,1)S(1)}, bf16[48,2304]{1,0:T(8,128)(2,1)S(1)}, u32[]{:S(2)}, u32[]{:S(2)}) collective-permute-start(bf16[48,2304]{1,0:T(8,128)(2,1)S(1)} %pad_maximum_fusion.3), channel_id=1, source_target_pairs={{0,8},{2,10},{4,12},{6,14},{8,0},{10,2},{12,4},{14,6},{16,24},{18,... | collective-permute-start | bytes 663560 | tf_op jit(solution)/shard_map/ppermute | solution.py:573
  4.7 18.7 %collective-permute-start.1 = (bf16[48,2304]{1,0:T(8,128)(2,1)S(1)}, bf16[48,2304]{1,0:T(8,128)(2,1)S(1)}, u32[]{:S(2)}, u32[]{:S(2)}) collective-permute-start(bf16[48,2304]{1,0:T(8,128)(2,1)S(1)} %pad_maximum_fusion.3), channel_id=1, source_target_pairs={{0,16},{2,18},{4,20},{6,22},{8,24},{10,26},{12,28},{14,30},{16,0},... | collective-permute-start | bytes 663560 | tf_op jit(solution)/shard_map/ppermute | solution.py:573
  7.3 16.1 %collective-permute-start.2 = (bf16[48,2304]{1,0:T(8,128)(2,1)S(1)}, bf16[48,2304]{1,0:T(8,128)(2,1)S(1)}, u32[]{:S(2)}, u32[]{:S(2)}) collective-permute-start(bf16[48,2304]{1,0:T(8,128)(2,1)S(1)} %pad_maximum_fusion.3), channel_id=1, source_target_pairs={{0,24},{2,26},{4,28},{6,30},{8,16},{10,18},{12,20},{14,22},{16,8},... | collective-permute-start | bytes 663560 | tf_op jit(solution)/shard_map/ppermute | solution.py:573
  8.9 6.1 %collective-permute-start.3 = (bf16[48,384]{1,0:T(8,128)(2,1)S(1)}, bf16[48,384]{1,0:T(8,128)(2,1)S(1)}, u32[]{:S(2)}, u32[]{:S(2)}) collective-permute-start(bf16[48,384]{1,0:T(8,128)(2,1)S(1)} %pad_maximum_fusion.9), channel_id=1, source_target_pairs={{0,2},{2,0},{4,6},{6,4},{8,10},{10,8},{12,14},{14,12},{16,18},{18,... | collective-permute-start | bytes 110600 | tf_op jit(solution)/shard_map/ppermute | solution.py:573
  10.6 8.5 %collective-permute-start.4 = (bf16[48,384]{1,0:T(8,128)(2,1)S(1)}, bf16[48,384]{1,0:T(8,128)(2,1)S(1)}, u32[]{:S(2)}, u32[]{:S(2)}) collective-permute-start(bf16[48,384]{1,0:T(8,128)(2,1)S(1)} %pad_maximum_fusion.9), channel_id=1, source_target_pairs={{0,4},{2,6},{4,0},{6,2},{8,12},{10,14},{12,8},{14,10},{16,20},{18,... | collective-permute-start | bytes 110600 | tf_op jit(solution)/shard_map/ppermute | solution.py:573
  15.0 4.9 %collective-permute-start.5 = (bf16[48,384]{1,0:T(8,128)(2,1)S(1)}, bf16[48,384]{1,0:T(8,128)(2,1)S(1)}, u32[]{:S(2)}, u32[]{:S(2)}) collective-permute-start(bf16[48,384]{1,0:T(8,128)(2,1)S(1)} %pad_maximum_fusion.9), channel_id=1, source_target_pairs={{0,6},{2,4},{4,2},{6,0},{8,14},{10,12},{12,10},{14,8},{16,22},{18,... | collective-permute-start | bytes 110600 | tf_op jit(solution)/shard_map/ppermute | solution.py:573
  23.5 8.7 %collective-permute-start.11 = (bf16[4,48,384]{2,1,0:T(8,128)(2,1)S(1)}, bf16[4,48,384]{2,1,0:T(8,128)(2,1)S(1)}, u32[]{:S(2)}, u32[]{:S(2)}) collective-permute-start(bf16[4,48,384]{2,1,0:T(8,128)(2,1)S(1)} %pad_maximum_fusion.7), channel_id=1, source_target_pairs={{0,8},{2,10},{4,12},{6,14},{8,0},{10,2},{12,4},{14,6},{16,24},{18,... | collective-permute-start | bytes 442376 | tf_op jit(solution)/shard_map/ppermute | solution.py:573
  27.4 13.0 %collective-permute-start.12 = (bf16[4,48,384]{2,1,0:T(8,128)(2,1)S(1)}, bf16[4,48,384]{2,1,0:T(8,128)(2,1)S(1)}, u32[]{:S(2)}, u32[]{:S(2)}) collective-permute-start(bf16[4,48,384]{2,1,0:T(8,128)(2,1)S(1)} %pad_maximum_fusion.7), channel_id=1, source_target_pairs={{0,16},{2,18},{4,20},{6,22},{8,24},{10,26},{12,28},{14,30},{16,0},... | collective-permute-start | bytes 442376 | tf_op jit(solution)/shard_map/ppermute | solution.py:573
  28.5 13.4 %collective-permute-start.13 = (bf16[4,48,384]{2,1,0:T(8,128)(2,1)S(1)}, bf16[4,48,384]{2,1,0:T(8,128)(2,1)S(1)}, u32[]{:S(2)}, u32[]{:S(2)}) collective-permute-start(bf16[4,48,384]{2,1,0:T(8,128)(2,1)S(1)} %pad_maximum_fusion.7), channel_id=1, source_target_pairs={{0,24},{2,26},{4,28},{6,30},{8,16},{10,18},{12,20},{14,22},{16,8},... | collective-permute-start | bytes 442376 | tf_op jit(solution)/shard_map/ppermute | solution.py:573
  29.9 18.8 %collective-permute-start.6 = (bf16[1024,768]{1,0:T(8,128)(2,1)}, bf16[1024,768]{1,0:T(8,128)(2,1)S(1)}, u32[]{:S(2)}, u32[]{:S(2)}) collective-permute-start(bf16[1024,768]{1,0:T(8,128)(2,1)} %refs_0_.1), channel_id=1, source_target_pairs={{0,1},{1,0},{2,3},{3,2},{4,5},{5,4},{6,7},{7,6},{8,9},{9,8},{10,11... | collective-permute-start | bytes 4718600 | tf_op jit(solution)/shard_map/ppermute | solution.py:573
  29.9 18.8 %collective-permute-start.7 = (bf16[1024,768]{1,0:T(8,128)(2,1)}, bf16[1024,768]{1,0:T(8,128)(2,1)S(1)}, u32[]{:S(2)}, u32[]{:S(2)}) collective-permute-start(bf16[1024,768]{1,0:T(8,128)(2,1)} %refs_1_.1), channel_id=1, source_target_pairs={{0,1},{1,0},{2,3},{3,2},{4,5},{5,4},{6,7},{7,6},{8,9},{9,8},{10,11... | collective-permute-start | bytes 4718600 | tf_op jit(solution)/shard_map/ppermute | solution.py:573
  32.2 11.4 %collective-permute-start.10 = (bf16[4,48,768]{2,1,0:T(8,128)(2,1)S(1)}, bf16[4,48,768]{2,1,0:T(8,128)(2,1)S(1)}, u32[]{:S(2)}, u32[]{:S(2)}) collective-permute-start(bf16[4,48,768]{2,1,0:T(8,128)(2,1)S(1)} %pad_maximum_fusion.1.rest_0_.rest_4_), channel_id=1, source_target_pairs={{0,6},{2,4},{4,2},{6,0},{8,14},{10,12},{12,10},{14,8},{16,22},{18,... | collective-permute-start | bytes 884744 | tf_op jit(solution)/shard_map/ppermute | solution.py:573
  40.4 6.7 %collective-permute-start.8 = (bf16[4,48,768]{2,1,0:T(8,128)(2,1)S(1)}, bf16[4,48,768]{2,1,0:T(8,128)(2,1)S(1)}, u32[]{:S(2)}, u32[]{:S(2)}) collective-permute-start(bf16[4,48,768]{2,1,0:T(8,128)(2,1)S(1)} %pad_maximum_fusion.1.rest_0_.rest_4_), channel_id=1, source_target_pairs={{0,2},{2,0},{4,6},{6,4},{8,10},{10,8},{12,14},{14,12},{16,18},{18,... | collective-permute-start | bytes 884744 | tf_op jit(solution)/shard_map/ppermute | solution.py:573
  41.9 6.7 %collective-permute-start.9 = (bf16[4,48,768]{2,1,0:T(8,128)(2,1)S(1)}, bf16[4,48,768]{2,1,0:T(8,128)(2,1)S(1)}, u32[]{:S(2)}, u32[]{:S(2)}) collective-permute-start(bf16[4,48,768]{2,1,0:T(8,128)(2,1)S(1)} %pad_maximum_fusion.1.rest_0_.rest_4_), channel_id=1, source_target_pairs={{0,4},{2,6},{4,0},{6,2},{8,12},{10,14},{12,8},{14,10},{16,20},{18,... | collective-permute-start | bytes 884744 | tf_op jit(solution)/shard_map/ppermute | solution.py:573
  50.5 34.3 %collective-permute-start.14 = (bf16[4,48,1536]{2,1,0:T(8,128)(2,1)S(1)}, bf16[4,48,1536]{2,1,0:T(8,128)(2,1)S(1)}, u32[]{:S(2)}, u32[]{:S(2)}) collective-permute-start(bf16[4,48,1536]{2,1,0:T(8,128)(2,1)S(1)} %pad_maximum_fusion.rest_0_), channel_id=1, source_target_pairs={{0,2},{2,0},{4,6},{6,4},{8,10},{10,8},{12,14},{14,12},{16,18},{18,... | collective-permute-start | bytes 1769480 | tf_op jit(solution)/shard_map/ppermute | solution.py:573
  51.1 33.7 %collective-permute-start.15 = (bf16[4,48,1536]{2,1,0:T(8,128)(2,1)S(1)}, bf16[4,48,1536]{2,1,0:T(8,128)(2,1)S(1)}, u32[]{:S(2)}, u32[]{:S(2)}) collective-permute-start(bf16[4,48,1536]{2,1,0:T(8,128)(2,1)S(1)} %pad_maximum_fusion.rest_0_), channel_id=1, source_target_pairs={{0,4},{2,6},{4,0},{6,2},{8,12},{10,14},{12,8},{14,10},{16,20},{18,... | collective-permute-start | bytes 1769480 | tf_op jit(solution)/shard_map/ppermute | solution.py:573
  52.6 32.2 %collective-permute-start.16 = (bf16[4,48,1536]{2,1,0:T(8,128)(2,1)S(1)}, bf16[4,48,1536]{2,1,0:T(8,128)(2,1)S(1)}, u32[]{:S(2)}, u32[]{:S(2)}) collective-permute-start(bf16[4,48,1536]{2,1,0:T(8,128)(2,1)S(1)} %pad_maximum_fusion.rest_0_), channel_id=1, source_target_pairs={{0,6},{2,4},{4,2},{6,0},{8,14},{10,12},{12,10},{14,8},{16,22},{18,... | collective-permute-start | bytes 1769480 | tf_op jit(solution)/shard_map/ppermute | solution.py:573
  126.6 47.4 %collective-permute-start.21 = (bf16[1024,768]{1,0:T(8,128)(2,1)}, bf16[1024,768]{1,0:T(8,128)(2,1)S(1)}, u32[]{:S(2)}, u32[]{:S(2)}) collective-permute-start(bf16[1024,768]{1,0:T(8,128)(2,1)} %get-tuple-element.129), channel_id=1, source_target_pairs={{0,1},{1,0},{2,3},{3,2},{4,5},{5,4},{6,7},{7,6},{8,9},{9,8},{10,11... | collective-permute-start | bytes 4718600 | tf_op jit(solution)/shard_map/ppermute | solution.py:573
  126.9 47.1 %collective-permute-start.18 = (bf16[192,1536]{1,0:T(8,128)(2,1)S(1)}, bf16[192,1536]{1,0:T(8,128)(2,1)S(1)}, u32[]{:S(2)}, u32[]{:S(2)}) collective-permute-start(bf16[192,1536]{1,0:T(8,128)(2,1)S(1)} %get-tuple-element.126), channel_id=1, source_target_pairs={{0,2},{2,0},{4,6},{6,4},{8,10},{10,8},{12,14},{14,12},{16,18},{18,... | collective-permute-start | bytes 1769480 | tf_op jit(solution)/shard_map/ppermute | solution.py:573
  127.5 46.5 %collective-permute-start.19 = (bf16[192,1536]{1,0:T(8,128)(2,1)}, bf16[192,1536]{1,0:T(8,128)(2,1)S(1)}, u32[]{:S(2)}, u32[]{:S(2)}) collective-permute-start(bf16[192,1536]{1,0:T(8,128)(2,1)} %get-tuple-element.127), channel_id=1, source_target_pairs={{0,4},{2,6},{4,0},{6,2},{8,12},{10,14},{12,8},{14,10},{16,20},{18,... | collective-permute-start | bytes 1769480 | tf_op jit(solution)/shard_map/ppermute | solution.py:573
  129.0 45.0 %collective-permute-start.20 = (bf16[192,1536]{1,0:T(8,128)(2,1)}, bf16[192,1536]{1,0:T(8,128)(2,1)S(1)}, u32[]{:S(2)}, u32[]{:S(2)}) collective-permute-start(bf16[192,1536]{1,0:T(8,128)(2,1)} %get-tuple-element.128), channel_id=1, source_target_pairs={{0,6},{2,4},{4,2},{6,0},{8,14},{10,12},{12,10},{14,8},{16,22},{18,... | collective-permute-start | bytes 1769480 | tf_op jit(solution)/shard_map/ppermute | solution.py:573
  174.0 19.3 %collective-permute-start.25 = (bf16[208,1152]{1,0:T(8,128)(2,1)}, bf16[208,1152]{1,0:T(8,128)(2,1)S(1)}, u32[]{:S(2)}, u32[]{:S(2)}) collective-permute-start(bf16[208,1152]{1,0:T(8,128)(2,1)} %get-tuple-element.149), channel_id=1, source_target_pairs={{0,2},{2,0},{4,6},{6,4},{8,10},{10,8},{12,14},{14,12},{16,18},{18,... | collective-permute-start | bytes 1437704 | tf_op jit(solution)/shard_map/ppermute | solution.py:573
  174.6 21.7 %collective-permute-start.26 = (bf16[208,1152]{1,0:T(8,128)(2,1)}, bf16[208,1152]{1,0:T(8,128)(2,1)S(1)}, u32[]{:S(2)}, u32[]{:S(2)}) collective-permute-start(bf16[208,1152]{1,0:T(8,128)(2,1)} %get-tuple-element.150), channel_id=1, source_target_pairs={{0,4},{2,6},{4,0},{6,2},{8,12},{10,14},{12,8},{14,10},{16,20},{18,... | collective-permute-start | bytes 1437704 | tf_op jit(solution)/shard_map/ppermute | solution.py:573
  176.1 21.7 %collective-permute-start.27 = (bf16[208,1152]{1,0:T(8,128)(2,1)}, bf16[208,1152]{1,0:T(8,128)(2,1)S(1)}, u32[]{:S(2)}, u32[]{:S(2)}) collective-permute-start(bf16[208,1152]{1,0:T(8,128)(2,1)} %get-tuple-element.151), channel_id=1, source_target_pairs={{0,6},{2,4},{4,2},{6,0},{8,14},{10,12},{12,10},{14,8},{16,22},{18,... | collective-permute-start | bytes 1437704 | tf_op jit(solution)/shard_map/ppermute | solution.py:573
  177.9 22.3 %collective-permute-start.22 = (bf16[48,1536]{1,0:T(8,128)(2,1)S(1)}, bf16[48,1536]{1,0:T(8,128)(2,1)S(1)}, u32[]{:S(2)}, u32[]{:S(2)}) collective-permute-start(bf16[48,1536]{1,0:T(8,128)(2,1)S(1)} %get-tuple-element.208), channel_id=1, source_target_pairs={{0,24},{2,26},{4,28},{6,30},{8,16},{10,18},{12,20},{14,22},{16,8},... | collective-permute-start | bytes 442376 | tf_op jit(solution)/shard_map/ppermute | solution.py:573
  179.9 22.2 %collective-permute-start.23 = (bf16[48,1536]{1,0:T(8,128)(2,1)S(1)}, bf16[48,1536]{1,0:T(8,128)(2,1)S(1)}, u32[]{:S(2)}, u32[]{:S(2)}) collective-permute-start(bf16[48,1536]{1,0:T(8,128)(2,1)S(1)} %get-tuple-element.207), channel_id=1, source_target_pairs={{0,16},{2,18},{4,20},{6,22},{8,24},{10,26},{12,28},{14,30},{16,0},... | collective-permute-start | bytes 442376 | tf_op jit(solution)/shard_map/ppermute | solution.py:573
  193.3 9.5 %collective-permute-start.24 = (bf16[48,1536]{1,0:T(8,128)(2,1)S(1)}, bf16[48,1536]{1,0:T(8,128)(2,1)S(1)}, u32[]{:S(2)}, u32[]{:S(2)}) collective-permute-start(bf16[48,1536]{1,0:T(8,128)(2,1)S(1)} %get-tuple-element.206), channel_id=1, source_target_pairs={{0,8},{2,10},{4,12},{6,14},{8,0},{10,2},{12,4},{14,6},{16,24},{18,... | collective-permute-start | bytes 442376 | tf_op jit(solution)/shard_map/ppermute | solution.py:573
  197.8 5.0 %collective-permute-start.28 = (bf16[1024,768]{1,0:T(8,128)(2,1)S(1)}, bf16[1024,768]{1,0:T(8,128)(2,1)S(1)}, u32[]{:S(2)}, u32[]{:S(2)}) collective-permute-start(bf16[1024,768]{1,0:T(8,128)(2,1)S(1)} %get-tuple-element.156), channel_id=1, source_target_pairs={{0,1},{1,0},{2,3},{3,2},{4,5},{5,4},{6,7},{7,6},{8,9},{9,8},{10,11... | collective-permute-start | bytes 4718600 | tf_op jit(solution)/shard_map/ppermute | solution.py:573
  198.2 9.3 %collective-permute-start.29 = (bf16[56,1152]{1,0:T(8,128)(2,1)S(1)}, bf16[56,1152]{1,0:T(8,128)(2,1)S(1)}, u32[]{:S(2)}, u32[]{:S(2)}) collective-permute-start(bf16[56,1152]{1,0:T(8,128)(2,1)S(1)} %get-tuple-element.217), channel_id=1, source_target_pairs={{0,24},{2,26},{4,28},{6,30},{8,16},{10,18},{12,20},{14,22},{16,8},... | collective-permute-start | bytes 387080 | tf_op jit(solution)/shard_map/ppermute | solution.py:573
  200.3 14.0 %collective-permute-start.30 = (bf16[56,1152]{1,0:T(8,128)(2,1)S(1)}, bf16[56,1152]{1,0:T(8,128)(2,1)S(1)}, u32[]{:S(2)}, u32[]{:S(2)}) collective-permute-start(bf16[56,1152]{1,0:T(8,128)(2,1)S(1)} %get-tuple-element.218), channel_id=1, source_target_pairs={{0,16},{2,18},{4,20},{6,22},{8,24},{10,26},{12,28},{14,30},{16,0},... | collective-permute-start | bytes 387080 | tf_op jit(solution)/shard_map/ppermute | solution.py:573
  202.2 12.1 %collective-permute-start.31 = (bf16[56,1152]{1,0:T(8,128)(2,1)S(1)}, bf16[56,1152]{1,0:T(8,128)(2,1)S(1)}, u32[]{:S(2)}, u32[]{:S(2)}) collective-permute-start(bf16[56,1152]{1,0:T(8,128)(2,1)S(1)} %get-tuple-element.216), channel_id=1, source_target_pairs={{0,8},{2,10},{4,12},{6,14},{8,0},{10,2},{12,4},{14,6},{16,24},{18,... | collective-permute-start | bytes 387080 | tf_op jit(solution)/shard_map/ppermute | solution.py:573
  215.0 3.3 %collective-permute-start.32 = (f32[14336]{0:T(1024)S(1)}, f32[14336]{0:T(1024)S(1)}, u32[]{:S(2)}, u32[]{:S(2)}) collective-permute-start(f32[14336]{0:T(1024)S(1)} %pad_maximum_fusion.8), channel_id=1, source_target_pairs={{0,1},{1,0},{2,3},{3,2},{4,5},{5,4},{6,7},{7,6},{8,9},{9,8},{10,11... | collective-permute-start | bytes 172040 | tf_op jit(solution)/shard_map/ppermute | solution.py:573
  (27 other events, 289.6 us)
